TPU v7x, 256 devices: a whole 4x4x8 slice. The times are simulated.
256 devices in a mesh: gx: 32 (over y_hi, z, core), gy: 8 (over x, y_lo).
Axes of the slice: x: 4, y: 4 (y_hi: 2, y_lo: 2; y = y_hi * 2 + y_lo), z: 8, core: 2. Of those that a mesh axis runs over, the one named last changes fastest.
Arguments:
- flow_speed_vectors: float32 [3, 10, 2048, 2048], P(None, None, 'gx', 'gy'), may hold values from -6 to 6
- thermal_state: float32 [10, 2048, 2048], P(None, 'gx', 'gy'), may hold values from 0.5 to 2
- northward_basis_matrix: bfloat16 [2048, 256], P('gy'), may hold values from -0.125 to 0.125
Outputs:
- gram: float32 [2048, 2048], P('gx')
All inputs are finite; a program needn't handle non-finite values.
Results may differ from a plain program's by a relative error of at most 0.0003.
Values may be sent and summed in bfloat16 or wider, within the bound.
No kernel may reach another device: no remote copies, remote signals or barrier semaphores. Data moves between devices by JAX's collectives and lax.ppermute only.
A program may use at most 64 MiB of HBM per device.

v0:
```python
import jax
import jax.numpy as jnp
from jax import lax
from jax.sharding import PartitionSpec as P


def extended(block, sides, width):
    for axis, dim in sides:
        count = lax.axis_size(axis)
        forward = [(i, i + 1) for i in range(count - 1)]
        forward.append((count - 1, 0))
        backward = [(target, source) for source, target in forward]
        low = lax.ppermute(
            lax.slice_in_dim(block, block.shape[dim] - width, None, axis=dim), axis, forward
        )
        high = lax.ppermute(lax.slice_in_dim(block, 0, width, axis=dim), axis, backward)
        block = jnp.concatenate([low, block, high], axis=dim)
    return block


def energy_loss_rate(partial_derivatives, thermal_state):
    deformation_norm = jnp.zeros_like(thermal_state)
    for source in range(3):
        for target in range(3):
            strain = 0.5 * (
                partial_derivatives[source][target] + partial_derivatives[target][source]
            )
            deformation_norm = deformation_norm + strain * strain
    flow_expansion = (
        partial_derivatives[0][0] + partial_derivatives[1][1] + partial_derivatives[2][2]
    )
    return (
        0.1
        * thermal_state**0.7
        * (2.0 * deformation_norm - 2.0 / 3.0 * flow_expansion * flow_expansion)
    )


def body(flow_speed_vectors, thermal_state, northward_basis_matrix):
    deriv_z = (
        -flow_speed_vectors[:, 4:]
        + 8.0 * flow_speed_vectors[:, 3:-1]
        - 8.0 * flow_speed_vectors[:, 1:-3]
        + flow_speed_vectors[:, :-4]
    ) / 12.0
    center = flow_speed_vectors[:, 2:-2]
    padded = extended(center, (("gx", 2), ("gy", 3)), 2)
    deriv_x = (
        -padded[:, :, 4:, 2:-2]
        + 8.0 * padded[:, :, 3:-1, 2:-2]
        - 8.0 * padded[:, :, 1:-3, 2:-2]
        + padded[:, :, :-4, 2:-2]
    ) / 12.0
    deriv_y = (
        -padded[:, :, 2:-2, 4:]
        + 8.0 * padded[:, :, 2:-2, 3:-1]
        - 8.0 * padded[:, :, 2:-2, 1:-3]
        + padded[:, :, 2:-2, :-4]
    ) / 12.0
    partial_derivatives = [[deriv_z[comp], deriv_x[comp], deriv_y[comp]] for comp in range(3)]
    pointwise_quantity = energy_loss_rate(partial_derivatives, thermal_state[2:-2]).astype(
        jnp.bfloat16
    )
    planes = pointwise_quantity.shape[0]
    rank = northward_basis_matrix.shape[1]
    partial_core = jnp.einsum(
        "zxy,yr->xzr",
        pointwise_quantity,
        northward_basis_matrix,
        preferred_element_type=jnp.float32,
    )
    rows_local = partial_core.shape[0]
    flat_core = partial_core.reshape(rows_local, planes * rank)
    scale = 1.0 / (planes * rank)
    summed = lax.psum(flat_core, "gy")
    core = summed.astype(jnp.bfloat16)
    gram = lax.dot_general(
        core,
        lax.all_gather(core, "gx", axis=0, tiled=True),
        (((1,), (1,)), ((), ())),
        preferred_element_type=jnp.float32,
    )
    return gram * scale


def solution(mesh):
    placed = (P(None, None, "gx", "gy"), P(None, "gx", "gy"), P("gy", None))
    return jax.shard_map(body, mesh=mesh, in_specs=placed, out_specs=P("gx", None), check_vma=False)
```

profile of v0, /device:TPU:32, one launch (start us, length us, event | category | flops | bytes accessed | tf_op | source)
XLA Modules:
  0.0 203.6 jit_solution(8058766201857614093)
XLA Ops:
  6.5 0.0 copy-start
  6.5 0.0 all-gather.2.cloned.1.call-start
  6.5 1.0 fusion.34
  7.6 0.1 collective-permute-start.1
  7.7 1.7 collective-permute-start
  9.4 5.8 %fusion.33 = (f32[3,6,64,256]{3,2,1,0:T(8,128)}, f32[3,6,64,256]{3,2,1,0:T(8,128)}, f32[3,6,64,256]{3,2,1,0:T(8,128)}, f32[3,6,64,256]{3,2,1,0:T(8,128)}, f32[3,6,64,256]{3,2,1,0:T(8,128)}) fusion(f32[3,10,64,256]{3,2,1,0:T(8,128)} %param.3), kind=kLoop, calls=%fused_computation.55 | loop fusion | bytes 11796480 | tf_op jit(solution)/shard_map/slice | solution.py:41
  15.2 1.8 copy.32
  17.0 2.9 %copy.31 = f32[3,6,64,256]{2,3,1,0:T(8,128)} copy(f32[3,6,64,256]{3,2,1,0:T(8,128)} %get-tuple-element.11) | data formatting | bytes 2359296
  19.9 2.9 %copy.30 = f32[3,6,64,256]{2,3,1,0:T(8,128)} copy(f32[3,6,64,256]{3,2,1,0:T(8,128)} %get-tuple-element.12) | data formatting | bytes 2359296
  22.8 2.9 %copy.29 = f32[3,6,64,256]{2,3,1,0:T(8,128)} copy(f32[3,6,64,256]{3,2,1,0:T(8,128)} %get-tuple-element.9) | data formatting | bytes 2359296
  25.7 5.3 %add_multiply_fusion = f32[3,6,64,256]{2,3,1,0:T(8,128)} fusion(f32[3,6,64,256]{2,3,1,0:T(8,128)S(1)} %copy.32, f32[3,6,64,256]{2,3,1,0:T(8,128)} %copy.31, f32[3,6,64,256]{2,3,1,0:T(8,128)} %copy.30, f32[3,6,64,256]{2,3,1,0:T(8,128)} %copy.29), kind=kLoop, calls=%fused_computation.18 | loop fusion | flops 2064384 | bytes 5898240 | tf_op jit(solution)/shard_map/div | solution.py:40
  31.1 0.0 slice-start
  31.1 1.9 copy.33
  33.0 0.0 slice-done
  33.0 1.2 copy.28
  34.1 0.0 collective-permute-done.1
  34.1 2.1 %copy.22 = f32[3,6,2,256]{2,3,1,0:T(8,128)} copy(f32[3,6,2,256]{3,2,1,0:T(2,128)S(1)} %collective-permute-done.1) | data formatting | bytes 73728 | tf_op jit(solution)/shard_map/ppermute | solution.py:13
  36.3 0.0 collective-permute-done
  36.3 2.2 %copy.21 = f32[3,6,2,256]{2,3,1,0:T(8,128)} copy(f32[3,6,2,256]{3,2,1,0:T(2,128)S(1)} %collective-permute-done) | data formatting | bytes 73728 | tf_op jit(solution)/shard_map/ppermute | solution.py:16
  38.4 0.0 copy-start.1
  38.4 0.0 copy-start.2
  38.4 1.3 pad_maximum_fusion.5
  39.7 3.8 %collective-permute-start.2 = (f32[3,6,68,2]{2,3,1,0:T(2,128)S(1)}, f32[3,6,68,2]{2,3,1,0:T(2,128)S(1)}, u32[]{:S(2)}, u32[]{:S(2)}) collective-permute-start(f32[3,6,68,2]{2,3,1,0:T(2,128)S(1)} %get-tuple-element.7), channel_id=1, source_target_pairs={{1,0},{2,1},{3,2},{4,3},{5,4},{6,5},{7,6},{0,7},{9,8},{10,9},{11,1... | collective-permute-start | bytes 29384 | tf_op jit(solution)/shard_map/ppermute | solution.py:16
  43.6 0.0 collective-permute-start.3
  43.6 0.0 copy-done.1
  43.6 0.0 copy-done.2
  43.6 4.4 %fusion.4 = f32[3,6,64,256]{2,3,1,0:T(8,128)S(1)} fusion(f32[3,6,64,256]{2,3,1,0:T(8,128)S(1)} %copy.33, f32[3,6,2,256]{2,3,1,0:T(8,128)S(1)} %copy-done.1, f32[3,6,2,256]{2,3,1,0:T(8,128)S(1)} %copy-done.2), kind=kLoop, calls=%fused_computation.11 | loop fusion | flops 3244032 | bytes 2433024 | tf_op jit(solution)/shard_map/div | solution.py:48
  48.0 0.0 collective-permute-done.2
  48.0 1.4 collective-permute-done.3
  49.5 2.5 %pad_maximum_fusion = (f32[3,6,68,258]{2,3,1,0:T(8,128)S(1)}, f32[3,6,68,258]{2,3,1,0:T(8,128)S(1)}) fusion(f32[3,6,68,2]{2,3,1,0:T(2,128)S(1)} %collective-permute-done.2, f32[3,6,2,256]{2,3,1,0:T(8,128)S(1)} %copy-done.2, f32[3,6,64,256]{2,3,1,0:T(8,128)S(1)} %copy.33, f32[3,6,2,256]{2,3,1,0:T(8,128)S(1)} %copy-done.1, ...), kind=kLoop, calls=%fused_computation | loop fusion | flops 1894752 | bytes 3799296 | tf_op jit(solution)/shard_map/concatenate | solution.py:17
  52.0 0.0 copy-start.3
  52.0 2.5 %fusion = f32[3,6,64,256]{2,3,1,0:T(8,128)S(1)} fusion(f32[3,6,68,258]{2,3,1,0:T(8,128)S(1)} %get-tuple-element.6, f32[3,6,68,258]{2,3,1,0:T(8,128)S(1)} %get-tuple-element.5), kind=kLoop, calls=%fused_computation.3 | loop fusion | flops 2064384 | bytes 5898240 | tf_op jit(solution)/shard_map/div | solution.py:54
  54.5 0.0 copy-done
  54.5 0.0 copy-done.3
  54.5 3.0 %convolution_bitcast_fusion = f32[6,8,8,256]{3,2,1,0:T(8,128)S(1)} fusion(f32[3,6,64,256]{2,3,1,0:T(8,128)S(1)} %fusion.4, f32[3,6,64,256]{2,3,1,0:T(8,128)S(1)} %fusion, f32[3,6,64,256]{2,3,1,0:T(8,128)} %add_multiply_fusion, f32[6,64,256]{1,2,0:T(8,128)S(1)} %copy-done.3, bf16[256,256]{1,0:T(8,128)(2,1)S(1)} %copy-done), kind=kOutput, calls=%fused_computation.20 | convolution fusion | flops 53772288 | bytes 4456448 | tf_op jit(solution)/shard_map/zxy,yr->xzr/dot_general | solution.py:66
  57.6 38.3 %all-reduce.1 = bf16[64,1536]{1,0:T(8,128)(2,1)} all-reduce(f32[64,1536]{1,0:T(8,128)S(1)} %bitcast.54), channel_id=1, replica_groups=mesh['gx'=32,'gy'=8] {'gy'}, use_global_device_ids=true, to_apply=%region_0.0 | all-reduce | flops 98304 | bytes 589824 | tf_op jit(solution)/shard_map/psum | solution.py:75
  95.9 0.0 all-gather.2.cloned.1.call-update
  95.9 95.2 %all-gather.2.cloned.1.call-done = bf16[2048,1536]{1,0:T(8,128)(2,1)} async-done(((bf16[64,1536]{1,0:T(8,128)(2,1)}), bf16[2048,1536]{1,0:T(8,128)(2,1)}) %all-gather.2.cloned.1.call-update) | async-done | bytes 6291472 | tf_op jit(solution)/shard_map/all_gather | solution.py:79
  191.0 5.7 %convolution_multiply_fusion = f32[64,2048]{1,0:T(8,128)} fusion(bf16[64,1536]{1,0:T(8,128)(2,1)} %all-reduce.1, bf16[2048,1536]{1,0:T(8,128)(2,1)} %all-gather.2.cloned.1.call-done), kind=kOutput, calls=%fused_computation.19 | convolution fusion | flops 402784256 | bytes 7012352 | tf_op jit(solution)/shard_map/dot_general | solution.py:77
  (1 shorter events, 0.0 us)
Async XLA Ops:
  6.5 48.0 %copy-start = (bf16[256,256]{1,0:T(8,128)(2,1)S(1)}, bf16[256,256]{1,0:T(8,128)(2,1)}, u32[]{:S(2)}) copy-start(bf16[256,256]{1,0:T(8,128)(2,1)} %param.5) | copy-start | bytes 393220
  6.5 184.5 %all-gather.2.cloned.1.call-start = ((), (), s32[]{:S(2)}) async-start(), calls=%async_computation | async-start | bytes 6488064 | tf_op jit(solution)/shard_map/all_gather | solution.py:79
  7.6 26.5 %collective-permute-start.1 = (f32[3,6,2,256]{3,2,1,0:T(2,128)S(1)}, f32[3,6,2,256]{3,2,1,0:T(2,128)S(1)}, u32[]{:S(2)}, u32[]{:S(2)}) collective-permute-start(f32[3,6,2,256]{3,2,1,0:T(2,128)S(1)} %get-tuple-element.15), channel_id=1, source_target_pairs={{0,8},{8,16},{16,24},{24,32},{32,40},{40,48},{48,56},{56,64},{64,7... | collective-permute-start | bytes 110600 | tf_op jit(solution)/shard_map/ppermute | solution.py:13
  7.7 28.6 %collective-permute-start = (f32[3,6,2,256]{3,2,1,0:T(2,128)S(1)}, f32[3,6,2,256]{3,2,1,0:T(2,128)S(1)}, u32[]{:S(2)}, u32[]{:S(2)}) collective-permute-start(f32[3,6,2,256]{3,2,1,0:T(2,128)S(1)} %get-tuple-element.14), channel_id=1, source_target_pairs={{8,0},{16,8},{24,16},{32,24},{40,32},{48,40},{56,48},{64,56},{72,6... | collective-permute-start | bytes 110600 | tf_op jit(solution)/shard_map/ppermute | solution.py:16
  31.1 1.9 slice-start
  38.4 5.2 %copy-start.1 = (f32[3,6,2,256]{2,3,1,0:T(8,128)S(1)}, f32[3,6,2,256]{2,3,1,0:T(8,128)}, u32[]{:S(2)}) copy-start(f32[3,6,2,256]{2,3,1,0:T(8,128)} %copy.22) | copy-start | bytes 110596
  38.4 5.2 %copy-start.2 = (f32[3,6,2,256]{2,3,1,0:T(8,128)S(1)}, f32[3,6,2,256]{2,3,1,0:T(8,128)}, u32[]{:S(2)}) copy-start(f32[3,6,2,256]{2,3,1,0:T(8,128)} %copy.21) | copy-start | bytes 110596
  39.7 8.3 %collective-permute-start.2 = (f32[3,6,68,2]{2,3,1,0:T(2,128)S(1)}, f32[3,6,68,2]{2,3,1,0:T(2,128)S(1)}, u32[]{:S(2)}, u32[]{:S(2)}) collective-permute-start(f32[3,6,68,2]{2,3,1,0:T(2,128)S(1)} %get-tuple-element.7), channel_id=1, source_target_pairs={{1,0},{2,1},{3,2},{4,3},{5,4},{6,5},{7,6},{0,7},{9,8},{10,9},{11,1... | collective-permute-start | bytes 29384 | tf_op jit(solution)/shard_map/ppermute | solution.py:16
  43.6 5.9 %collective-permute-start.3 = (f32[3,6,68,2]{2,3,1,0:T(2,128)S(1)}, f32[3,6,68,2]{2,3,1,0:T(2,128)S(1)}, u32[]{:S(2)}, u32[]{:S(2)}) collective-permute-start(f32[3,6,68,2]{2,3,1,0:T(2,128)S(1)} %get-tuple-element.8), channel_id=1, source_target_pairs={{0,1},{1,2},{2,3},{3,4},{4,5},{5,6},{6,7},{7,0},{8,9},{9,10},{10,1... | collective-permute-start | bytes 29384 | tf_op jit(solution)/shard_map/ppermute | solution.py:13
  52.0 2.5 %copy-start.3 = (f32[6,64,256]{1,2,0:T(8,128)S(1)}, f32[6,64,256]{1,2,0:T(8,128)}, u32[]{:S(2)}) copy-start(f32[6,64,256]{1,2,0:T(8,128)} %copy.28) | copy-start | bytes 1179652
Sparse Core Ops, SparseCore 0:
  96.0 94.9 all-gather.1
where the time goes:
time: 206 us; the launch traced here: 204 us
  waiting for transfers between devices  96.6 us (47%)
  blocking collectives  38.3 us (19%)
  local copies, waits for them, and re-layouts  24.7 us (12%)
  other arithmetic  16.1 us (8%)
  between operations  13.5 us (7%)
  matrix products  8.73 us (4%)
  starting transfers between devices  5.67 us (3%)
    all_gather x1, waiting for transfers between devices, body(): lax.all_gather(core, 'gx', axis=0, tiled=True)  95.2 us
    psum x1, blocking collectives, body(): summed = lax.psum(flat_core, 'gy')  38.3 us
    unnamed x14, local copies, waits for them, and re-layouts  13.6 us
    slice x1, local copies, waits for them, and re-layouts, body(): flow_speed_vectors[:, 4:]  5.78 us
    dot_general x1, matrix products, body(): lax.dot_general(core, lax.all_gather(core, 'gx', axis=0, tiled=True), (((...  5.7 us
    ppermute x2, starting transfers between devices, extended(): lax.ppermute(lax.slice_in_dim(block, 0, width, axis=dim), axis, backward)  5.58 us
    div x1, other arithmetic, body(): (-flow_speed_vectors[:, 4:] + 8.0 * flow_speed_vectors[:, 3:-1] - 8.0 * f...  5.34 us
    div x1, other arithmetic, body(): (-padded[:, :, 4:, 2:-2] + 8.0 * padded[:, :, 3:-1, 2:-2] - 8.0 * padded[...  4.42 us
  transfers between devices with their start and end apart: 5, of which 2 were waited for; matrix products, arithmetic and copies ran while one was open for 15% of the time, Pallas kernels for 0%

commit v1 on v0

v1 whole, which is shorter than its diff:
```python
import jax
import jax.numpy as jnp
from jax import lax
from jax.experimental import pallas as pl
from jax.experimental.pallas import tpu as pltpu
from jax.sharding import Mesh
from jax.sharding import PartitionSpec as P

VMEM = pl.BlockSpec(memory_space=pltpu.VMEM)
NEAR = ("core", "x", "y_lo")
FAR = ("y_hi", "z")
EAST = ("y_hi", "z", "core")
NORTH = ("x", "y_lo")
LIMIT = 48 * 1024 * 1024


def params():
    return pltpu.CompilerParams(vmem_limit_bytes=LIMIT)


def shifted(value, axes, step):
    count = lax.axis_size(axes)
    return lax.ppermute(value, axes, [(k, (k + step) % count) for k in range(count)])


def faces_kernel(flow, x_first, x_last, y_first, y_last):
    planes = x_first.shape[1]
    lane = lax.broadcasted_iota(jnp.int32, y_first.shape, 1)
    first = jnp.zeros(y_first.shape, jnp.float32)
    last = jnp.zeros(y_first.shape, jnp.float32)
    width = flow.shape[3]
    rows = flow.shape[2]
    for comp in range(3):
        for plane in range(planes):
            x_first[comp, plane] = flow[comp, plane + 2, 0:2, :]
            x_last[comp, plane] = flow[comp, plane + 2, rows - 2 : rows, :]
            at = 2 * (comp * planes + plane)
            here = (lane == at) | (lane == at + 1)
            low = flow[comp, plane + 2, :, 0:128]
            high = flow[comp, plane + 2, :, width - 128 : width]
            first = jnp.where(here, pltpu.roll(low, at, 1) if at else low, first)
            last = jnp.where(here, pltpu.roll(high, (at + 2) % 128, 1), last)
    y_first[...] = first
    y_last[...] = last


def difference(ahead_two, ahead_one, behind_one, behind_two):
    return (8.0 * (ahead_one - behind_one) - (ahead_two - behind_two)) * (1.0 / 12.0)


def field_kernel(flow, thermal, basis, x_low, x_high, y_low, y_high, out, padded):
    planes = thermal.shape[0] - 4
    rows, width = thermal.shape[1], thermal.shape[2]
    rank = basis.shape[1]
    matrix = basis[...]
    lane = lax.broadcasted_iota(jnp.int32, (rows, 128), 1)
    for plane in range(planes):
        grads = []
        for comp in range(3):
            here = flow[comp, plane + 2]
            along_z = difference(
                flow[comp, plane + 4], flow[comp, plane + 3], flow[comp, plane + 1], flow[comp, plane]
            )
            padded[comp, 8 : 8 + rows, :] = here
            padded[comp, 6:8, :] = x_low[comp, plane]
            padded[comp, 8 + rows : 10 + rows, :] = x_high[comp, plane]
            along_x = difference(
                padded[comp, 10 : 10 + rows, :],
                padded[comp, 9 : 9 + rows, :],
                padded[comp, 7 : 7 + rows, :],
                padded[comp, 6 : 6 + rows, :],
            )
            at = 2 * (comp * planes + plane)
            low = pltpu.roll(y_low[...], 126 - at, 1)
            high = pltpu.roll(y_high[...], (128 - at) % 128, 1) if at else y_high[...]
            halo = jnp.where(lane < 64, high, low)
            wide = jnp.concatenate([here, halo], axis=1)
            total = width + 128
            along_y = difference(
                pltpu.roll(wide, total - 2, 1)[:, :width],
                pltpu.roll(wide, total - 1, 1)[:, :width],
                pltpu.roll(wide, 1, 1)[:, :width],
                pltpu.roll(wide, 2, 1)[:, :width],
            )
            grads.append((along_z, along_x, along_y))
        diagonal = grads[0][0] * grads[0][0] + grads[1][1] * grads[1][1] + grads[2][2] * grads[2][2]
        cross = None
        for a, b in ((0, 1), (0, 2), (1, 2)):
            both = grads[a][b] + grads[b][a]
            cross = both * both if cross is None else cross + both * both
        expansion = grads[0][0] + grads[1][1] + grads[2][2]
        rate = 2.0 * diagonal + cross - (2.0 / 3.0) * (expansion * expansion)
        field = 0.1 * jnp.exp(0.7 * jnp.log(thermal[plane + 2])) * rate
        out[:, plane * rank : (plane + 1) * rank] = jnp.dot(
            field.astype(jnp.bfloat16), matrix, preferred_element_type=jnp.float32
        )


def sum_kernel(parts, near, far):
    total = parts[0]
    for part in range(1, parts.shape[0]):
        total = total + parts[part]
    piece = total.astype(jnp.bfloat16)
    for at in range(near.shape[0]):
        near[at] = piece
    for at in range(far.shape[0]):
        far[at] = piece


def block_kernel(scale, left, right, out):
    count, piece, depth = left.shape
    a = left[...].reshape(count * piece, depth)
    w = right[...].reshape(right.shape[0] * piece, depth)
    block = lax.dot_general(w, a, (((1,), (1,)), ((), ())), preferred_element_type=jnp.float32)
    block = block * scale
    half = block.shape[0] // 2
    side = block.shape[1] // 2
    top, bottom = block[:half], block[half:]
    first = jnp.concatenate([top[:, :side], bottom[:, :side]], axis=1)
    second = jnp.concatenate([top[:, side:], bottom[:, side:]], axis=1)
    copies = out.shape[0] // 2
    for at in range(copies):
        out[at] = first
        out[copies + at] = second


def place_kernel(piece, blocks, out):
    count, half, _ = blocks.shape
    tiles = half // piece
    side = out.shape[0]
    for tile in range(tiles):
        stacked = jnp.concatenate(
            [blocks[at, tile * piece : (tile + 1) * piece, :] for at in range(count)], axis=0
        )
        turned = stacked.T
        out[:, tile * 128 : (tile + 1) * 128] = turned[:side]
        out[:, (tiles + tile) * 128 : (tiles + tile + 1) * 128] = turned[side:]


def body(flow, thermal, basis):
    planes = thermal.shape[0] - 4
    rows, width = thermal.shape[1], thermal.shape[2]
    rank = basis.shape[1]
    f32 = jnp.float32
    x_face = jax.ShapeDtypeStruct((3, planes, 2, width), f32)
    y_face = jax.ShapeDtypeStruct((rows, 128), f32)
    x_first, x_last, y_first, y_last = pl.pallas_call(
        faces_kernel,
        out_shape=(x_face, x_face, y_face, y_face),
        in_specs=[VMEM],
        out_specs=(VMEM,) * 4,
        compiler_params=params(),
        name="faces",
    )(flow)
    x_low = shifted(x_last, EAST, 1)
    x_high = shifted(x_first, EAST, -1)
    y_low = shifted(y_last, NORTH, 1)
    y_high = shifted(y_first, NORTH, -1)
    partial = pl.pallas_call(
        field_kernel,
        out_shape=jax.ShapeDtypeStruct((rows, planes * rank), f32),
        in_specs=[VMEM] * 7,
        out_specs=VMEM,
        scratch_shapes=[pltpu.VMEM((3, rows + 16, width), f32)],
        compiler_params=params(),
        name="field",
    )(flow, thermal, basis, x_low, x_high, y_low, y_high)
    north = lax.axis_size(NORTH)
    near = lax.axis_size(NEAR)
    far = lax.axis_size(FAR)
    piece = rows // north
    depth = planes * rank
    parts = lax.all_to_all(partial.reshape(north, piece, depth), NORTH, 0, 0)
    to_near, to_far = pl.pallas_call(
        sum_kernel,
        out_shape=(
            jax.ShapeDtypeStruct((near, piece, depth), jnp.bfloat16),
            jax.ShapeDtypeStruct((far, piece, depth), jnp.bfloat16),
        ),
        in_specs=[VMEM],
        out_specs=(VMEM, VMEM),
        compiler_params=params(),
        name="total",
    )(parts)
    left = lax.all_to_all(to_near, NEAR, 0, 0)
    right = lax.all_to_all(to_far, FAR, 0, 0)
    scale = 1.0 / depth
    block = pl.pallas_call(
        lambda *refs: block_kernel(scale, *refs),
        out_shape=jax.ShapeDtypeStruct((near, far * piece // 2, 128), f32),
        in_specs=[VMEM, VMEM],
        out_specs=VMEM,
        compiler_params=params(),
        name="block",
    )(left, right)
    blocks = lax.all_to_all(block, NEAR, 0, 0)
    return pl.pallas_call(
        lambda *refs: place_kernel(piece, *refs),
        out_shape=jax.ShapeDtypeStruct((rows, far * 128), f32),
        in_specs=[VMEM],
        out_specs=VMEM,
        compiler_params=params(),
        name="place",
    )(blocks)


def solution(mesh):
    fine = Mesh(mesh.devices.reshape(2, 8, 2, 4, 2), ("y_hi", "z", "core", "x", "y_lo"))
    placed = (P(None, None, EAST, NORTH), P(None, EAST, NORTH), P(NORTH, None))
    return jax.shard_map(body, mesh=fine, in_specs=placed, out_specs=P(EAST, None), check_vma=False)
```

time: 206 us -> 80.4 us (0.39)
  waiting for transfers between devices: 96.6 us -> 1.92 us
  blocking collectives: 38.3 us -> 64.9 us
  local copies, waits for them, and re-layouts: 24.7 us -> 1.55 us
  other arithmetic: 16.1 us -> 0 us
  between operations: 13.5 us -> 0.06 us
  matrix products: 8.73 us -> 0 us
  Pallas kernels: 0 us -> 4.89 us
    all_gather x1 -> x0, waiting for transfers between devices: 95.2 us -> none  [body(): lax.all_gather(core, 'gx', axis=0, tiled=True)]
    all_to_all x0 -> x4, blocking collectives: none -> 64.9 us  [the longest x1 25.5 us: body(): right = lax.all_to_all(to_far, FAR, 0, 0)]
    psum x1 -> x0, blocking collectives: 38.3 us -> none  [body(): summed = lax.psum(flat_core, 'gy')]
    div x3 -> x0, other arithmetic: 12.3 us -> none  [the longest x1 5.34 us: body(): (-flow_speed_vectors[:, 4:] + 8.0 * flow_speed_vectors[:, 3:-1] - 8.0 * f...]
    unnamed x14 -> x6, local copies, waits for them, and re-layouts: 13.6 us -> 1.55 us
    dot_general x2 -> x0, matrix products: 8.73 us -> none  [the longest x1 5.7 us: body(): lax.dot_general(core, lax.all_gather(core, 'gx', axis=0, tiled=True), (((...]
    slice x4 -> x0, local copies, waits for them, and re-layouts: 6.83 us -> none  [the longest x1 5.78 us: body(): flow_speed_vectors[:, 4:]]
    pallas_call x0 -> x5, Pallas kernels: none -> 4.89 us  [the longest x1 3.14 us: body(): pl.pallas_call(field_kernel, out_shape=jax.ShapeDtypeStruct((rows, planes...]
  transfers between devices with their start and end apart: 5 -> 4, of which waited for: 2 -> 1; matrix products, arithmetic and copies ran while one was open for 15% -> 0% of each run, Pallas kernels for 0% -> 0%
where the time goes in v1:
time: 80.4 us; the launch traced here: 79.2 us
  blocking collectives  64.9 us (81%)
  starting transfers between devices  5.95 us (7%)
  Pallas kernels  4.89 us (6%)
  waiting for transfers between devices  1.92 us (2%)
  local copies, waits for them, and re-layouts  1.55 us (2%)
    all_to_all x1, blocking collectives, body(): right = lax.all_to_all(to_far, FAR, 0, 0)  25.5 us
    all_to_all x1, blocking collectives, body(): blocks = lax.all_to_all(block, NEAR, 0, 0)  14 us
    all_to_all x1, blocking collectives, body(): parts = lax.all_to_all(partial.reshape(north, piece, depth), NORTH, 0, 0)  13 us
    all_to_all x1, blocking collectives, body(): left = lax.all_to_all(to_near, NEAR, 0, 0)  12.3 us
    ppermute x4, starting transfers between devices, shifted(): lax.ppermute(value, axes, [(k, (k + step) % count) for k in range(count)])  5.95 us
    pallas_call x1, Pallas kernels, body(): pl.pallas_call(field_kernel, out_shape=jax.ShapeDtypeStruct((rows, planes...  3.14 us
    ppermute x4, waiting for transfers between devices, shifted(): lax.ppermute(value, axes, [(k, (k + step) % count) for k in range(count)])  1.92 us
  transfers between devices with their start and end apart: 4, of which 1 were waited for; matrix products, arithmetic and copies ran while one was open for 0% of the time, Pallas kernels for 0%

profile of v1, /device:TPU:32, one launch (start us, length us, event | category | flops | bytes accessed | tf_op | source)
XLA Modules:
  0.0 79.2 jit_solution(5785991640145722720)
XLA Ops:
  0.0 0.0 copy-start
  0.0 1.5 %copy-done = f32[3,10,64,256]{3,2,1,0:T(8,128)S(1)} copy-done((f32[3,10,64,256]{3,2,1,0:T(8,128)S(1)}, f32[3,10,64,256]{3,2,1,0:T(8,128)}, u32[]{:S(2)}) %copy-start) | copy-done | bytes 1966104
  1.5 0.0 copy-start.1
  1.5 0.0 copy-start.2
  1.6 0.4 faces.1
  1.9 0.1 collective-permute-start
  2.0 1.7 %collective-permute-start.1 = (f32[3,6,2,256]{3,2,1,0:T(2,128)S(1)}, f32[3,6,2,256]{3,2,1,0:T(2,128)S(1)}, u32[]{:S(2)}, u32[]{:S(2)}) collective-permute-start(f32[3,6,2,256]{3,2,1,0:T(2,128)S(1)} %get-tuple-element.12), channel_id=1, source_target_pairs={{0,248},{8,0},{16,8},{24,16},{32,24},{40,32},{48,40},{56,48},{64,5... | collective-permute-start | bytes 110600 | tf_op jit(solution)/shard_map/ppermute | solution.py:23
  3.7 1.6 %collective-permute-start.2 = (f32[64,128]{1,0:T(8,128)S(1)}, f32[64,128]{1,0:T(8,128)S(1)}, u32[]{:S(2)}, u32[]{:S(2)}) collective-permute-start(f32[64,128]{1,0:T(8,128)S(1)} %get-tuple-element.13), channel_id=1, source_target_pairs={{0,1},{1,2},{2,3},{3,4},{4,5},{5,6},{6,7},{7,0},{8,9},{9,10},{10,1... | collective-permute-start | bytes 98312 | tf_op jit(solution)/shard_map/ppermute | solution.py:23
  5.3 2.6 %collective-permute-start.3 = (f32[64,128]{1,0:T(8,128)S(1)}, f32[64,128]{1,0:T(8,128)S(1)}, u32[]{:S(2)}, u32[]{:S(2)}) collective-permute-start(f32[64,128]{1,0:T(8,128)S(1)} %get-tuple-element.14), channel_id=1, source_target_pairs={{0,7},{1,0},{2,1},{3,2},{4,3},{5,4},{6,5},{7,6},{8,15},{9,8},{10,9... | collective-permute-start | bytes 98312 | tf_op jit(solution)/shard_map/ppermute | solution.py:23
  7.9 1.9 %collective-permute-done.2.y_low = f32[64,128]{1,0:T(8,128)S(1)} collective-permute-done((f32[64,128]{1,0:T(8,128)S(1)}, f32[64,128]{1,0:T(8,128)S(1)}, u32[]{:S(2)}, u32[]{:S(2)}) %collective-permute-start.2) | collective-permute-done | bytes 32800 | tf_op jit(solution)/shard_map/ppermute | solution.py:23
  9.8 0.0 collective-permute-done.3.y_high
  9.8 0.0 collective-permute-done.x_low
  9.8 0.0 collective-permute-done.1.x_high
  9.8 0.0 copy-done.1
  9.8 0.0 copy-done.2
  9.8 3.1 %field.1 = f32[64,1536]{1,0:T(8,128)S(1)} custom-call(f32[3,10,64,256]{3,2,1,0:T(8,128)S(1)} %copy-done, f32[10,64,256]{2,1,0:T(8,128)S(1)} %copy-done.1, bf16[256,256]{1,0:T(8,128)(2,1)S(1)} %copy-done.2, f32[3,6,2,256]{3,2,1,0:T(2,128)S(1)} %collective-permute-done.x_low, f32[3,6,2,256]{3,2,1,0:T(2,128)S(1)} %collective-permute-done.1.x_high, ...), custom_call_target="tpu_custom_call" | custom-call | tf_op jit(solution)/shard_map/field/pallas_call | solution.py:159
  13.0 13.0 %all_to_all.20.parts = f32[8,8,1536]{2,1,0:T(8,128)S(1)} all-to-all(f32[8,8,1536]{2,1,0:T(8,128)S(1)} %bitcast.1), channel_id=1, replica_groups=mesh['y_hi'=2,'z'=8,'core'=2,'x'=4,'y_lo'=2] {'x','y_lo'}, dimensions={0} | all-to-all | bytes 786432 | tf_op jit(solution)/shard_map/all_to_all | solution.py:173
  25.9 0.1 total.1
  26.0 12.3 %all_to_all.21.refs_0_ = bf16[16,8,1536]{2,1,0:T(8,128)(2,1)S(1)} all-to-all(bf16[16,8,1536]{2,1,0:T(8,128)(2,1)S(1)} %get-tuple-element.15), channel_id=1, replica_groups=mesh['y_hi'=2,'z'=8,'core'=2,'x'=4,'y_lo'=2] {'core','x','y_lo'}, dimensions={0} | all-to-all | bytes 786432 | tf_op jit(solution)/shard_map/all_to_all | solution.py:185
  38.3 25.5 %all_to_all.22.refs_1_ = bf16[16,8,1536]{2,1,0:T(8,128)(2,1)S(1)} all-to-all(bf16[16,8,1536]{2,1,0:T(8,128)(2,1)S(1)} %get-tuple-element.16), channel_id=1, replica_groups=mesh['y_hi'=2,'z'=8,'core'=2,'x'=4,'y_lo'=2] {'y_hi','z'}, dimensions={0} | all-to-all | bytes 786432 | tf_op jit(solution)/shard_map/all_to_all | solution.py:186
  63.9 0.3 block.1
  64.2 14.0 %all_to_all.23.refs_0_ = f32[16,64,128]{2,1,0:T(8,128)S(1)} all-to-all(f32[16,64,128]{2,1,0:T(8,128)S(1)} %block.1), channel_id=1, replica_groups=mesh['y_hi'=2,'z'=8,'core'=2,'x'=4,'y_lo'=2] {'core','x','y_lo'}, dimensions={0} | all-to-all | bytes 1048576 | tf_op jit(solution)/shard_map/all_to_all | solution.py:196
  78.2 1.0 %place.1 = f32[64,2048]{1,0:T(8,128)} custom-call(f32[16,64,128]{2,1,0:T(8,128)S(1)} %all_to_all.23.refs_0_), custom_call_target="tpu_custom_call" | custom-call | tf_op jit(solution)/shard_map/place/pallas_call | solution.py:197
Async XLA Ops:
  0.0 1.5 %copy-start = (f32[3,10,64,256]{3,2,1,0:T(8,128)S(1)}, f32[3,10,64,256]{3,2,1,0:T(8,128)}, u32[]{:S(2)}) copy-start(f32[3,10,64,256]{3,2,1,0:T(8,128)} %flow.3) | copy-start | bytes 5898244
  1.5 8.3 %copy-start.1 = (f32[10,64,256]{2,1,0:T(8,128)S(1)}, f32[10,64,256]{2,1,0:T(8,128)}, u32[]{:S(2)}) copy-start(f32[10,64,256]{2,1,0:T(8,128)} %thermal.1) | copy-start | bytes 1966084
  1.5 8.3 %copy-start.2 = (bf16[256,256]{1,0:T(8,128)(2,1)S(1)}, bf16[256,256]{1,0:T(8,128)(2,1)}, u32[]{:S(2)}) copy-start(bf16[256,256]{1,0:T(8,128)(2,1)} %basis.1) | copy-start | bytes 393220
  1.9 7.9 %collective-permute-start = (f32[3,6,2,256]{3,2,1,0:T(2,128)S(1)}, f32[3,6,2,256]{3,2,1,0:T(2,128)S(1)}, u32[]{:S(2)}, u32[]{:S(2)}) collective-permute-start(f32[3,6,2,256]{3,2,1,0:T(2,128)S(1)} %get-tuple-element.11), channel_id=1, source_target_pairs={{0,8},{8,16},{16,24},{24,32},{32,40},{40,48},{48,56},{56,64},{64,7... | collective-permute-start | bytes 110600 | tf_op jit(solution)/shard_map/ppermute | solution.py:23
  2.0 7.8 %collective-permute-start.1 = (f32[3,6,2,256]{3,2,1,0:T(2,128)S(1)}, f32[3,6,2,256]{3,2,1,0:T(2,128)S(1)}, u32[]{:S(2)}, u32[]{:S(2)}) collective-permute-start(f32[3,6,2,256]{3,2,1,0:T(2,128)S(1)} %get-tuple-element.12), channel_id=1, source_target_pairs={{0,248},{8,0},{16,8},{24,16},{32,24},{40,32},{48,40},{56,48},{64,5... | collective-permute-start | bytes 110600 | tf_op jit(solution)/shard_map/ppermute | solution.py:23
  3.7 6.0 %collective-permute-start.2 = (f32[64,128]{1,0:T(8,128)S(1)}, f32[64,128]{1,0:T(8,128)S(1)}, u32[]{:S(2)}, u32[]{:S(2)}) collective-permute-start(f32[64,128]{1,0:T(8,128)S(1)} %get-tuple-element.13), channel_id=1, source_target_pairs={{0,1},{1,2},{2,3},{3,4},{4,5},{5,6},{6,7},{7,0},{8,9},{9,10},{10,1... | collective-permute-start | bytes 98312 | tf_op jit(solution)/shard_map/ppermute | solution.py:23
  5.3 4.5 %collective-permute-start.3 = (f32[64,128]{1,0:T(8,128)S(1)}, f32[64,128]{1,0:T(8,128)S(1)}, u32[]{:S(2)}, u32[]{:S(2)}) collective-permute-start(f32[64,128]{1,0:T(8,128)S(1)} %get-tuple-element.14), channel_id=1, source_target_pairs={{0,7},{1,0},{2,1},{3,2},{4,3},{5,4},{6,5},{7,6},{8,15},{9,8},{10,9... | collective-permute-start | bytes 98312 | tf_op jit(solution)/shard_map/ppermute | solution.py:23

commit v2 on v1

v2 whole, which is shorter than its diff:
```python
import jax
import jax.numpy as jnp
from jax import lax
from jax.experimental import pallas as pl
from jax.experimental.pallas import tpu as pltpu
from jax.sharding import Mesh
from jax.sharding import PartitionSpec as P

VMEM = pl.BlockSpec(memory_space=pltpu.VMEM)
FAR = ("y_hi", "z")
EAST = ("y_hi", "z", "core")
NORTH = ("x", "y_lo")
LIMIT = 48 * 1024 * 1024


def params():
    return pltpu.CompilerParams(vmem_limit_bytes=LIMIT)


def exchanged(value, axes, outer):
    count = lax.axis_size(axes)
    flip = [k ^ 1 for k in range(count)]
    if outer:
        flip = [(k + 1 if k % 2 else k - 1) % count for k in range(count)]
    return lax.ppermute(value, axes, list(enumerate(flip)))


def shifted(value, axes, step):
    count = lax.axis_size(axes)
    return lax.ppermute(value, axes, [(k, (k + step) % count) for k in range(count)])


def faces_kernel(flow, x_inner, x_outer, y_inner, y_outer):
    planes = x_inner.shape[1]
    x_even, y_even = lax.axis_index("core") == 0, lax.axis_index("y_lo") == 0
    lane = lax.broadcasted_iota(jnp.int32, y_inner.shape, 1)
    first = jnp.zeros(y_inner.shape, jnp.float32)
    last = jnp.zeros(y_inner.shape, jnp.float32)
    width = flow.shape[3]
    rows = flow.shape[2]
    for comp in range(3):
        for plane in range(planes):
            top = flow[comp, plane + 2, 0:2, :]
            bottom = flow[comp, plane + 2, rows - 2 : rows, :]
            x_inner[comp, plane] = jnp.where(x_even, bottom, top)
            x_outer[comp, plane] = jnp.where(x_even, top, bottom)
            at = 2 * (comp * planes + plane)
            here = (lane == at) | (lane == at + 1)
            low = flow[comp, plane + 2, :, 0:128]
            high = flow[comp, plane + 2, :, width - 128 : width]
            first = jnp.where(here, pltpu.roll(low, at, 1) if at else low, first)
            last = jnp.where(here, pltpu.roll(high, (at + 2) % 128, 1), last)
    y_inner[...] = jnp.where(y_even, last, first)
    y_outer[...] = jnp.where(y_even, first, last)


def difference(ahead_two, ahead_one, behind_one, behind_two):
    return (8.0 * (ahead_one - behind_one) - (ahead_two - behind_two)) * (1.0 / 12.0)


def inner_kernel(flow, thermal, *refs):
    outs, padded = refs[:7], refs[7]
    planes = thermal.shape[0] - 4
    rows, width = thermal.shape[1], thermal.shape[2]
    total = width + 128
    none = jnp.zeros((rows, 128), jnp.float32)
    padded[:, 0:8, :] = jnp.zeros((3, 8, width), jnp.float32)
    padded[:, 8 + rows :, :] = jnp.zeros((3, 8, width), jnp.float32)
    for plane in range(planes):
        grads = []
        for comp in range(3):
            here = flow[comp, plane + 2]
            along_z = difference(
                flow[comp, plane + 4], flow[comp, plane + 3], flow[comp, plane + 1], flow[comp, plane]
            )
            padded[comp, 8 : 8 + rows, :] = here
            along_x = difference(
                padded[comp, 10 : 10 + rows, :],
                padded[comp, 9 : 9 + rows, :],
                padded[comp, 7 : 7 + rows, :],
                padded[comp, 6 : 6 + rows, :],
            )
            wide = jnp.concatenate([here, none], axis=1)
            along_y = difference(
                pltpu.roll(wide, total - 2, 1)[:, :width],
                pltpu.roll(wide, total - 1, 1)[:, :width],
                pltpu.roll(wide, 1, 1)[:, :width],
                pltpu.roll(wide, 2, 1)[:, :width],
            )
            grads.append((along_z, along_x, along_y))
        outs[0][plane] = grads[0][0]
        outs[1][plane] = grads[1][1]
        outs[2][plane] = grads[2][2]
        outs[3][plane] = grads[0][1] + grads[1][0]
        outs[4][plane] = grads[0][2] + grads[2][0]
        outs[5][plane] = grads[1][2] + grads[2][1]
        outs[6][plane] = 0.1 * jnp.exp(0.7 * jnp.log(thermal[plane + 2]))


def field_kernel(*refs):
    parts, basis = refs[:7], refs[7]
    x_inner, x_outer, y_inner, y_outer, out = refs[8:]
    planes, rows, width = parts[0].shape
    rank = basis.shape[1]
    matrix = basis[...]
    x_even, y_even = lax.axis_index("core") == 0, lax.axis_index("y_lo") == 0
    lane = lax.broadcasted_iota(jnp.int32, (rows, 128), 1)
    even = lane % 2 == 0
    y_low = jnp.where(y_even, y_outer[...], y_inner[...])
    y_high = jnp.where(y_even, y_inner[...], y_outer[...])
    y_low = jnp.where(even, y_low - 8.0 * pltpu.roll(y_low, 127, 1), y_low) * (1.0 / 12.0)
    y_high = jnp.where(even, -y_high, 8.0 * pltpu.roll(y_high, 1, 1) - y_high) * (1.0 / 12.0)
    blank = jnp.zeros((6, width), jnp.float32)

    def with_x(value, comp, plane):
        inner, outer = x_inner[comp, plane], x_outer[comp, plane]
        low = jnp.where(x_even, outer, inner)
        high = jnp.where(x_even, inner, outer)
        head = jnp.concatenate([low[0:1] - 8.0 * low[1:2], low[1:2], blank], axis=0)
        tail = jnp.concatenate([blank, -high[0:1], 8.0 * high[0:1] - high[1:2]], axis=0)
        return jnp.concatenate(
            [value[:8] + head * (1.0 / 12.0), value[8 : rows - 8], value[rows - 8 :] + tail * (1.0 / 12.0)],
            axis=0,
        )

    def with_y(value, comp, plane):
        at = 2 * (comp * planes + plane)
        low = pltpu.roll(y_low, 128 - at, 1) if at else y_low
        high = pltpu.roll(y_high, 126 - at, 1)
        return jnp.concatenate(
            [
                value[:, :128] + jnp.where(lane < 2, low, 0.0),
                        value[:, width - 128 :] + jnp.where(lane >= 126, high, 0.0),
            ],
            axis=1,
        )

    for plane in range(planes):
        along = parts[0][plane]
        down = with_x(parts[1][plane], 1, plane)
        over = with_y(parts[2][plane], 2, plane)
        cross_x = with_x(parts[3][plane], 0, plane)
        cross_y = with_y(parts[4][plane], 0, plane)
        cross_xy = with_x(with_y(parts[5][plane], 1, plane), 2, plane)
        expansion = along + down + over
        rate = (
            2.0 * (along * along + down * down + over * over)
            + (cross_x * cross_x + cross_y * cross_y + cross_xy * cross_xy)
            - (2.0 / 3.0) * (expansion * expansion)
        )
        field = parts[6][plane] * rate
        out[:, plane * rank : (plane + 1) * rank] = jnp.dot(
            field.astype(jnp.bfloat16), matrix, preferred_element_type=jnp.float32
        )


def sum_kernel(parts, own, far):
    total = parts[0]
    for part in range(1, parts.shape[0]):
        total = total + parts[part]
    piece = total.astype(jnp.bfloat16)
    own[0] = piece
    for at in range(far.shape[0]):
        far[at] = piece


def arrange_kernel(*refs):
    pieces, left = refs[:8], refs[8]
    x, y_lo = lax.axis_index("x"), lax.axis_index("y_lo")
    for step in range(4):
        at = 2 * lax.rem(x + step, 4)
        left[at + y_lo] = pieces[step][0]
        left[at + 1 - y_lo] = pieces[4 + step][0]


def block_kernel(scale, left, own, other, out, right):
    core = lax.axis_index("core")
    count, piece, depth = own.shape
    a = left[...].reshape(left.shape[0] * piece, depth)
    half = count // 2
    right[core] = own[...]
    right[1 - core] = other[...]
    sides = []
    for side in range(2):
        w = right[:, side * half : (side + 1) * half].reshape(count * piece, depth)
        sides.append(lax.dot_general(w, a, (((1,), (1,)), ((), ())), preferred_element_type=jnp.float32))
    block = jnp.concatenate(sides, axis=1) * scale
    for at in range(out.shape[0]):
        out[at] = block


def place_kernel(piece, blocks, out):
    count, total, _ = blocks.shape
    tiles = total // (2 * piece)
    side = out.shape[0]
    for tile in range(tiles):
        rows = [
            blocks[at, (core * tiles + tile) * piece : (core * tiles + tile + 1) * piece, :]
            for core in range(2)
            for at in range(count)
        ]
        turned = jnp.concatenate(rows, axis=0).T
        out[:, tile * 128 : (tile + 1) * 128] = turned[:side]
        out[:, (tiles + tile) * 128 : (tiles + tile + 1) * 128] = turned[side:]


def body(flow, thermal, basis):
    planes = thermal.shape[0] - 4
    rows, width = thermal.shape[1], thermal.shape[2]
    rank = basis.shape[1]
    f32 = jnp.float32
    x_face = jax.ShapeDtypeStruct((3, planes, 2, width), f32)
    y_face = jax.ShapeDtypeStruct((rows, 128), f32)
    x_inner, x_outer, y_inner, y_outer = pl.pallas_call(
        faces_kernel,
        out_shape=(x_face, x_face, y_face, y_face),
        in_specs=[VMEM],
        out_specs=(VMEM,) * 4,
        compiler_params=params(),
        name="faces",
    )(flow)
    x_outer = exchanged(x_outer, EAST, True)
    y_outer = exchanged(y_outer, NORTH, True)
    y_inner = exchanged(y_inner, NORTH, False)
    x_inner = exchanged(x_inner, EAST, False)
    parts = pl.pallas_call(
        inner_kernel,
        out_shape=(jax.ShapeDtypeStruct((planes, rows, width), f32),) * 7,
        in_specs=[VMEM, VMEM],
        out_specs=(VMEM,) * 7,
        scratch_shapes=[pltpu.VMEM((3, rows + 16, width), f32)],
        compiler_params=params(),
        cost_estimate=pl.CostEstimate(flops=2_500_000_000, bytes_accessed=5_000_000, transcendentals=0),
        name="inner",
    )(flow, thermal)
    partial = pl.pallas_call(
        field_kernel,
        out_shape=jax.ShapeDtypeStruct((rows, planes * rank), f32),
        in_specs=[VMEM] * 12,
        out_specs=VMEM,
        compiler_params=params(),
        name="field",
    )(*parts, basis, x_inner, x_outer, y_inner, y_outer)
    north = lax.axis_size(NORTH)
    far = lax.axis_size(FAR)
    piece = rows // north
    depth = planes * rank
    gathered = lax.all_to_all(partial.reshape(north, piece, depth), NORTH, 0, 0)
    own, to_far = pl.pallas_call(
        sum_kernel,
        out_shape=(
            jax.ShapeDtypeStruct((1, piece, depth), jnp.bfloat16),
            jax.ShapeDtypeStruct((far, piece, depth), jnp.bfloat16),
        ),
        in_specs=[VMEM],
        out_specs=(VMEM, VMEM),
        compiler_params=params(),
        name="total",
    )(gathered)
    right = lax.all_to_all(to_far, FAR, 0, 0)
    pieces = [own] + [shifted(own, "x", -step) for step in range(1, 4)]
    for step in range(4):
        pairs = [(2 * k + b, 2 * ((k - step) % 4) + 1 - b) for k in range(4) for b in range(2)]
        pieces.append(lax.ppermute(own, NORTH, pairs))
    left = pl.pallas_call(
        arrange_kernel,
        out_shape=jax.ShapeDtypeStruct((north, piece, depth), jnp.bfloat16),
        in_specs=[VMEM] * 8,
        out_specs=VMEM,
        compiler_params=params(),
        cost_estimate=pl.CostEstimate(flops=5_000_000_000, bytes_accessed=4 * piece * depth * north, transcendentals=0),
        name="arrange",
    )(*pieces)
    other = shifted(right, "core", 1)
    scale = 1.0 / depth
    block = pl.pallas_call(
        lambda *refs: block_kernel(scale, *refs),
        out_shape=jax.ShapeDtypeStruct((north, far * piece, 128), f32),
        in_specs=[VMEM] * 3,
        out_specs=VMEM,
        scratch_shapes=[pltpu.VMEM((2, far, piece, depth), jnp.bfloat16)],
        compiler_params=params(),
        name="block",
    )(left, right, other)
    blocks = lax.all_to_all(block, NORTH, 0, 0)
    return pl.pallas_call(
        lambda *refs: place_kernel(piece, *refs),
        out_shape=jax.ShapeDtypeStruct((rows, far * 128), f32),
        in_specs=[VMEM],
        out_specs=VMEM,
        compiler_params=params(),
        name="place",
    )(blocks)


def solution(mesh):
    fine = Mesh(mesh.devices.reshape(2, 8, 2, 4, 2), ("y_hi", "z", "core", "x", "y_lo"))
    placed = (P(None, None, EAST, NORTH), P(None, EAST, NORTH), P(NORTH, None))
    return jax.shard_map(body, mesh=fine, in_specs=placed, out_specs=P(EAST, None), check_vma=False)
```

time: 80.4 us -> 65.1 us (0.81)
  blocking collectives: 64.9 us -> 25.4 us
  starting transfers between devices: 5.95 us -> 26.9 us
  waiting for transfers between devices: 1.92 us -> 5.87 us
    all_to_all x4 -> x2, blocking collectives: 64.9 us -> 25.4 us  [the longest x1 12.7 us: body(): blocks = lax.all_to_all(block, NORTH, 0, 0)]
    all_to_all x0 -> x1, starting transfers between devices: none -> 11.2 us  [body(): right = lax.all_to_all(to_far, FAR, 0, 0)]
    ppermute x0 -> x8, starting transfers between devices: none -> 11 us  [the longest x4 6.45 us: body(): pieces.append(lax.ppermute(own, NORTH, pairs))]
    all_to_all x0 -> x1, waiting for transfers between devices: none -> 2.56 us  [body(): right = lax.all_to_all(to_far, FAR, 0, 0)]
    pallas_call x1, Pallas kernels: 3.14 us -> 0.68 us  [body(): pl.pallas_call(field_kernel, out_shape=jax.ShapeDtypeStruct((rows, planes...]
    pallas_call x1 -> x3, Pallas kernels: 0.06 us -> 2.31 us  [the longest x1 1.5 us: body(): pl.pallas_call(inner_kernel, out_shape=(jax.ShapeDtypeStruct((planes, row...]
    ppermute x0 -> x8, waiting for transfers between devices: none -> 1.66 us  [the longest x4 1.65 us: exchanged(): return lax.ppermute(value, axes, list(enumerate(flip)))]
    ppermute x4, starting transfers between devices: 5.95 us -> 4.7 us  [shifted(): lax.ppermute(value, axes, [(k, (k + step) % count) for k in range(count)])]
  transfers between devices with their start and end apart: 4 -> 13, of which waited for: 1 -> 3; matrix products, arithmetic and copies ran while one was open for 0% -> 0% of each run, Pallas kernels for 0% -> 2%
where the time goes in v2:
time: 65.1 us; the launch traced here: 64.6 us
  starting transfers between devices  26.9 us (41%)
  blocking collectives  25.4 us (39%)
  waiting for transfers between devices  5.87 us (9%)
  Pallas kernels  4.79 us (7%)
  local copies, waits for them, and re-layouts  1.55 us (2%)
    all_to_all x1, blocking collectives, body(): blocks = lax.all_to_all(block, NORTH, 0, 0)  12.7 us
    all_to_all x1, blocking collectives, body(): gathered = lax.all_to_all(partial.reshape(north, piece, depth), NORTH, 0, 0)  12.7 us
    all_to_all x1, starting transfers between devices, body(): right = lax.all_to_all(to_far, FAR, 0, 0)  11.2 us
    ppermute x4, starting transfers between devices, body(): pieces.append(lax.ppermute(own, NORTH, pairs))  6.45 us
    ppermute x4, starting transfers between devices, shifted(): lax.ppermute(value, axes, [(k, (k + step) % count) for k in range(count)])  4.7 us
    ppermute x4, starting transfers between devices, exchanged(): return lax.ppermute(value, axes, list(enumerate(flip)))  4.53 us
    all_to_all x1, waiting for transfers between devices, body(): right = lax.all_to_all(to_far, FAR, 0, 0)  2.56 us
    ppermute x4, waiting for transfers between devices, shifted(): lax.ppermute(value, axes, [(k, (k + step) % count) for k in range(count)])  1.66 us
  transfers between devices with their start and end apart: 13, of which 3 were waited for; matrix products, arithmetic and copies ran while one was open for 0% of the time, Pallas kernels for 2%

profile of v2, /device:TPU:32, one launch (start us, length us, event | category | flops | bytes accessed | tf_op | source)
XLA Modules:
  0.0 64.6 jit_solution(14768209295425205532)
XLA Ops:
  0.0 0.0 copy-start
  0.0 1.5 %copy-done = f32[3,10,64,256]{3,2,1,0:T(8,128)S(1)} copy-done((f32[3,10,64,256]{3,2,1,0:T(8,128)S(1)}, f32[3,10,64,256]{3,2,1,0:T(8,128)}, u32[]{:S(2)}) %copy-start) | copy-done | bytes 1966104
  1.5 0.0 copy-start.2
  1.5 0.4 faces.1
  1.9 1.7 %collective-permute-start.2 = (f32[64,128]{1,0:T(8,128)S(1)}, f32[64,128]{1,0:T(8,128)S(1)}, u32[]{:S(2)}, u32[]{:S(2)}) collective-permute-start(f32[64,128]{1,0:T(8,128)S(1)} %get-tuple-element.27), channel_id=1, source_target_pairs={{0,1},{1,0},{2,3},{3,2},{4,5},{5,4},{6,7},{7,6},{8,9},{9,8},{10,11... | collective-permute-start | bytes 98312 | tf_op jit(solution)/shard_map/ppermute | solution.py:25
  3.6 2.6 %collective-permute-start.3 = (f32[64,128]{1,0:T(8,128)S(1)}, f32[64,128]{1,0:T(8,128)S(1)}, u32[]{:S(2)}, u32[]{:S(2)}) collective-permute-start(f32[64,128]{1,0:T(8,128)S(1)} %get-tuple-element.28), channel_id=1, source_target_pairs={{0,7},{1,2},{2,1},{3,4},{4,3},{5,6},{6,5},{7,0},{8,15},{9,10},{10,... | collective-permute-start | bytes 98312 | tf_op jit(solution)/shard_map/ppermute | solution.py:25
  6.2 0.0 collective-permute-start
  6.2 0.0 copy-start.1
  6.2 0.2 collective-permute-start.1
  6.4 0.0 copy-done.2
  6.5 1.5 %inner.1 = (f32[6,64,256]{2,1,0:T(8,128)S(1)}, f32[6,64,256]{2,1,0:T(8,128)S(1)}, f32[6,64,256]{2,1,0:T(8,128)S(1)}, f32[6,64,256]{2,1,0:T(8,128)S(1)}, f32[6,64...) custom-call(f32[3,10,64,256]{3,2,1,0:T(8,128)S(1)} %copy-done, f32[10,64,256]{2,1,0:T(8,128)S(1)} %copy-done.2), custom_call_target="tpu_custom_call" | custom-call | flops 2500000000 | bytes 5000000 | tf_op jit(solution)/shard_map/inner/pallas_call | solution.py:226
  8.0 0.0 collective-permute-done.2.refs_10_
  8.0 1.6 %collective-permute-done.3.refs_11_ = f32[64,128]{1,0:T(8,128)S(1)} collective-permute-done((f32[64,128]{1,0:T(8,128)S(1)}, f32[64,128]{1,0:T(8,128)S(1)}, u32[]{:S(2)}, u32[]{:S(2)}) %collective-permute-start.3) | collective-permute-done | bytes 32800 | tf_op jit(solution)/shard_map/ppermute | solution.py:25
  9.6 0.0 collective-permute-done.refs_8_
  9.6 0.0 collective-permute-done.1.refs_9_
  9.6 0.0 copy-done.1
  9.6 0.7 %field.1 = f32[64,1536]{1,0:T(8,128)S(1)} custom-call(f32[6,64,256]{2,1,0:T(8,128)S(1)} %get-tuple-element.18.refs_0_, f32[6,64,256]{2,1,0:T(8,128)S(1)} %get-tuple-element.19.refs_1_, f32[6,64,256]{2,1,0:T(8,128)S(1)} %get-tuple-element.20.refs_2_, f32[6,64,256]{2,1,0:T(8,128)S(1)} %get-tuple-element.21.refs_3_, ...), custom_call_target="tpu_custom_call" | custom-call | tf_op jit(solution)/shard_map/field/pallas_call | solution.py:236
  10.3 12.7 %all_to_all.15.parts = f32[8,8,1536]{2,1,0:T(8,128)S(1)} all-to-all(f32[8,8,1536]{2,1,0:T(8,128)S(1)} %bitcast.1), channel_id=1, replica_groups=mesh['y_hi'=2,'z'=8,'core'=2,'x'=4,'y_lo'=2] {'x','y_lo'}, dimensions={0} | all-to-all | bytes 786432 | tf_op jit(solution)/shard_map/all_to_all | solution.py:248
  23.0 0.8 %total.1 = (bf16[1,8,1536]{2,1,0:T(8,128)(2,1)S(1)}, bf16[16,8,1536]{2,1,0:T(8,128)(2,1)}) custom-call(f32[8,8,1536]{2,1,0:T(8,128)S(1)} %all_to_all.15.parts), custom_call_target="tpu_custom_call" | custom-call | tf_op jit(solution)/shard_map/total/pallas_call | solution.py:249
  23.8 11.2 %all-to-all-start.1 = ((bf16[16,8,1536]{2,1,0:T(8,128)(2,1)}), bf16[16,8,1536]{2,1,0:T(8,128)(2,1)S(1)}, u32[]{:S(2)}, u32[]{:S(2)}) async-start(bf16[16,8,1536]{2,1,0:T(8,128)(2,1)} %get-tuple-element.30), calls=%async_computation.1 | async-start | bytes 786432 | tf_op jit(solution)/shard_map/all_to_all | solution.py:260
  35.0 0.4 collective-permute-start.10
  35.4 3.0 %collective-permute-start.9 = (bf16[1,8,1536]{2,1,0:T(8,128)(2,1)S(1)}, bf16[1,8,1536]{2,1,0:T(8,128)(2,1)S(1)}, u32[]{:S(2)}, u32[]{:S(2)}) collective-permute-start(bf16[1,8,1536]{2,1,0:T(8,128)(2,1)S(1)} %get-tuple-element.29.refs_0_), channel_id=1, source_target_pairs={{0,5},{1,4},{2,7},{3,6},{4,1},{5,0},{6,3},{7,2},{8,13},{9,12},{10,... | collective-permute-start | bytes 73736 | tf_op jit(solution)/shard_map/ppermute | solution.py:264
  38.5 0.7 %collective-permute-start.8 = (bf16[1,8,1536]{2,1,0:T(8,128)(2,1)S(1)}, bf16[1,8,1536]{2,1,0:T(8,128)(2,1)S(1)}, u32[]{:S(2)}, u32[]{:S(2)}) collective-permute-start(bf16[1,8,1536]{2,1,0:T(8,128)(2,1)S(1)} %get-tuple-element.29.refs_0_), channel_id=1, source_target_pairs={{0,7},{1,6},{2,1},{3,0},{4,3},{5,2},{6,5},{7,4},{8,15},{9,14},{10,... | collective-permute-start | bytes 73736 | tf_op jit(solution)/shard_map/ppermute | solution.py:264
  39.2 2.2 %collective-permute-start.7 = (bf16[1,8,1536]{2,1,0:T(8,128)(2,1)S(1)}, bf16[1,8,1536]{2,1,0:T(8,128)(2,1)S(1)}, u32[]{:S(2)}, u32[]{:S(2)}) collective-permute-start(bf16[1,8,1536]{2,1,0:T(8,128)(2,1)S(1)} %get-tuple-element.29.refs_0_), channel_id=1, source_target_pairs={{0,1},{1,0},{2,3},{3,2},{4,5},{5,4},{6,7},{7,6},{8,9},{9,8},{10,11... | collective-permute-start | bytes 73736 | tf_op jit(solution)/shard_map/ppermute | solution.py:264
  41.5 0.5 collective-permute-start.6
  42.0 0.0 collective-permute-done.10.refs_7_
  42.0 1.6 %collective-permute-start.5 = (bf16[1,8,1536]{2,1,0:T(8,128)(2,1)S(1)}, bf16[1,8,1536]{2,1,0:T(8,128)(2,1)S(1)}, u32[]{:S(2)}, u32[]{:S(2)}) collective-permute-start(bf16[1,8,1536]{2,1,0:T(8,128)(2,1)S(1)} %get-tuple-element.29.refs_0_), channel_id=1, source_target_pairs={{0,4},{2,6},{4,0},{6,2},{1,5},{3,7},{5,1},{7,3},{8,12},{10,14},{12... | collective-permute-start | bytes 73736 | tf_op jit(solution)/shard_map/ppermute | solution.py:30
  43.5 0.0 collective-permute-done.9.refs_6_
  43.5 2.6 %collective-permute-start.4 = (bf16[1,8,1536]{2,1,0:T(8,128)(2,1)S(1)}, bf16[1,8,1536]{2,1,0:T(8,128)(2,1)S(1)}, u32[]{:S(2)}, u32[]{:S(2)}) collective-permute-start(bf16[1,8,1536]{2,1,0:T(8,128)(2,1)S(1)} %get-tuple-element.29.refs_0_), channel_id=1, source_target_pairs={{0,6},{2,0},{4,2},{6,4},{1,7},{3,1},{5,3},{7,5},{8,14},{10,8},{12,... | collective-permute-start | bytes 73736 | tf_op jit(solution)/shard_map/ppermute | solution.py:30
  46.2 0.0 collective-permute-done.8.refs_5_
  46.2 2.6 %all-to-all-done.1.refs_1_ = bf16[16,8,1536]{2,1,0:T(8,128)(2,1)S(1)} async-done(((bf16[16,8,1536]{2,1,0:T(8,128)(2,1)}), bf16[16,8,1536]{2,1,0:T(8,128)(2,1)S(1)}, u32[]{:S(2)}, u32[]{:S(2)}) %all-to-all-start.1) | async-done | bytes 393248 | tf_op jit(solution)/shard_map/all_to_all | solution.py:260
  48.7 0.0 collective-permute-start.11
  48.7 0.0 collective-permute-done.7.refs_4_
  48.7 0.0 collective-permute-done.6.refs_3_
  48.7 0.0 collective-permute-done.5.refs_2_
  48.8 0.0 collective-permute-done.4.refs_1_
  48.8 1.6 %collective-permute-done.11.refs_2_ = bf16[16,8,1536]{2,1,0:T(8,128)(2,1)S(1)} collective-permute-done((bf16[16,8,1536]{2,1,0:T(8,128)(2,1)S(1)}, bf16[16,8,1536]{2,1,0:T(8,128)(2,1)S(1)}, u32[]{:S(2)}, u32[]{:S(2)}) %collective-permute-start.11) | collective-permute-done | bytes 393248 | tf_op jit(solution)/shard_map/ppermute | solution.py:30
  50.5 0.4 block.1
  50.9 12.7 %all_to_all.16.refs_0_ = f32[8,128,128]{2,1,0:T(8,128)S(1)} all-to-all(f32[8,128,128]{2,1,0:T(8,128)S(1)} %block.1), channel_id=1, replica_groups=mesh['y_hi'=2,'z'=8,'core'=2,'x'=4,'y_lo'=2] {'x','y_lo'}, dimensions={0} | all-to-all | bytes 1048576 | tf_op jit(solution)/shard_map/all_to_all | solution.py:285
  63.6 1.0 %place.1 = f32[64,2048]{1,0:T(8,128)} custom-call(f32[8,128,128]{2,1,0:T(8,128)S(1)} %all_to_all.16.refs_0_), custom_call_target="tpu_custom_call" | custom-call | tf_op jit(solution)/shard_map/place/pallas_call | solution.py:286
  (1 shorter events, 0.0 us)
Async XLA Ops:
  0.0 1.5 %copy-start = (f32[3,10,64,256]{3,2,1,0:T(8,128)S(1)}, f32[3,10,64,256]{3,2,1,0:T(8,128)}, u32[]{:S(2)}) copy-start(f32[3,10,64,256]{3,2,1,0:T(8,128)} %flow.3) | copy-start | bytes 5898244
  1.5 4.9 %copy-start.2 = (f32[10,64,256]{2,1,0:T(8,128)S(1)}, f32[10,64,256]{2,1,0:T(8,128)}, u32[]{:S(2)}) copy-start(f32[10,64,256]{2,1,0:T(8,128)} %thermal.1) | copy-start | bytes 1966084
  1.9 6.0 %collective-permute-start.2 = (f32[64,128]{1,0:T(8,128)S(1)}, f32[64,128]{1,0:T(8,128)S(1)}, u32[]{:S(2)}, u32[]{:S(2)}) collective-permute-start(f32[64,128]{1,0:T(8,128)S(1)} %get-tuple-element.27), channel_id=1, source_target_pairs={{0,1},{1,0},{2,3},{3,2},{4,5},{5,4},{6,7},{7,6},{8,9},{9,8},{10,11... | collective-permute-start | bytes 98312 | tf_op jit(solution)/shard_map/ppermute | solution.py:25
  3.6 6.0 %collective-permute-start.3 = (f32[64,128]{1,0:T(8,128)S(1)}, f32[64,128]{1,0:T(8,128)S(1)}, u32[]{:S(2)}, u32[]{:S(2)}) collective-permute-start(f32[64,128]{1,0:T(8,128)S(1)} %get-tuple-element.28), channel_id=1, source_target_pairs={{0,7},{1,2},{2,1},{3,4},{4,3},{5,6},{6,5},{7,0},{8,15},{9,10},{10,... | collective-permute-start | bytes 98312 | tf_op jit(solution)/shard_map/ppermute | solution.py:25
  6.2 3.4 %collective-permute-start = (f32[3,6,2,256]{3,2,1,0:T(2,128)S(1)}, f32[3,6,2,256]{3,2,1,0:T(2,128)S(1)}, u32[]{:S(2)}, u32[]{:S(2)}) collective-permute-start(f32[3,6,2,256]{3,2,1,0:T(2,128)S(1)} %get-tuple-element.25), channel_id=1, source_target_pairs={{0,8},{8,0},{16,24},{24,16},{32,40},{40,32},{48,56},{56,48},{64,72... | collective-permute-start | bytes 110600 | tf_op jit(solution)/shard_map/ppermute | solution.py:25
  6.2 3.4 %copy-start.1 = (bf16[256,256]{1,0:T(8,128)(2,1)S(1)}, bf16[256,256]{1,0:T(8,128)(2,1)}, u32[]{:S(2)}) copy-start(bf16[256,256]{1,0:T(8,128)(2,1)} %refs_7_.1) | copy-start | bytes 393220
  6.2 3.4 %collective-permute-start.1 = (f32[3,6,2,256]{3,2,1,0:T(2,128)S(1)}, f32[3,6,2,256]{3,2,1,0:T(2,128)S(1)}, u32[]{:S(2)}, u32[]{:S(2)}) collective-permute-start(f32[3,6,2,256]{3,2,1,0:T(2,128)S(1)} %get-tuple-element.26), channel_id=1, source_target_pairs={{0,248},{8,16},{16,8},{24,32},{32,24},{40,48},{48,40},{56,64},{64,... | collective-permute-start | bytes 110600 | tf_op jit(solution)/shard_map/ppermute | solution.py:25
  23.8 24.9 %all-to-all-start.1 = ((bf16[16,8,1536]{2,1,0:T(8,128)(2,1)}), bf16[16,8,1536]{2,1,0:T(8,128)(2,1)S(1)}, u32[]{:S(2)}, u32[]{:S(2)}) async-start(bf16[16,8,1536]{2,1,0:T(8,128)(2,1)} %get-tuple-element.30), calls=%async_computation.1 | async-start | bytes 786432 | tf_op jit(solution)/shard_map/all_to_all | solution.py:260
  35.0 7.0 %collective-permute-start.10 = (bf16[1,8,1536]{2,1,0:T(8,128)(2,1)S(1)}, bf16[1,8,1536]{2,1,0:T(8,128)(2,1)S(1)}, u32[]{:S(2)}, u32[]{:S(2)}) collective-permute-start(bf16[1,8,1536]{2,1,0:T(8,128)(2,1)S(1)} %get-tuple-element.29.refs_0_), channel_id=1, source_target_pairs={{0,3},{1,2},{2,5},{3,4},{4,7},{5,6},{6,1},{7,0},{8,11},{9,10},{10,... | collective-permute-start | bytes 73736 | tf_op jit(solution)/shard_map/ppermute | solution.py:264
  35.4 8.1 %collective-permute-start.9 = (bf16[1,8,1536]{2,1,0:T(8,128)(2,1)S(1)}, bf16[1,8,1536]{2,1,0:T(8,128)(2,1)S(1)}, u32[]{:S(2)}, u32[]{:S(2)}) collective-permute-start(bf16[1,8,1536]{2,1,0:T(8,128)(2,1)S(1)} %get-tuple-element.29.refs_0_), channel_id=1, source_target_pairs={{0,5},{1,4},{2,7},{3,6},{4,1},{5,0},{6,3},{7,2},{8,13},{9,12},{10,... | collective-permute-start | bytes 73736 | tf_op jit(solution)/shard_map/ppermute | solution.py:264
  38.5 7.7 %collective-permute-start.8 = (bf16[1,8,1536]{2,1,0:T(8,128)(2,1)S(1)}, bf16[1,8,1536]{2,1,0:T(8,128)(2,1)S(1)}, u32[]{:S(2)}, u32[]{:S(2)}) collective-permute-start(bf16[1,8,1536]{2,1,0:T(8,128)(2,1)S(1)} %get-tuple-element.29.refs_0_), channel_id=1, source_target_pairs={{0,7},{1,6},{2,1},{3,0},{4,3},{5,2},{6,5},{7,4},{8,15},{9,14},{10,... | collective-permute-start | bytes 73736 | tf_op jit(solution)/shard_map/ppermute | solution.py:264
  39.2 9.5 %collective-permute-start.7 = (bf16[1,8,1536]{2,1,0:T(8,128)(2,1)S(1)}, bf16[1,8,1536]{2,1,0:T(8,128)(2,1)S(1)}, u32[]{:S(2)}, u32[]{:S(2)}) collective-permute-start(bf16[1,8,1536]{2,1,0:T(8,128)(2,1)S(1)} %get-tuple-element.29.refs_0_), channel_id=1, source_target_pairs={{0,1},{1,0},{2,3},{3,2},{4,5},{5,4},{6,7},{7,6},{8,9},{9,8},{10,11... | collective-permute-start | bytes 73736 | tf_op jit(solution)/shard_map/ppermute | solution.py:264
  41.5 7.3 %collective-permute-start.6 = (bf16[1,8,1536]{2,1,0:T(8,128)(2,1)S(1)}, bf16[1,8,1536]{2,1,0:T(8,128)(2,1)S(1)}, u32[]{:S(2)}, u32[]{:S(2)}) collective-permute-start(bf16[1,8,1536]{2,1,0:T(8,128)(2,1)S(1)} %get-tuple-element.29.refs_0_), channel_id=1, source_target_pairs={{0,2},{2,4},{4,6},{6,0},{1,3},{3,5},{5,7},{7,1},{8,10},{10,12},{12... | collective-permute-start | bytes 73736 | tf_op jit(solution)/shard_map/ppermute | solution.py:30
  42.0 6.8 %collective-permute-start.5 = (bf16[1,8,1536]{2,1,0:T(8,128)(2,1)S(1)}, bf16[1,8,1536]{2,1,0:T(8,128)(2,1)S(1)}, u32[]{:S(2)}, u32[]{:S(2)}) collective-permute-start(bf16[1,8,1536]{2,1,0:T(8,128)(2,1)S(1)} %get-tuple-element.29.refs_0_), channel_id=1, source_target_pairs={{0,4},{2,6},{4,0},{6,2},{1,5},{3,7},{5,1},{7,3},{8,12},{10,14},{12... | collective-permute-start | bytes 73736 | tf_op jit(solution)/shard_map/ppermute | solution.py:30
  43.5 5.2 %collective-permute-start.4 = (bf16[1,8,1536]{2,1,0:T(8,128)(2,1)S(1)}, bf16[1,8,1536]{2,1,0:T(8,128)(2,1)S(1)}, u32[]{:S(2)}, u32[]{:S(2)}) collective-permute-start(bf16[1,8,1536]{2,1,0:T(8,128)(2,1)S(1)} %get-tuple-element.29.refs_0_), channel_id=1, source_target_pairs={{0,6},{2,0},{4,2},{6,4},{1,7},{3,1},{5,3},{7,5},{8,14},{10,8},{12,... | collective-permute-start | bytes 73736 | tf_op jit(solution)/shard_map/ppermute | solution.py:30
  48.7 1.7 %collective-permute-start.11 = (bf16[16,8,1536]{2,1,0:T(8,128)(2,1)S(1)}, bf16[16,8,1536]{2,1,0:T(8,128)(2,1)S(1)}, u32[]{:S(2)}, u32[]{:S(2)}) collective-permute-start(bf16[16,8,1536]{2,1,0:T(8,128)(2,1)S(1)} %all-to-all-done.1.refs_1_), channel_id=1, source_target_pairs={{0,8},{8,0},{1,9},{9,1},{2,10},{10,2},{3,11},{11,3},{4,12},{12,4},... | collective-permute-start | bytes 1179656 | tf_op jit(solution)/shard_map/ppermute | solution.py:30

commit v3 on v2

--- a/solution.py
+++ b/solution.py
@@ -33,11 +33,11 @@
 def faces_kernel(flow, x_inner, x_outer, y_inner, y_outer):
     planes = x_inner.shape[1]
     x_even, y_even = lax.axis_index("core") == 0, lax.axis_index("y_lo") == 0
-    lane = lax.broadcasted_iota(jnp.int32, y_inner.shape, 1)
-    first = jnp.zeros(y_inner.shape, jnp.float32)
-    last = jnp.zeros(y_inner.shape, jnp.float32)
     width = flow.shape[3]
     rows = flow.shape[2]
+    lane = lax.broadcasted_iota(jnp.int32, (rows, 128), 1)
+    first = jnp.zeros((rows, 128), jnp.float32)
+    last = jnp.zeros((rows, 128), jnp.float32)
     for comp in range(3):
         for plane in range(planes):
             top = flow[comp, plane + 2, 0:2, :]
@@ -50,8 +50,8 @@
             high = flow[comp, plane + 2, :, width - 128 : width]
             first = jnp.where(here, pltpu.roll(low, at, 1) if at else low, first)
             last = jnp.where(here, pltpu.roll(high, (at + 2) % 128, 1), last)
-    y_inner[...] = jnp.where(y_even, last, first)
-    y_outer[...] = jnp.where(y_even, first, last)
+    y_inner[:rows] = jnp.where(y_even, last, first)
+    y_outer[:rows] = jnp.where(y_even, first, last)
 
 
 def difference(ahead_two, ahead_one, behind_one, behind_two):
@@ -99,15 +99,15 @@
 
 def field_kernel(*refs):
     parts, basis = refs[:7], refs[7]
-    x_inner, x_outer, y_inner, y_outer, out = refs[8:]
+    x_outer, y_outer, y_inner, x_inner, out = refs[8:]
     planes, rows, width = parts[0].shape
     rank = basis.shape[1]
     matrix = basis[...]
     x_even, y_even = lax.axis_index("core") == 0, lax.axis_index("y_lo") == 0
     lane = lax.broadcasted_iota(jnp.int32, (rows, 128), 1)
     even = lane % 2 == 0
-    y_low = jnp.where(y_even, y_outer[...], y_inner[...])
-    y_high = jnp.where(y_even, y_inner[...], y_outer[...])
+    y_low = jnp.where(y_even, y_outer[:rows], y_inner[:rows])
+    y_high = jnp.where(y_even, y_inner[:rows], y_outer[:rows])
     y_low = jnp.where(even, y_low - 8.0 * pltpu.roll(y_low, 127, 1), y_low) * (1.0 / 12.0)
     y_high = jnp.where(even, -y_high, 8.0 * pltpu.roll(y_high, 1, 1) - y_high) * (1.0 / 12.0)
     blank = jnp.zeros((6, width), jnp.float32)
@@ -164,13 +164,16 @@
         far[at] = piece
 
 
-def arrange_kernel(*refs):
-    pieces, left = refs[:8], refs[8]
+def copy_kernel(source, target):
+    target[...] = source[...]
+
+
+def arrange_kernel(near, across, left):
     x, y_lo = lax.axis_index("x"), lax.axis_index("y_lo")
     for step in range(4):
         at = 2 * lax.rem(x + step, 4)
-        left[at + y_lo] = pieces[step][0]
-        left[at + 1 - y_lo] = pieces[4 + step][0]
+        left[at + y_lo] = near[step]
+        left[at + 1 - y_lo] = across[step]
 
 
 def block_kernel(scale, left, own, other, out, right):
@@ -210,7 +213,7 @@
     rank = basis.shape[1]
     f32 = jnp.float32
     x_face = jax.ShapeDtypeStruct((3, planes, 2, width), f32)
-    y_face = jax.ShapeDtypeStruct((rows, 128), f32)
+    y_face = jax.ShapeDtypeStruct((rows + 16, 128), f32)
     x_inner, x_outer, y_inner, y_outer = pl.pallas_call(
         faces_kernel,
         out_shape=(x_face, x_face, y_face, y_face),
@@ -240,7 +243,7 @@
         out_specs=VMEM,
         compiler_params=params(),
         name="field",
-    )(*parts, basis, x_inner, x_outer, y_inner, y_outer)
+    )(*parts, basis, x_outer, y_outer, y_inner, x_inner)
     north = lax.axis_size(NORTH)
     far = lax.axis_size(FAR)
     piece = rows // north
@@ -258,19 +261,26 @@
         name="total",
     )(gathered)
     right = lax.all_to_all(to_far, FAR, 0, 0)
-    pieces = [own] + [shifted(own, "x", -step) for step in range(1, 4)]
-    for step in range(4):
-        pairs = [(2 * k + b, 2 * ((k - step) % 4) + 1 - b) for k in range(4) for b in range(2)]
-        pieces.append(lax.ppermute(own, NORTH, pairs))
+    own = pl.pallas_call(
+        copy_kernel,
+        out_shape=jax.ShapeDtypeStruct(own.shape, own.dtype),
+        in_specs=[VMEM],
+        out_specs=VMEM,
+        compiler_params=params(),
+        cost_estimate=pl.CostEstimate(flops=10_000_000_000, bytes_accessed=4 * piece * depth, transcendentals=0),
+        name="own",
+    )(own)
+    near = jnp.concatenate([own] + [shifted(own, "x", -step) for step in range(1, 4)])
+    across = shifted(near, "y_lo", 1)
     left = pl.pallas_call(
         arrange_kernel,
         out_shape=jax.ShapeDtypeStruct((north, piece, depth), jnp.bfloat16),
-        in_specs=[VMEM] * 8,
+        in_specs=[VMEM] * 2,
         out_specs=VMEM,
         compiler_params=params(),
         cost_estimate=pl.CostEstimate(flops=5_000_000_000, bytes_accessed=4 * piece * depth * north, transcendentals=0),
         name="arrange",
-    )(*pieces)
+    )(near, across)
     other = shifted(right, "core", 1)
     scale = 1.0 / depth
     block = pl.pallas_call(

time: 65.1 us -> 63.4 us (0.974)
  waiting for transfers between devices: 5.87 us -> 12.4 us
  starting transfers between devices: 26.9 us -> 20.7 us
  blocking collectives: 25.4 us -> 23.7 us
    ppermute x4 -> x0, starting transfers between devices: 6.45 us -> none  [body(): pieces.append(lax.ppermute(own, NORTH, pairs))]
    all_to_all x1, waiting for transfers between devices: 2.56 us -> 5.91 us  [body(): right = lax.all_to_all(to_far, FAR, 0, 0)]
    ppermute x4 -> x5, waiting for transfers between devices: 1.66 us -> 3.99 us  [shifted(): lax.ppermute(value, axes, [(k, (k + step) % count) for k in range(count)])]
    all_to_all x1, blocking collectives: 12.7 us -> 11 us  [body(): gathered = lax.all_to_all(partial.reshape(north, piece, depth), NORTH, 0, 0)]
    ppermute x4, starting transfers between devices: 4.53 us -> 5.89 us  [exchanged(): return lax.ppermute(value, axes, list(enumerate(flip)))]
    all_to_all x1, starting transfers between devices: 11.2 us -> 10 us  [body(): right = lax.all_to_all(to_far, FAR, 0, 0)]
    ppermute x4, waiting for transfers between devices: 1.65 us -> 2.47 us  [exchanged(): return lax.ppermute(value, axes, list(enumerate(flip)))]
    ppermute x4 -> x5, starting transfers between devices: 4.7 us -> 4.74 us  [shifted(): lax.ppermute(value, axes, [(k, (k + step) % count) for k in range(count)])]
  transfers between devices with their start and end apart: 13 -> 10, of which waited for: 3 -> 7; matrix products, arithmetic and copies ran while one was open for 0% -> 0% of each run, Pallas kernels for 2% -> 2%
where the time goes in v3:
time: 63.4 us; the launch traced here: 63.2 us
  blocking collectives  23.7 us (37%)
  starting transfers between devices  20.7 us (33%)
  waiting for transfers between devices  12.4 us (20%)
  Pallas kernels  4.78 us (8%)
  local copies, waits for them, and re-layouts  1.55 us (2%)
    all_to_all x1, blocking collectives, body(): blocks = lax.all_to_all(block, NORTH, 0, 0)  12.7 us
    all_to_all x1, blocking collectives, body(): gathered = lax.all_to_all(partial.reshape(north, piece, depth), NORTH, 0, 0)  11 us
    all_to_all x1, starting transfers between devices, body(): right = lax.all_to_all(to_far, FAR, 0, 0)  10 us
    all_to_all x1, waiting for transfers between devices, body(): right = lax.all_to_all(to_far, FAR, 0, 0)  5.91 us
    ppermute x4, starting transfers between devices, exchanged(): return lax.ppermute(value, axes, list(enumerate(flip)))  5.89 us
    ppermute x5, starting transfers between devices, shifted(): lax.ppermute(value, axes, [(k, (k + step) % count) for k in range(count)])  4.74 us
    ppermute x5, waiting for transfers between devices, shifted(): lax.ppermute(value, axes, [(k, (k + step) % count) for k in range(count)])  3.99 us
    ppermute x4, waiting for transfers between devices, exchanged(): return lax.ppermute(value, axes, list(enumerate(flip)))  2.47 us
  transfers between devices with their start and end apart: 10, of which 7 were waited for; matrix products, arithmetic and copies ran while one was open for 0% of the time, Pallas kernels for 2%

profile of v3, /device:TPU:32, one launch (start us, length us, event | category | flops | bytes accessed | tf_op | source)
XLA Modules:
  0.0 63.2 jit_solution(14700910212831061328)
XLA Ops:
  0.0 0.0 copy-start
  0.0 1.5 %copy-done = f32[3,10,64,256]{3,2,1,0:T(8,128)S(1)} copy-done((f32[3,10,64,256]{3,2,1,0:T(8,128)S(1)}, f32[3,10,64,256]{3,2,1,0:T(8,128)}, u32[]{:S(2)}) %copy-start) | copy-done | bytes 1966104
  1.5 0.0 copy-start.2
  1.5 0.4 faces.1
  1.9 0.1 collective-permute-start
  2.0 2.0 %collective-permute-start.3 = (f32[3,6,2,256]{3,2,1,0:T(2,128)S(1)}, f32[3,6,2,256]{3,2,1,0:T(2,128)S(1)}, u32[]{:S(2)}, u32[]{:S(2)}) collective-permute-start(f32[3,6,2,256]{3,2,1,0:T(2,128)S(1)} %get-tuple-element.28), channel_id=1, source_target_pairs={{0,8},{8,0},{16,24},{24,16},{32,40},{40,32},{48,56},{56,48},{64,72... | collective-permute-start | bytes 110600 | tf_op jit(solution)/shard_map/ppermute | solution.py:25
  4.0 3.8 %collective-permute-start.1 = (f32[80,128]{1,0:T(8,128)S(1)}, f32[80,128]{1,0:T(8,128)S(1)}, u32[]{:S(2)}, u32[]{:S(2)}) collective-permute-start(f32[80,128]{1,0:T(8,128)S(1)} %get-tuple-element.26), channel_id=1, source_target_pairs={{0,7},{1,2},{2,1},{3,4},{4,3},{5,6},{6,5},{7,0},{8,15},{9,10},{10,... | collective-permute-start | bytes 122888 | tf_op jit(solution)/shard_map/ppermute | solution.py:25
  7.8 0.0 copy-start.1
  7.8 0.0 collective-permute-start.2
  7.8 0.0 copy-done.2
  7.8 1.5 %inner.1 = (f32[6,64,256]{2,1,0:T(8,128)S(1)}, f32[6,64,256]{2,1,0:T(8,128)S(1)}, f32[6,64,256]{2,1,0:T(8,128)S(1)}, f32[6,64,256]{2,1,0:T(8,128)S(1)}, f32[6,64...) custom-call(f32[3,10,64,256]{3,2,1,0:T(8,128)S(1)} %copy-done, f32[10,64,256]{2,1,0:T(8,128)S(1)} %copy-done.2), custom_call_target="tpu_custom_call" | custom-call | flops 2500000000 | bytes 5000000 | tf_op jit(solution)/shard_map/inner/pallas_call | solution.py:229
  9.3 0.0 collective-permute-done.refs_8_
  9.3 0.0 collective-permute-done.3.refs_11_
  9.3 0.8 %collective-permute-done.1.refs_9_ = f32[80,128]{1,0:T(8,128)S(1)} collective-permute-done((f32[80,128]{1,0:T(8,128)S(1)}, f32[80,128]{1,0:T(8,128)S(1)}, u32[]{:S(2)}, u32[]{:S(2)}) %collective-permute-start.1) | collective-permute-done | bytes 40992 | tf_op jit(solution)/shard_map/ppermute | solution.py:25
  10.1 1.7 %collective-permute-done.2.refs_10_ = f32[80,128]{1,0:T(8,128)S(1)} collective-permute-done((f32[80,128]{1,0:T(8,128)S(1)}, f32[80,128]{1,0:T(8,128)S(1)}, u32[]{:S(2)}, u32[]{:S(2)}) %collective-permute-start.2) | collective-permute-done | bytes 40992 | tf_op jit(solution)/shard_map/ppermute | solution.py:25
  11.8 0.0 copy-done.1
  11.8 0.7 %field.1 = f32[64,1536]{1,0:T(8,128)S(1)} custom-call(f32[6,64,256]{2,1,0:T(8,128)S(1)} %get-tuple-element.18.refs_0_, f32[6,64,256]{2,1,0:T(8,128)S(1)} %get-tuple-element.19.refs_1_, f32[6,64,256]{2,1,0:T(8,128)S(1)} %get-tuple-element.20.refs_2_, f32[6,64,256]{2,1,0:T(8,128)S(1)} %get-tuple-element.21.refs_3_, ...), custom_call_target="tpu_custom_call" | custom-call | tf_op jit(solution)/shard_map/field/pallas_call | solution.py:239
  12.5 11.0 %all_to_all.15.parts = f32[8,8,1536]{2,1,0:T(8,128)S(1)} all-to-all(f32[8,8,1536]{2,1,0:T(8,128)S(1)} %bitcast.1), channel_id=1, replica_groups=mesh['y_hi'=2,'z'=8,'core'=2,'x'=4,'y_lo'=2] {'x','y_lo'}, dimensions={0} | all-to-all | bytes 786432 | tf_op jit(solution)/shard_map/all_to_all | solution.py:251
  23.5 0.8 %total.1 = (bf16[1,8,1536]{2,1,0:T(8,128)(2,1)S(1)}, bf16[16,8,1536]{2,1,0:T(8,128)(2,1)}) custom-call(f32[8,8,1536]{2,1,0:T(8,128)S(1)} %all_to_all.15.parts), custom_call_target="tpu_custom_call" | custom-call | tf_op jit(solution)/shard_map/total/pallas_call | solution.py:252
  24.3 10.0 %all-to-all-start.1 = ((bf16[16,8,1536]{2,1,0:T(8,128)(2,1)}), bf16[16,8,1536]{2,1,0:T(8,128)(2,1)S(1)}, u32[]{:S(2)}, u32[]{:S(2)}) async-start(bf16[16,8,1536]{2,1,0:T(8,128)(2,1)} %get-tuple-element.30), calls=%async_computation.1 | async-start | bytes 786432 | tf_op jit(solution)/shard_map/all_to_all | solution.py:263
  34.3 0.6 collective-permute-start.6
  34.9 2.1 %collective-permute-start.5 = (bf16[1,8,1536]{2,1,0:T(8,128)(2,1)S(1)}, bf16[1,8,1536]{2,1,0:T(8,128)(2,1)S(1)}, u32[]{:S(2)}, u32[]{:S(2)}) collective-permute-start(bf16[1,8,1536]{2,1,0:T(8,128)(2,1)S(1)} %own.1), channel_id=1, source_target_pairs={{0,4},{2,6},{4,0},{6,2},{1,5},{3,7},{5,1},{7,3},{8,12},{10,14},{12... | collective-permute-start | bytes 73736 | tf_op jit(solution)/shard_map/ppermute | solution.py:30
  36.9 1.5 %collective-permute-start.4 = (bf16[1,8,1536]{2,1,0:T(8,128)(2,1)S(1)}, bf16[1,8,1536]{2,1,0:T(8,128)(2,1)S(1)}, u32[]{:S(2)}, u32[]{:S(2)}) collective-permute-start(bf16[1,8,1536]{2,1,0:T(8,128)(2,1)S(1)} %own.1), channel_id=1, source_target_pairs={{0,6},{2,0},{4,2},{6,4},{1,7},{3,1},{5,3},{7,5},{8,14},{10,8},{12,... | collective-permute-start | bytes 73736 | tf_op jit(solution)/shard_map/ppermute | solution.py:30
  38.5 0.9 %collective-permute-done.6 = bf16[1,8,1536]{2,1,0:T(8,128)(2,1)S(1)} collective-permute-done((bf16[1,8,1536]{2,1,0:T(8,128)(2,1)S(1)}, bf16[1,8,1536]{2,1,0:T(8,128)(2,1)S(1)}, u32[]{:S(2)}, u32[]{:S(2)}) %collective-permute-start.6) | collective-permute-done | bytes 24608 | tf_op jit(solution)/shard_map/ppermute | solution.py:30
  39.4 0.8 %collective-permute-done.5 = bf16[1,8,1536]{2,1,0:T(8,128)(2,1)S(1)} collective-permute-done((bf16[1,8,1536]{2,1,0:T(8,128)(2,1)S(1)}, bf16[1,8,1536]{2,1,0:T(8,128)(2,1)S(1)}, u32[]{:S(2)}, u32[]{:S(2)}) %collective-permute-start.5) | collective-permute-done | bytes 24608 | tf_op jit(solution)/shard_map/ppermute | solution.py:30
  40.2 0.6 collective-permute-done.4
  40.8 0.6 collective-permute-start.7
  41.4 5.9 %all-to-all-done.1.refs_1_ = bf16[16,8,1536]{2,1,0:T(8,128)(2,1)S(1)} async-done(((bf16[16,8,1536]{2,1,0:T(8,128)(2,1)}), bf16[16,8,1536]{2,1,0:T(8,128)(2,1)S(1)}, u32[]{:S(2)}, u32[]{:S(2)}) %all-to-all-start.1) | async-done | bytes 393248 | tf_op jit(solution)/shard_map/all_to_all | solution.py:263
  47.3 0.0 collective-permute-start.8
  47.3 0.0 collective-permute-done.7.across
  47.3 1.7 %collective-permute-done.8.refs_2_ = bf16[16,8,1536]{2,1,0:T(8,128)(2,1)S(1)} collective-permute-done((bf16[16,8,1536]{2,1,0:T(8,128)(2,1)S(1)}, bf16[16,8,1536]{2,1,0:T(8,128)(2,1)S(1)}, u32[]{:S(2)}, u32[]{:S(2)}) %collective-permute-start.8) | collective-permute-done | bytes 393248 | tf_op jit(solution)/shard_map/ppermute | solution.py:30
  49.0 0.4 block.1
  49.4 12.7 %all_to_all.16.refs_0_ = f32[8,128,128]{2,1,0:T(8,128)S(1)} all-to-all(f32[8,128,128]{2,1,0:T(8,128)S(1)} %block.1), channel_id=1, replica_groups=mesh['y_hi'=2,'z'=8,'core'=2,'x'=4,'y_lo'=2] {'x','y_lo'}, dimensions={0} | all-to-all | bytes 1048576 | tf_op jit(solution)/shard_map/all_to_all | solution.py:295
  62.2 1.0 %place.1 = f32[64,2048]{1,0:T(8,128)} custom-call(f32[8,128,128]{2,1,0:T(8,128)S(1)} %all_to_all.16.refs_0_), custom_call_target="tpu_custom_call" | custom-call | tf_op jit(solution)/shard_map/place/pallas_call | solution.py:296
  (3 shorter events, 0.0 us)
Async XLA Ops:
  0.0 1.5 %copy-start = (f32[3,10,64,256]{3,2,1,0:T(8,128)S(1)}, f32[3,10,64,256]{3,2,1,0:T(8,128)}, u32[]{:S(2)}) copy-start(f32[3,10,64,256]{3,2,1,0:T(8,128)} %flow.3) | copy-start | bytes 5898244
  1.5 6.3 %copy-start.2 = (f32[10,64,256]{2,1,0:T(8,128)S(1)}, f32[10,64,256]{2,1,0:T(8,128)}, u32[]{:S(2)}) copy-start(f32[10,64,256]{2,1,0:T(8,128)} %thermal.1) | copy-start | bytes 1966084
  1.9 7.4 %collective-permute-start = (f32[3,6,2,256]{3,2,1,0:T(2,128)S(1)}, f32[3,6,2,256]{3,2,1,0:T(2,128)S(1)}, u32[]{:S(2)}, u32[]{:S(2)}) collective-permute-start(f32[3,6,2,256]{3,2,1,0:T(2,128)S(1)} %get-tuple-element.25), channel_id=1, source_target_pairs={{0,248},{8,16},{16,8},{24,32},{32,24},{40,48},{48,40},{56,64},{64,... | collective-permute-start | bytes 110600 | tf_op jit(solution)/shard_map/ppermute | solution.py:25
  2.0 7.3 %collective-permute-start.3 = (f32[3,6,2,256]{3,2,1,0:T(2,128)S(1)}, f32[3,6,2,256]{3,2,1,0:T(2,128)S(1)}, u32[]{:S(2)}, u32[]{:S(2)}) collective-permute-start(f32[3,6,2,256]{3,2,1,0:T(2,128)S(1)} %get-tuple-element.28), channel_id=1, source_target_pairs={{0,8},{8,0},{16,24},{24,16},{32,40},{40,32},{48,56},{56,48},{64,72... | collective-permute-start | bytes 110600 | tf_op jit(solution)/shard_map/ppermute | solution.py:25
  4.0 6.1 %collective-permute-start.1 = (f32[80,128]{1,0:T(8,128)S(1)}, f32[80,128]{1,0:T(8,128)S(1)}, u32[]{:S(2)}, u32[]{:S(2)}) collective-permute-start(f32[80,128]{1,0:T(8,128)S(1)} %get-tuple-element.26), channel_id=1, source_target_pairs={{0,7},{1,2},{2,1},{3,4},{4,3},{5,6},{6,5},{7,0},{8,15},{9,10},{10,... | collective-permute-start | bytes 122888 | tf_op jit(solution)/shard_map/ppermute | solution.py:25
  7.8 4.0 %copy-start.1 = (bf16[256,256]{1,0:T(8,128)(2,1)S(1)}, bf16[256,256]{1,0:T(8,128)(2,1)}, u32[]{:S(2)}) copy-start(bf16[256,256]{1,0:T(8,128)(2,1)} %refs_7_.1) | copy-start | bytes 393220
  7.8 4.0 %collective-permute-start.2 = (f32[80,128]{1,0:T(8,128)S(1)}, f32[80,128]{1,0:T(8,128)S(1)}, u32[]{:S(2)}, u32[]{:S(2)}) collective-permute-start(f32[80,128]{1,0:T(8,128)S(1)} %get-tuple-element.27), channel_id=1, source_target_pairs={{0,1},{1,0},{2,3},{3,2},{4,5},{5,4},{6,7},{7,6},{8,9},{9,8},{10,11... | collective-permute-start | bytes 122888 | tf_op jit(solution)/shard_map/ppermute | solution.py:25
  24.3 23.0 %all-to-all-start.1 = ((bf16[16,8,1536]{2,1,0:T(8,128)(2,1)}), bf16[16,8,1536]{2,1,0:T(8,128)(2,1)S(1)}, u32[]{:S(2)}, u32[]{:S(2)}) async-start(bf16[16,8,1536]{2,1,0:T(8,128)(2,1)} %get-tuple-element.30), calls=%async_computation.1 | async-start | bytes 786432 | tf_op jit(solution)/shard_map/all_to_all | solution.py:263
  34.3 5.1 %collective-permute-start.6 = (bf16[1,8,1536]{2,1,0:T(8,128)(2,1)S(1)}, bf16[1,8,1536]{2,1,0:T(8,128)(2,1)S(1)}, u32[]{:S(2)}, u32[]{:S(2)}) collective-permute-start(bf16[1,8,1536]{2,1,0:T(8,128)(2,1)S(1)} %own.1), channel_id=1, source_target_pairs={{0,2},{2,4},{4,6},{6,0},{1,3},{3,5},{5,7},{7,1},{8,10},{10,12},{12... | collective-permute-start | bytes 73736 | tf_op jit(solution)/shard_map/ppermute | solution.py:30
  34.9 5.3 %collective-permute-start.5 = (bf16[1,8,1536]{2,1,0:T(8,128)(2,1)S(1)}, bf16[1,8,1536]{2,1,0:T(8,128)(2,1)S(1)}, u32[]{:S(2)}, u32[]{:S(2)}) collective-permute-start(bf16[1,8,1536]{2,1,0:T(8,128)(2,1)S(1)} %own.1), channel_id=1, source_target_pairs={{0,4},{2,6},{4,0},{6,2},{1,5},{3,7},{5,1},{7,3},{8,12},{10,14},{12... | collective-permute-start | bytes 73736 | tf_op jit(solution)/shard_map/ppermute | solution.py:30
  36.9 3.8 %collective-permute-start.4 = (bf16[1,8,1536]{2,1,0:T(8,128)(2,1)S(1)}, bf16[1,8,1536]{2,1,0:T(8,128)(2,1)S(1)}, u32[]{:S(2)}, u32[]{:S(2)}) collective-permute-start(bf16[1,8,1536]{2,1,0:T(8,128)(2,1)S(1)} %own.1), channel_id=1, source_target_pairs={{0,6},{2,0},{4,2},{6,4},{1,7},{3,1},{5,3},{7,5},{8,14},{10,8},{12,... | collective-permute-start | bytes 73736 | tf_op jit(solution)/shard_map/ppermute | solution.py:30
  40.8 6.5 %collective-permute-start.7 = (bf16[4,8,1536]{2,1,0:T(8,128)(2,1)S(1)}, bf16[4,8,1536]{2,1,0:T(8,128)(2,1)S(1)}, u32[]{:S(2)}, u32[]{:S(2)}) collective-permute-start(bf16[4,8,1536]{2,1,0:T(8,128)(2,1)S(1)} %pad_maximum_fusion.near), channel_id=1, source_target_pairs={{0,1},{1,0},{2,3},{3,2},{4,5},{5,4},{6,7},{7,6},{8,9},{9,8},{10,11... | collective-permute-start | bytes 294920 | tf_op jit(solution)/shard_map/ppermute | solution.py:30
  47.3 1.7 %collective-permute-start.8 = (bf16[16,8,1536]{2,1,0:T(8,128)(2,1)S(1)}, bf16[16,8,1536]{2,1,0:T(8,128)(2,1)S(1)}, u32[]{:S(2)}, u32[]{:S(2)}) collective-permute-start(bf16[16,8,1536]{2,1,0:T(8,128)(2,1)S(1)} %all-to-all-done.1.refs_1_), channel_id=1, source_target_pairs={{0,8},{8,0},{1,9},{9,1},{2,10},{10,2},{3,11},{11,3},{4,12},{12,4},... | collective-permute-start | bytes 1179656 | tf_op jit(solution)/shard_map/ppermute | solution.py:30

commit v4 on v3

--- a/solution.py
+++ b/solution.py
@@ -30,20 +30,33 @@
     return lax.ppermute(value, axes, [(k, (k + step) % count) for k in range(count)])
 
 
-def faces_kernel(flow, x_inner, x_outer, y_inner, y_outer):
-    planes = x_inner.shape[1]
-    x_even, y_even = lax.axis_index("core") == 0, lax.axis_index("y_lo") == 0
-    width = flow.shape[3]
-    rows = flow.shape[2]
+def x_faces_kernel(flow, x_inner, x_outer, top, bottom, sems):
+    planes, rows = x_inner.shape[1], flow.shape[2]
+    middle = slice(2, planes + 2)
+    copies = [
+        pltpu.make_async_copy(flow.at[:, middle, 0:8], top, sems.at[0]),
+        pltpu.make_async_copy(flow.at[:, middle, rows - 8 : rows], bottom, sems.at[1]),
+    ]
+    for copy in copies:
+        copy.start()
+    for copy in copies:
+        copy.wait()
+    x_even = lax.axis_index("core") == 0
+    for comp in range(3):
+        for plane in range(planes):
+            first, last = top[comp, plane, 0:2], bottom[comp, plane, 6:8]
+            x_inner[comp, plane] = jnp.where(x_even, last, first)
+            x_outer[comp, plane] = jnp.where(x_even, first, last)
+
+
+def y_faces_kernel(flow, y_inner, y_outer):
+    planes, rows, width = flow.shape[1] - 4, flow.shape[2], flow.shape[3]
+    y_even = lax.axis_index("y_lo") == 0
     lane = lax.broadcasted_iota(jnp.int32, (rows, 128), 1)
     first = jnp.zeros((rows, 128), jnp.float32)
     last = jnp.zeros((rows, 128), jnp.float32)
     for comp in range(3):
         for plane in range(planes):
-            top = flow[comp, plane + 2, 0:2, :]
-            bottom = flow[comp, plane + 2, rows - 2 : rows, :]
-            x_inner[comp, plane] = jnp.where(x_even, bottom, top)
-            x_outer[comp, plane] = jnp.where(x_even, top, bottom)
             at = 2 * (comp * planes + plane)
             here = (lane == at) | (lane == at + 1)
             low = flow[comp, plane + 2, :, 0:128]
@@ -214,13 +227,27 @@
     f32 = jnp.float32
     x_face = jax.ShapeDtypeStruct((3, planes, 2, width), f32)
     y_face = jax.ShapeDtypeStruct((rows + 16, 128), f32)
-    x_inner, x_outer, y_inner, y_outer = pl.pallas_call(
-        faces_kernel,
-        out_shape=(x_face, x_face, y_face, y_face),
+    x_inner, x_outer = pl.pallas_call(
+        x_faces_kernel,
+        out_shape=(x_face, x_face),
+        in_specs=[pl.BlockSpec(memory_space=pltpu.HBM)],
+        out_specs=(VMEM, VMEM),
+        scratch_shapes=[
+            pltpu.VMEM((3, planes, 8, width), f32),
+            pltpu.VMEM((3, planes, 8, width), f32),
+            pltpu.SemaphoreType.DMA((2,)),
+        ],
+        compiler_params=params(),
+        name="x_faces",
+    )(flow)
+    y_inner, y_outer = pl.pallas_call(
+        y_faces_kernel,
+        out_shape=(y_face, y_face),
         in_specs=[VMEM],
-        out_specs=(VMEM,) * 4,
-        compiler_params=params(),
-        name="faces",
+        out_specs=(VMEM, VMEM),
+        compiler_params=params(),
+        cost_estimate=pl.CostEstimate(flops=500_000_000, bytes_accessed=1_000_000, transcendentals=0),
+        name="y_faces",
     )(flow)
     x_outer = exchanged(x_outer, EAST, True)
     y_outer = exchanged(y_outer, NORTH, True)

time: 63.4 us -> 62.6 us (0.987)
  waiting for transfers between devices: 12.4 us -> 11.1 us
    all_to_all x1, waiting for transfers between devices: 5.91 us -> 4.68 us  [body(): right = lax.all_to_all(to_far, FAR, 0, 0)]
  transfers between devices with their start and end apart: 10 -> 10, of which waited for: 7 -> 7; matrix products, arithmetic and copies ran while one was open for 0% -> 0% of each run, Pallas kernels for 2% -> 3%
where the time goes in v4:
time: 62.6 us; the launch traced here: 62.2 us
  blocking collectives  23.8 us (38%)
  starting transfers between devices  20.7 us (33%)
  waiting for transfers between devices  11.1 us (18%)
  Pallas kernels  4.88 us (8%)
  local copies, waits for them, and re-layouts  1.55 us (2%)
    all_to_all x1, blocking collectives, body(): blocks = lax.all_to_all(block, NORTH, 0, 0)  12.8 us
    all_to_all x1, blocking collectives, body(): gathered = lax.all_to_all(partial.reshape(north, piece, depth), NORTH, 0, 0)  11 us
    all_to_all x1, starting transfers between devices, body(): right = lax.all_to_all(to_far, FAR, 0, 0)  10 us
    ppermute x4, starting transfers between devices, exchanged(): return lax.ppermute(value, axes, list(enumerate(flip)))  5.97 us
    ppermute x5, starting transfers between devices, shifted(): lax.ppermute(value, axes, [(k, (k + step) % count) for k in range(count)])  4.74 us
    all_to_all x1, waiting for transfers between devices, body(): right = lax.all_to_all(to_far, FAR, 0, 0)  4.68 us
    ppermute x5, waiting for transfers between devices, shifted(): lax.ppermute(value, axes, [(k, (k + step) % count) for k in range(count)])  3.99 us
    ppermute x4, waiting for transfers between devices, exchanged(): return lax.ppermute(value, axes, list(enumerate(flip)))  2.47 us
  transfers between devices with their start and end apart: 10, of which 7 were waited for; matrix products, arithmetic and copies ran while one was open for 0% of the time, Pallas kernels for 3%

profile of v4, /device:TPU:32, one launch (start us, length us, event | category | flops | bytes accessed | tf_op | source)
XLA Modules:
  0.0 62.2 jit_solution(5480771858524458275)
XLA Ops:
  0.0 0.0 copy-start
  0.0 1.5 %copy-done = f32[3,10,64,256]{3,2,1,0:T(8,128)S(1)} copy-done((f32[3,10,64,256]{3,2,1,0:T(8,128)S(1)}, f32[3,10,64,256]{3,2,1,0:T(8,128)}, u32[]{:S(2)}) %copy-start) | copy-done | bytes 1966104
  1.5 0.0 copy-start.2
  1.5 0.1 x_faces.1
  1.7 0.1 collective-permute-start
  1.8 2.0 %collective-permute-start.3 = (f32[3,6,2,256]{3,2,1,0:T(2,128)S(1)}, f32[3,6,2,256]{3,2,1,0:T(2,128)S(1)}, u32[]{:S(2)}, u32[]{:S(2)}) collective-permute-start(f32[3,6,2,256]{3,2,1,0:T(2,128)S(1)} %get-tuple-element.28), channel_id=1, source_target_pairs={{0,8},{8,0},{16,24},{24,16},{32,40},{40,32},{48,56},{56,48},{64,72... | collective-permute-start | bytes 110600 | tf_op jit(solution)/shard_map/ppermute | solution.py:25
  3.8 0.4 y_faces.1
  4.1 3.9 %collective-permute-start.1 = (f32[80,128]{1,0:T(8,128)S(1)}, f32[80,128]{1,0:T(8,128)S(1)}, u32[]{:S(2)}, u32[]{:S(2)}) collective-permute-start(f32[80,128]{1,0:T(8,128)S(1)} %get-tuple-element.26), channel_id=1, source_target_pairs={{0,7},{1,2},{2,1},{3,4},{4,3},{5,6},{6,5},{7,0},{8,15},{9,10},{10,... | collective-permute-start | bytes 122888 | tf_op jit(solution)/shard_map/ppermute | solution.py:25
  8.0 0.0 copy-start.1
  8.0 0.0 collective-permute-start.2
  8.0 0.0 copy-done.2
  8.0 1.5 %inner.1 = (f32[6,64,256]{2,1,0:T(8,128)S(1)}, f32[6,64,256]{2,1,0:T(8,128)S(1)}, f32[6,64,256]{2,1,0:T(8,128)S(1)}, f32[6,64,256]{2,1,0:T(8,128)S(1)}, f32[6,64...) custom-call(f32[3,10,64,256]{3,2,1,0:T(8,128)S(1)} %copy-done, f32[10,64,256]{2,1,0:T(8,128)S(1)} %copy-done.2), custom_call_target="tpu_custom_call" | custom-call | flops 2500000000 | bytes 5000000 | tf_op jit(solution)/shard_map/inner/pallas_call | solution.py:256
  9.5 0.0 collective-permute-done.refs_8_
  9.5 0.0 collective-permute-done.3.refs_11_
  9.5 0.8 %collective-permute-done.1.refs_9_ = f32[80,128]{1,0:T(8,128)S(1)} collective-permute-done((f32[80,128]{1,0:T(8,128)S(1)}, f32[80,128]{1,0:T(8,128)S(1)}, u32[]{:S(2)}, u32[]{:S(2)}) %collective-permute-start.1) | collective-permute-done | bytes 40992 | tf_op jit(solution)/shard_map/ppermute | solution.py:25
  10.3 1.7 %collective-permute-done.2.refs_10_ = f32[80,128]{1,0:T(8,128)S(1)} collective-permute-done((f32[80,128]{1,0:T(8,128)S(1)}, f32[80,128]{1,0:T(8,128)S(1)}, u32[]{:S(2)}, u32[]{:S(2)}) %collective-permute-start.2) | collective-permute-done | bytes 40992 | tf_op jit(solution)/shard_map/ppermute | solution.py:25
  12.0 0.0 copy-done.1
  12.0 0.7 %field.1 = f32[64,1536]{1,0:T(8,128)S(1)} custom-call(f32[6,64,256]{2,1,0:T(8,128)S(1)} %get-tuple-element.18.refs_0_, f32[6,64,256]{2,1,0:T(8,128)S(1)} %get-tuple-element.19.refs_1_, f32[6,64,256]{2,1,0:T(8,128)S(1)} %get-tuple-element.20.refs_2_, f32[6,64,256]{2,1,0:T(8,128)S(1)} %get-tuple-element.21.refs_3_, ...), custom_call_target="tpu_custom_call" | custom-call | tf_op jit(solution)/shard_map/field/pallas_call | solution.py:266
  12.7 11.0 %all_to_all.15.parts = f32[8,8,1536]{2,1,0:T(8,128)S(1)} all-to-all(f32[8,8,1536]{2,1,0:T(8,128)S(1)} %bitcast.1), channel_id=1, replica_groups=mesh['y_hi'=2,'z'=8,'core'=2,'x'=4,'y_lo'=2] {'x','y_lo'}, dimensions={0} | all-to-all | bytes 786432 | tf_op jit(solution)/shard_map/all_to_all | solution.py:278
  23.7 0.8 %total.1 = (bf16[1,8,1536]{2,1,0:T(8,128)(2,1)S(1)}, bf16[16,8,1536]{2,1,0:T(8,128)(2,1)}) custom-call(f32[8,8,1536]{2,1,0:T(8,128)S(1)} %all_to_all.15.parts), custom_call_target="tpu_custom_call" | custom-call | tf_op jit(solution)/shard_map/total/pallas_call | solution.py:279
  24.5 10.0 %all-to-all-start.1 = ((bf16[16,8,1536]{2,1,0:T(8,128)(2,1)}), bf16[16,8,1536]{2,1,0:T(8,128)(2,1)S(1)}, u32[]{:S(2)}, u32[]{:S(2)}) async-start(bf16[16,8,1536]{2,1,0:T(8,128)(2,1)} %get-tuple-element.30), calls=%async_computation.1 | async-start | bytes 786432 | tf_op jit(solution)/shard_map/all_to_all | solution.py:290
  34.5 0.6 collective-permute-start.6
  35.1 2.1 %collective-permute-start.5 = (bf16[1,8,1536]{2,1,0:T(8,128)(2,1)S(1)}, bf16[1,8,1536]{2,1,0:T(8,128)(2,1)S(1)}, u32[]{:S(2)}, u32[]{:S(2)}) collective-permute-start(bf16[1,8,1536]{2,1,0:T(8,128)(2,1)S(1)} %own.1), channel_id=1, source_target_pairs={{0,4},{2,6},{4,0},{6,2},{1,5},{3,7},{5,1},{7,3},{8,12},{10,14},{12... | collective-permute-start | bytes 73736 | tf_op jit(solution)/shard_map/ppermute | solution.py:30
  37.1 1.5 %collective-permute-start.4 = (bf16[1,8,1536]{2,1,0:T(8,128)(2,1)S(1)}, bf16[1,8,1536]{2,1,0:T(8,128)(2,1)S(1)}, u32[]{:S(2)}, u32[]{:S(2)}) collective-permute-start(bf16[1,8,1536]{2,1,0:T(8,128)(2,1)S(1)} %own.1), channel_id=1, source_target_pairs={{0,6},{2,0},{4,2},{6,4},{1,7},{3,1},{5,3},{7,5},{8,14},{10,8},{12,... | collective-permute-start | bytes 73736 | tf_op jit(solution)/shard_map/ppermute | solution.py:30
  38.7 0.9 %collective-permute-done.6 = bf16[1,8,1536]{2,1,0:T(8,128)(2,1)S(1)} collective-permute-done((bf16[1,8,1536]{2,1,0:T(8,128)(2,1)S(1)}, bf16[1,8,1536]{2,1,0:T(8,128)(2,1)S(1)}, u32[]{:S(2)}, u32[]{:S(2)}) %collective-permute-start.6) | collective-permute-done | bytes 24608 | tf_op jit(solution)/shard_map/ppermute | solution.py:30
  39.6 0.8 %collective-permute-done.5 = bf16[1,8,1536]{2,1,0:T(8,128)(2,1)S(1)} collective-permute-done((bf16[1,8,1536]{2,1,0:T(8,128)(2,1)S(1)}, bf16[1,8,1536]{2,1,0:T(8,128)(2,1)S(1)}, u32[]{:S(2)}, u32[]{:S(2)}) %collective-permute-start.5) | collective-permute-done | bytes 24608 | tf_op jit(solution)/shard_map/ppermute | solution.py:30
  40.4 0.6 collective-permute-done.4
  41.0 0.6 collective-permute-start.7
  41.6 4.7 %all-to-all-done.1.refs_1_ = bf16[16,8,1536]{2,1,0:T(8,128)(2,1)S(1)} async-done(((bf16[16,8,1536]{2,1,0:T(8,128)(2,1)}), bf16[16,8,1536]{2,1,0:T(8,128)(2,1)S(1)}, u32[]{:S(2)}, u32[]{:S(2)}) %all-to-all-start.1) | async-done | bytes 393248 | tf_op jit(solution)/shard_map/all_to_all | solution.py:290
  46.2 0.0 collective-permute-start.8
  46.2 0.0 collective-permute-done.7.across
  46.3 1.7 %collective-permute-done.8.refs_2_ = bf16[16,8,1536]{2,1,0:T(8,128)(2,1)S(1)} collective-permute-done((bf16[16,8,1536]{2,1,0:T(8,128)(2,1)S(1)}, bf16[16,8,1536]{2,1,0:T(8,128)(2,1)S(1)}, u32[]{:S(2)}, u32[]{:S(2)}) %collective-permute-start.8) | collective-permute-done | bytes 393248 | tf_op jit(solution)/shard_map/ppermute | solution.py:30
  48.0 0.4 block.1
  48.4 12.8 %all_to_all.16.refs_0_ = f32[8,128,128]{2,1,0:T(8,128)S(1)} all-to-all(f32[8,128,128]{2,1,0:T(8,128)S(1)} %block.1), channel_id=1, replica_groups=mesh['y_hi'=2,'z'=8,'core'=2,'x'=4,'y_lo'=2] {'x','y_lo'}, dimensions={0} | all-to-all | bytes 1048576 | tf_op jit(solution)/shard_map/all_to_all | solution.py:322
  61.2 1.0 %place.1 = f32[64,2048]{1,0:T(8,128)} custom-call(f32[8,128,128]{2,1,0:T(8,128)S(1)} %all_to_all.16.refs_0_), custom_call_target="tpu_custom_call" | custom-call | tf_op jit(solution)/shard_map/place/pallas_call | solution.py:323
  (3 shorter events, 0.0 us)
Async XLA Ops:
  0.0 1.5 %copy-start = (f32[3,10,64,256]{3,2,1,0:T(8,128)S(1)}, f32[3,10,64,256]{3,2,1,0:T(8,128)}, u32[]{:S(2)}) copy-start(f32[3,10,64,256]{3,2,1,0:T(8,128)} %flow.5) | copy-start | bytes 5898244
  1.5 6.5 %copy-start.2 = (f32[10,64,256]{2,1,0:T(8,128)S(1)}, f32[10,64,256]{2,1,0:T(8,128)}, u32[]{:S(2)}) copy-start(f32[10,64,256]{2,1,0:T(8,128)} %thermal.1) | copy-start | bytes 1966084
  1.7 7.9 %collective-permute-start = (f32[3,6,2,256]{3,2,1,0:T(2,128)S(1)}, f32[3,6,2,256]{3,2,1,0:T(2,128)S(1)}, u32[]{:S(2)}, u32[]{:S(2)}) collective-permute-start(f32[3,6,2,256]{3,2,1,0:T(2,128)S(1)} %get-tuple-element.25), channel_id=1, source_target_pairs={{0,248},{8,16},{16,8},{24,32},{32,24},{40,48},{48,40},{56,64},{64,... | collective-permute-start | bytes 110600 | tf_op jit(solution)/shard_map/ppermute | solution.py:25
  1.8 7.8 %collective-permute-start.3 = (f32[3,6,2,256]{3,2,1,0:T(2,128)S(1)}, f32[3,6,2,256]{3,2,1,0:T(2,128)S(1)}, u32[]{:S(2)}, u32[]{:S(2)}) collective-permute-start(f32[3,6,2,256]{3,2,1,0:T(2,128)S(1)} %get-tuple-element.28), channel_id=1, source_target_pairs={{0,8},{8,0},{16,24},{24,16},{32,40},{40,32},{48,56},{56,48},{64,72... | collective-permute-start | bytes 110600 | tf_op jit(solution)/shard_map/ppermute | solution.py:25
  4.1 6.2 %collective-permute-start.1 = (f32[80,128]{1,0:T(8,128)S(1)}, f32[80,128]{1,0:T(8,128)S(1)}, u32[]{:S(2)}, u32[]{:S(2)}) collective-permute-start(f32[80,128]{1,0:T(8,128)S(1)} %get-tuple-element.26), channel_id=1, source_target_pairs={{0,7},{1,2},{2,1},{3,4},{4,3},{5,6},{6,5},{7,0},{8,15},{9,10},{10,... | collective-permute-start | bytes 122888 | tf_op jit(solution)/shard_map/ppermute | solution.py:25
  8.0 4.0 %copy-start.1 = (bf16[256,256]{1,0:T(8,128)(2,1)S(1)}, bf16[256,256]{1,0:T(8,128)(2,1)}, u32[]{:S(2)}) copy-start(bf16[256,256]{1,0:T(8,128)(2,1)} %refs_7_.1) | copy-start | bytes 393220
  8.0 4.0 %collective-permute-start.2 = (f32[80,128]{1,0:T(8,128)S(1)}, f32[80,128]{1,0:T(8,128)S(1)}, u32[]{:S(2)}, u32[]{:S(2)}) collective-permute-start(f32[80,128]{1,0:T(8,128)S(1)} %get-tuple-element.27), channel_id=1, source_target_pairs={{0,1},{1,0},{2,3},{3,2},{4,5},{5,4},{6,7},{7,6},{8,9},{9,8},{10,11... | collective-permute-start | bytes 122888 | tf_op jit(solution)/shard_map/ppermute | solution.py:25
  24.5 21.8 %all-to-all-start.1 = ((bf16[16,8,1536]{2,1,0:T(8,128)(2,1)}), bf16[16,8,1536]{2,1,0:T(8,128)(2,1)S(1)}, u32[]{:S(2)}, u32[]{:S(2)}) async-start(bf16[16,8,1536]{2,1,0:T(8,128)(2,1)} %get-tuple-element.30), calls=%async_computation.1 | async-start | bytes 786432 | tf_op jit(solution)/shard_map/all_to_all | solution.py:290
  34.5 5.1 %collective-permute-start.6 = (bf16[1,8,1536]{2,1,0:T(8,128)(2,1)S(1)}, bf16[1,8,1536]{2,1,0:T(8,128)(2,1)S(1)}, u32[]{:S(2)}, u32[]{:S(2)}) collective-permute-start(bf16[1,8,1536]{2,1,0:T(8,128)(2,1)S(1)} %own.1), channel_id=1, source_target_pairs={{0,2},{2,4},{4,6},{6,0},{1,3},{3,5},{5,7},{7,1},{8,10},{10,12},{12... | collective-permute-start | bytes 73736 | tf_op jit(solution)/shard_map/ppermute | solution.py:30
  35.1 5.3 %collective-permute-start.5 = (bf16[1,8,1536]{2,1,0:T(8,128)(2,1)S(1)}, bf16[1,8,1536]{2,1,0:T(8,128)(2,1)S(1)}, u32[]{:S(2)}, u32[]{:S(2)}) collective-permute-start(bf16[1,8,1536]{2,1,0:T(8,128)(2,1)S(1)} %own.1), channel_id=1, source_target_pairs={{0,4},{2,6},{4,0},{6,2},{1,5},{3,7},{5,1},{7,3},{8,12},{10,14},{12... | collective-permute-start | bytes 73736 | tf_op jit(solution)/shard_map/ppermute | solution.py:30
  37.1 3.8 %collective-permute-start.4 = (bf16[1,8,1536]{2,1,0:T(8,128)(2,1)S(1)}, bf16[1,8,1536]{2,1,0:T(8,128)(2,1)S(1)}, u32[]{:S(2)}, u32[]{:S(2)}) collective-permute-start(bf16[1,8,1536]{2,1,0:T(8,128)(2,1)S(1)} %own.1), channel_id=1, source_target_pairs={{0,6},{2,0},{4,2},{6,4},{1,7},{3,1},{5,3},{7,5},{8,14},{10,8},{12,... | collective-permute-start | bytes 73736 | tf_op jit(solution)/shard_map/ppermute | solution.py:30
  41.0 5.3 %collective-permute-start.7 = (bf16[4,8,1536]{2,1,0:T(8,128)(2,1)S(1)}, bf16[4,8,1536]{2,1,0:T(8,128)(2,1)S(1)}, u32[]{:S(2)}, u32[]{:S(2)}) collective-permute-start(bf16[4,8,1536]{2,1,0:T(8,128)(2,1)S(1)} %pad_maximum_fusion.near), channel_id=1, source_target_pairs={{0,1},{1,0},{2,3},{3,2},{4,5},{5,4},{6,7},{7,6},{8,9},{9,8},{10,11... | collective-permute-start | bytes 294920 | tf_op jit(solution)/shard_map/ppermute | solution.py:30
  46.2 1.7 %collective-permute-start.8 = (bf16[16,8,1536]{2,1,0:T(8,128)(2,1)S(1)}, bf16[16,8,1536]{2,1,0:T(8,128)(2,1)S(1)}, u32[]{:S(2)}, u32[]{:S(2)}) collective-permute-start(bf16[16,8,1536]{2,1,0:T(8,128)(2,1)S(1)} %all-to-all-done.1.refs_1_), channel_id=1, source_target_pairs={{0,8},{8,0},{1,9},{9,1},{2,10},{10,2},{3,11},{11,3},{4,12},{12,4},... | collective-permute-start | bytes 1179656 | tf_op jit(solution)/shard_map/ppermute | solution.py:30

commit v5 on v4

--- a/solution.py
+++ b/solution.py
@@ -239,7 +239,7 @@
         ],
         compiler_params=params(),
         name="x_faces",
-    )(flow)
+    )(pltpu.with_memory_space_constraint(flow, pltpu.HBM))
     y_inner, y_outer = pl.pallas_call(
         y_faces_kernel,
         out_shape=(y_face, y_face),

time: 62.6 us -> 62.1 us (level)
  local copies, waits for them, and re-layouts: 1.55 us -> 0.01 us
  Pallas kernels: 4.88 us -> 5.96 us
    unnamed x6, local copies, waits for them, and re-layouts: 1.55 us -> 0.01 us
    pallas_call x1, Pallas kernels: 0.1 us -> 1.19 us  [body(): pl.pallas_call(x_faces_kernel, out_shape=(x_face, x_face), in_specs=[pl.B...]
where the time goes in v5:
time: 62.1 us; the launch traced here: 61.7 us
  blocking collectives  23.8 us (38%)
  starting transfers between devices  20.7 us (33%)
  waiting for transfers between devices  11.1 us (18%)
  Pallas kernels  5.96 us (10%)
    all_to_all x1, blocking collectives, body(): blocks = lax.all_to_all(block, NORTH, 0, 0)  12.8 us
    all_to_all x1, blocking collectives, body(): gathered = lax.all_to_all(partial.reshape(north, piece, depth), NORTH, 0, 0)  11 us
    all_to_all x1, starting transfers between devices, body(): right = lax.all_to_all(to_far, FAR, 0, 0)  10 us
    ppermute x4, starting transfers between devices, exchanged(): return lax.ppermute(value, axes, list(enumerate(flip)))  5.97 us
    ppermute x5, starting transfers between devices, shifted(): lax.ppermute(value, axes, [(k, (k + step) % count) for k in range(count)])  4.74 us
    all_to_all x1, waiting for transfers between devices, body(): right = lax.all_to_all(to_far, FAR, 0, 0)  4.68 us
    ppermute x5, waiting for transfers between devices, shifted(): lax.ppermute(value, axes, [(k, (k + step) % count) for k in range(count)])  3.99 us
    ppermute x4, waiting for transfers between devices, exchanged(): return lax.ppermute(value, axes, list(enumerate(flip)))  2.47 us
  transfers between devices with their start and end apart: 10, of which 7 were waited for; matrix products, arithmetic and copies ran while one was open for 0% of the time, Pallas kernels for 3%

profile of v5, /device:TPU:32, one launch (start us, length us, event | category | flops | bytes accessed | tf_op | source)
XLA Modules:
  0.0 61.7 jit_solution(16186816937945079482)
XLA Ops:
  0.0 0.0 copy-start
  0.0 0.0 copy-start.2
  0.0 1.2 %x_faces.1 = (f32[3,6,2,256]{3,2,1,0:T(2,128)S(1)}, f32[3,6,2,256]{3,2,1,0:T(2,128)S(1)}) custom-call(f32[3,10,64,256]{3,2,1,0:T(8,128)} %flow.5), custom_call_target="tpu_custom_call" | custom-call | tf_op jit(solution)/shard_map/x_faces/pallas_call | solution.py:230
  1.2 0.1 collective-permute-start
  1.3 2.0 %collective-permute-start.3 = (f32[3,6,2,256]{3,2,1,0:T(2,128)S(1)}, f32[3,6,2,256]{3,2,1,0:T(2,128)S(1)}, u32[]{:S(2)}, u32[]{:S(2)}) collective-permute-start(f32[3,6,2,256]{3,2,1,0:T(2,128)S(1)} %get-tuple-element.28), channel_id=1, source_target_pairs={{0,8},{8,0},{16,24},{24,16},{32,40},{40,32},{48,56},{56,48},{64,72... | collective-permute-start | bytes 110600 | tf_op jit(solution)/shard_map/ppermute | solution.py:25
  3.3 0.0 copy-done
  3.3 0.4 y_faces.1
  3.7 3.9 %collective-permute-start.1 = (f32[80,128]{1,0:T(8,128)S(1)}, f32[80,128]{1,0:T(8,128)S(1)}, u32[]{:S(2)}, u32[]{:S(2)}) collective-permute-start(f32[80,128]{1,0:T(8,128)S(1)} %get-tuple-element.26), channel_id=1, source_target_pairs={{0,7},{1,2},{2,1},{3,4},{4,3},{5,6},{6,5},{7,0},{8,15},{9,10},{10,... | collective-permute-start | bytes 122888 | tf_op jit(solution)/shard_map/ppermute | solution.py:25
  7.6 0.0 copy-start.1
  7.6 0.0 collective-permute-start.2
  7.6 0.0 copy-done.2
  7.6 1.5 %inner.1 = (f32[6,64,256]{2,1,0:T(8,128)S(1)}, f32[6,64,256]{2,1,0:T(8,128)S(1)}, f32[6,64,256]{2,1,0:T(8,128)S(1)}, f32[6,64,256]{2,1,0:T(8,128)S(1)}, f32[6,64...) custom-call(f32[3,10,64,256]{3,2,1,0:T(8,128)S(1)} %copy-done, f32[10,64,256]{2,1,0:T(8,128)S(1)} %copy-done.2), custom_call_target="tpu_custom_call" | custom-call | flops 2500000000 | bytes 5000000 | tf_op jit(solution)/shard_map/inner/pallas_call | solution.py:256
  9.1 0.0 collective-permute-done.refs_8_
  9.1 0.0 collective-permute-done.3.refs_11_
  9.1 0.8 %collective-permute-done.1.refs_9_ = f32[80,128]{1,0:T(8,128)S(1)} collective-permute-done((f32[80,128]{1,0:T(8,128)S(1)}, f32[80,128]{1,0:T(8,128)S(1)}, u32[]{:S(2)}, u32[]{:S(2)}) %collective-permute-start.1) | collective-permute-done | bytes 40992 | tf_op jit(solution)/shard_map/ppermute | solution.py:25
  9.9 1.7 %collective-permute-done.2.refs_10_ = f32[80,128]{1,0:T(8,128)S(1)} collective-permute-done((f32[80,128]{1,0:T(8,128)S(1)}, f32[80,128]{1,0:T(8,128)S(1)}, u32[]{:S(2)}, u32[]{:S(2)}) %collective-permute-start.2) | collective-permute-done | bytes 40992 | tf_op jit(solution)/shard_map/ppermute | solution.py:25
  11.6 0.0 copy-done.1
  11.6 0.7 %field.1 = f32[64,1536]{1,0:T(8,128)S(1)} custom-call(f32[6,64,256]{2,1,0:T(8,128)S(1)} %get-tuple-element.18.refs_0_, f32[6,64,256]{2,1,0:T(8,128)S(1)} %get-tuple-element.19.refs_1_, f32[6,64,256]{2,1,0:T(8,128)S(1)} %get-tuple-element.20.refs_2_, f32[6,64,256]{2,1,0:T(8,128)S(1)} %get-tuple-element.21.refs_3_, ...), custom_call_target="tpu_custom_call" | custom-call | tf_op jit(solution)/shard_map/field/pallas_call | solution.py:266
  12.2 11.0 %all_to_all.15.parts = f32[8,8,1536]{2,1,0:T(8,128)S(1)} all-to-all(f32[8,8,1536]{2,1,0:T(8,128)S(1)} %bitcast.1), channel_id=1, replica_groups=mesh['y_hi'=2,'z'=8,'core'=2,'x'=4,'y_lo'=2] {'x','y_lo'}, dimensions={0} | all-to-all | bytes 786432 | tf_op jit(solution)/shard_map/all_to_all | solution.py:278
  23.2 0.8 %total.1 = (bf16[1,8,1536]{2,1,0:T(8,128)(2,1)S(1)}, bf16[16,8,1536]{2,1,0:T(8,128)(2,1)}) custom-call(f32[8,8,1536]{2,1,0:T(8,128)S(1)} %all_to_all.15.parts), custom_call_target="tpu_custom_call" | custom-call | tf_op jit(solution)/shard_map/total/pallas_call | solution.py:279
  24.0 10.0 %all-to-all-start.1 = ((bf16[16,8,1536]{2,1,0:T(8,128)(2,1)}), bf16[16,8,1536]{2,1,0:T(8,128)(2,1)S(1)}, u32[]{:S(2)}, u32[]{:S(2)}) async-start(bf16[16,8,1536]{2,1,0:T(8,128)(2,1)} %get-tuple-element.30), calls=%async_computation.1 | async-start | bytes 786432 | tf_op jit(solution)/shard_map/all_to_all | solution.py:290
  34.0 0.6 collective-permute-start.6
  34.6 2.1 %collective-permute-start.5 = (bf16[1,8,1536]{2,1,0:T(8,128)(2,1)S(1)}, bf16[1,8,1536]{2,1,0:T(8,128)(2,1)S(1)}, u32[]{:S(2)}, u32[]{:S(2)}) collective-permute-start(bf16[1,8,1536]{2,1,0:T(8,128)(2,1)S(1)} %own.1), channel_id=1, source_target_pairs={{0,4},{2,6},{4,0},{6,2},{1,5},{3,7},{5,1},{7,3},{8,12},{10,14},{12... | collective-permute-start | bytes 73736 | tf_op jit(solution)/shard_map/ppermute | solution.py:30
  36.7 1.5 %collective-permute-start.4 = (bf16[1,8,1536]{2,1,0:T(8,128)(2,1)S(1)}, bf16[1,8,1536]{2,1,0:T(8,128)(2,1)S(1)}, u32[]{:S(2)}, u32[]{:S(2)}) collective-permute-start(bf16[1,8,1536]{2,1,0:T(8,128)(2,1)S(1)} %own.1), channel_id=1, source_target_pairs={{0,6},{2,0},{4,2},{6,4},{1,7},{3,1},{5,3},{7,5},{8,14},{10,8},{12,... | collective-permute-start | bytes 73736 | tf_op jit(solution)/shard_map/ppermute | solution.py:30
  38.2 0.9 %collective-permute-done.6 = bf16[1,8,1536]{2,1,0:T(8,128)(2,1)S(1)} collective-permute-done((bf16[1,8,1536]{2,1,0:T(8,128)(2,1)S(1)}, bf16[1,8,1536]{2,1,0:T(8,128)(2,1)S(1)}, u32[]{:S(2)}, u32[]{:S(2)}) %collective-permute-start.6) | collective-permute-done | bytes 24608 | tf_op jit(solution)/shard_map/ppermute | solution.py:30
  39.1 0.8 %collective-permute-done.5 = bf16[1,8,1536]{2,1,0:T(8,128)(2,1)S(1)} collective-permute-done((bf16[1,8,1536]{2,1,0:T(8,128)(2,1)S(1)}, bf16[1,8,1536]{2,1,0:T(8,128)(2,1)S(1)}, u32[]{:S(2)}, u32[]{:S(2)}) %collective-permute-start.5) | collective-permute-done | bytes 24608 | tf_op jit(solution)/shard_map/ppermute | solution.py:30
  39.9 0.6 collective-permute-done.4
  40.5 0.6 collective-permute-start.7
  41.1 4.7 %all-to-all-done.1.refs_1_ = bf16[16,8,1536]{2,1,0:T(8,128)(2,1)S(1)} async-done(((bf16[16,8,1536]{2,1,0:T(8,128)(2,1)}), bf16[16,8,1536]{2,1,0:T(8,128)(2,1)S(1)}, u32[]{:S(2)}, u32[]{:S(2)}) %all-to-all-start.1) | async-done | bytes 393248 | tf_op jit(solution)/shard_map/all_to_all | solution.py:290
  45.8 0.0 collective-permute-start.8
  45.8 0.0 collective-permute-done.7.across
  45.8 1.7 %collective-permute-done.8.refs_2_ = bf16[16,8,1536]{2,1,0:T(8,128)(2,1)S(1)} collective-permute-done((bf16[16,8,1536]{2,1,0:T(8,128)(2,1)S(1)}, bf16[16,8,1536]{2,1,0:T(8,128)(2,1)S(1)}, u32[]{:S(2)}, u32[]{:S(2)}) %collective-permute-start.8) | collective-permute-done | bytes 393248 | tf_op jit(solution)/shard_map/ppermute | solution.py:30
  47.5 0.4 block.1
  47.9 12.8 %all_to_all.16.refs_0_ = f32[8,128,128]{2,1,0:T(8,128)S(1)} all-to-all(f32[8,128,128]{2,1,0:T(8,128)S(1)} %block.1), channel_id=1, replica_groups=mesh['y_hi'=2,'z'=8,'core'=2,'x'=4,'y_lo'=2] {'x','y_lo'}, dimensions={0} | all-to-all | bytes 1048576 | tf_op jit(solution)/shard_map/all_to_all | solution.py:322
  60.7 1.0 %place.1 = f32[64,2048]{1,0:T(8,128)} custom-call(f32[8,128,128]{2,1,0:T(8,128)S(1)} %all_to_all.16.refs_0_), custom_call_target="tpu_custom_call" | custom-call | tf_op jit(solution)/shard_map/place/pallas_call | solution.py:323
  (3 shorter events, 0.0 us)
Async XLA Ops:
  0.0 3.3 %copy-start = (f32[3,10,64,256]{3,2,1,0:T(8,128)S(1)}, f32[3,10,64,256]{3,2,1,0:T(8,128)}, u32[]{:S(2)}) copy-start(f32[3,10,64,256]{3,2,1,0:T(8,128)} %flow.5) | copy-start | bytes 5898244
  0.0 7.6 %copy-start.2 = (f32[10,64,256]{2,1,0:T(8,128)S(1)}, f32[10,64,256]{2,1,0:T(8,128)}, u32[]{:S(2)}) copy-start(f32[10,64,256]{2,1,0:T(8,128)} %thermal.1) | copy-start | bytes 1966084
  1.2 7.9 %collective-permute-start = (f32[3,6,2,256]{3,2,1,0:T(2,128)S(1)}, f32[3,6,2,256]{3,2,1,0:T(2,128)S(1)}, u32[]{:S(2)}, u32[]{:S(2)}) collective-permute-start(f32[3,6,2,256]{3,2,1,0:T(2,128)S(1)} %get-tuple-element.25), channel_id=1, source_target_pairs={{0,248},{8,16},{16,8},{24,32},{32,24},{40,48},{48,40},{56,64},{64,... | collective-permute-start | bytes 110600 | tf_op jit(solution)/shard_map/ppermute | solution.py:25
  1.3 7.8 %collective-permute-start.3 = (f32[3,6,2,256]{3,2,1,0:T(2,128)S(1)}, f32[3,6,2,256]{3,2,1,0:T(2,128)S(1)}, u32[]{:S(2)}, u32[]{:S(2)}) collective-permute-start(f32[3,6,2,256]{3,2,1,0:T(2,128)S(1)} %get-tuple-element.28), channel_id=1, source_target_pairs={{0,8},{8,0},{16,24},{24,16},{32,40},{40,32},{48,56},{56,48},{64,72... | collective-permute-start | bytes 110600 | tf_op jit(solution)/shard_map/ppermute | solution.py:25
  3.7 6.2 %collective-permute-start.1 = (f32[80,128]{1,0:T(8,128)S(1)}, f32[80,128]{1,0:T(8,128)S(1)}, u32[]{:S(2)}, u32[]{:S(2)}) collective-permute-start(f32[80,128]{1,0:T(8,128)S(1)} %get-tuple-element.26), channel_id=1, source_target_pairs={{0,7},{1,2},{2,1},{3,4},{4,3},{5,6},{6,5},{7,0},{8,15},{9,10},{10,... | collective-permute-start | bytes 122888 | tf_op jit(solution)/shard_map/ppermute | solution.py:25
  7.6 4.0 %copy-start.1 = (bf16[256,256]{1,0:T(8,128)(2,1)S(1)}, bf16[256,256]{1,0:T(8,128)(2,1)}, u32[]{:S(2)}) copy-start(bf16[256,256]{1,0:T(8,128)(2,1)} %refs_7_.1) | copy-start | bytes 393220
  7.6 4.0 %collective-permute-start.2 = (f32[80,128]{1,0:T(8,128)S(1)}, f32[80,128]{1,0:T(8,128)S(1)}, u32[]{:S(2)}, u32[]{:S(2)}) collective-permute-start(f32[80,128]{1,0:T(8,128)S(1)} %get-tuple-element.27), channel_id=1, source_target_pairs={{0,1},{1,0},{2,3},{3,2},{4,5},{5,4},{6,7},{7,6},{8,9},{9,8},{10,11... | collective-permute-start | bytes 122888 | tf_op jit(solution)/shard_map/ppermute | solution.py:25
  24.0 21.8 %all-to-all-start.1 = ((bf16[16,8,1536]{2,1,0:T(8,128)(2,1)}), bf16[16,8,1536]{2,1,0:T(8,128)(2,1)S(1)}, u32[]{:S(2)}, u32[]{:S(2)}) async-start(bf16[16,8,1536]{2,1,0:T(8,128)(2,1)} %get-tuple-element.30), calls=%async_computation.1 | async-start | bytes 786432 | tf_op jit(solution)/shard_map/all_to_all | solution.py:290
  34.0 5.1 %collective-permute-start.6 = (bf16[1,8,1536]{2,1,0:T(8,128)(2,1)S(1)}, bf16[1,8,1536]{2,1,0:T(8,128)(2,1)S(1)}, u32[]{:S(2)}, u32[]{:S(2)}) collective-permute-start(bf16[1,8,1536]{2,1,0:T(8,128)(2,1)S(1)} %own.1), channel_id=1, source_target_pairs={{0,2},{2,4},{4,6},{6,0},{1,3},{3,5},{5,7},{7,1},{8,10},{10,12},{12... | collective-permute-start | bytes 73736 | tf_op jit(solution)/shard_map/ppermute | solution.py:30
  34.6 5.3 %collective-permute-start.5 = (bf16[1,8,1536]{2,1,0:T(8,128)(2,1)S(1)}, bf16[1,8,1536]{2,1,0:T(8,128)(2,1)S(1)}, u32[]{:S(2)}, u32[]{:S(2)}) collective-permute-start(bf16[1,8,1536]{2,1,0:T(8,128)(2,1)S(1)} %own.1), channel_id=1, source_target_pairs={{0,4},{2,6},{4,0},{6,2},{1,5},{3,7},{5,1},{7,3},{8,12},{10,14},{12... | collective-permute-start | bytes 73736 | tf_op jit(solution)/shard_map/ppermute | solution.py:30
  36.7 3.8 %collective-permute-start.4 = (bf16[1,8,1536]{2,1,0:T(8,128)(2,1)S(1)}, bf16[1,8,1536]{2,1,0:T(8,128)(2,1)S(1)}, u32[]{:S(2)}, u32[]{:S(2)}) collective-permute-start(bf16[1,8,1536]{2,1,0:T(8,128)(2,1)S(1)} %own.1), channel_id=1, source_target_pairs={{0,6},{2,0},{4,2},{6,4},{1,7},{3,1},{5,3},{7,5},{8,14},{10,8},{12,... | collective-permute-start | bytes 73736 | tf_op jit(solution)/shard_map/ppermute | solution.py:30
  40.5 5.3 %collective-permute-start.7 = (bf16[4,8,1536]{2,1,0:T(8,128)(2,1)S(1)}, bf16[4,8,1536]{2,1,0:T(8,128)(2,1)S(1)}, u32[]{:S(2)}, u32[]{:S(2)}) collective-permute-start(bf16[4,8,1536]{2,1,0:T(8,128)(2,1)S(1)} %pad_maximum_fusion.near), channel_id=1, source_target_pairs={{0,1},{1,0},{2,3},{3,2},{4,5},{5,4},{6,7},{7,6},{8,9},{9,8},{10,11... | collective-permute-start | bytes 294920 | tf_op jit(solution)/shard_map/ppermute | solution.py:30
  45.8 1.7 %collective-permute-start.8 = (bf16[16,8,1536]{2,1,0:T(8,128)(2,1)S(1)}, bf16[16,8,1536]{2,1,0:T(8,128)(2,1)S(1)}, u32[]{:S(2)}, u32[]{:S(2)}) collective-permute-start(bf16[16,8,1536]{2,1,0:T(8,128)(2,1)S(1)} %all-to-all-done.1.refs_1_), channel_id=1, source_target_pairs={{0,8},{8,0},{1,9},{9,1},{2,10},{10,2},{3,11},{11,3},{4,12},{12,4},... | collective-permute-start | bytes 1179656 | tf_op jit(solution)/shard_map/ppermute | solution.py:30

commit v6 on v5

--- a/solution.py
+++ b/solution.py
@@ -10,6 +10,7 @@
 FAR = ("y_hi", "z")
 EAST = ("y_hi", "z", "core")
 NORTH = ("x", "y_lo")
+ORDER = (0, 3, 6, 1, 4, 7, 2, 5, 8, 11, 14, 9, 12, 15, 10, 13)
 LIMIT = 48 * 1024 * 1024
 
 
@@ -181,12 +182,13 @@
     target[...] = source[...]
 
 
-def arrange_kernel(near, across, left):
+def arrange_kernel(*refs):
+    pairs, left = refs[:4], refs[4]
     x, y_lo = lax.axis_index("x"), lax.axis_index("y_lo")
-    for step in range(4):
+    for step, pair in enumerate(pairs):
         at = 2 * lax.rem(x + step, 4)
-        left[at + y_lo] = near[step]
-        left[at + 1 - y_lo] = across[step]
+        left[at + y_lo] = pair[0]
+        left[at + 1 - y_lo] = pair[1]
 
 
 def block_kernel(scale, left, own, other, out, right):
@@ -194,8 +196,9 @@
     count, piece, depth = own.shape
     a = left[...].reshape(left.shape[0] * piece, depth)
     half = count // 2
-    right[core] = own[...]
-    right[1 - core] = other[...]
+    for slot, at in enumerate(ORDER):
+        right[core, at] = own[slot]
+        right[1 - core, at] = other[slot]
     sides = []
     for side in range(2):
         w = right[:, side * half : (side + 1) * half].reshape(count * piece, depth)
@@ -287,7 +290,8 @@
         compiler_params=params(),
         name="total",
     )(gathered)
-    right = lax.all_to_all(to_far, FAR, 0, 0)
+    right = lax.all_to_all(to_far, FAR, 0, 0, axis_index_groups=[list(ORDER)])
+    beside = shifted(own, "y_lo", 1)
     own = pl.pallas_call(
         copy_kernel,
         out_shape=jax.ShapeDtypeStruct(own.shape, own.dtype),
@@ -297,17 +301,17 @@
         cost_estimate=pl.CostEstimate(flops=10_000_000_000, bytes_accessed=4 * piece * depth, transcendentals=0),
         name="own",
     )(own)
-    near = jnp.concatenate([own] + [shifted(own, "x", -step) for step in range(1, 4)])
-    across = shifted(near, "y_lo", 1)
+    pair = jnp.concatenate([own, beside])
+    pairs = [pair] + [shifted(pair, "x", -step) for step in range(1, 4)]
     left = pl.pallas_call(
         arrange_kernel,
         out_shape=jax.ShapeDtypeStruct((north, piece, depth), jnp.bfloat16),
-        in_specs=[VMEM] * 2,
+        in_specs=[VMEM] * 4,
         out_specs=VMEM,
         compiler_params=params(),
         cost_estimate=pl.CostEstimate(flops=5_000_000_000, bytes_accessed=4 * piece * depth * north, transcendentals=0),
         name="arrange",
-    )(near, across)
+    )(*pairs)
     other = shifted(right, "core", 1)
     scale = 1.0 / depth
     block = pl.pallas_call(

time: 62.1 us -> 61.8 us (level)
    ppermute x5, waiting for transfers between devices: 3.99 us -> 5.1 us  [shifted(): lax.ppermute(value, axes, [(k, (k + step) % count) for k in range(count)])]
    all_to_all x1, waiting for transfers between devices: 4.68 us -> 3.74 us  [body(): right = lax.all_to_all(to_far, FAR, 0, 0, axis_index_groups=[list(ORDER)])]
  transfers between devices with their start and end apart: 10 -> 10, of which waited for: 7 -> 5; matrix products, arithmetic and copies ran while one was open for 0% -> 0% of each run, Pallas kernels for 3% -> 3%
where the time goes in v6:
time: 61.8 us; the launch traced here: 61.6 us
  blocking collectives  23.7 us (38%)
  starting transfers between devices  20.5 us (33%)
  waiting for transfers between devices  11.3 us (18%)
  Pallas kernels  5.97 us (10%)
    all_to_all x1, blocking collectives, body(): blocks = lax.all_to_all(block, NORTH, 0, 0)  12.7 us
    all_to_all x1, blocking collectives, body(): gathered = lax.all_to_all(partial.reshape(north, piece, depth), NORTH, 0, 0)  11 us
    all_to_all x1, starting transfers between devices, body(): right = lax.all_to_all(to_far, FAR, 0, 0, axis_index_groups=[list(ORDER)])  10 us
    ppermute x4, starting transfers between devices, exchanged(): return lax.ppermute(value, axes, list(enumerate(flip)))  5.97 us
    ppermute x5, waiting for transfers between devices, shifted(): lax.ppermute(value, axes, [(k, (k + step) % count) for k in range(count)])  5.1 us
    ppermute x5, starting transfers between devices, shifted(): lax.ppermute(value, axes, [(k, (k + step) % count) for k in range(count)])  4.48 us
    all_to_all x1, waiting for transfers between devices, body(): right = lax.all_to_all(to_far, FAR, 0, 0, axis_index_groups=[list(ORDER)])  3.74 us
    ppermute x4, waiting for transfers between devices, exchanged(): return lax.ppermute(value, axes, list(enumerate(flip)))  2.47 us
  transfers between devices with their start and end apart: 10, of which 5 were waited for; matrix products, arithmetic and copies ran while one was open for 0% of the time, Pallas kernels for 3%

profile of v6, /device:TPU:32, one launch (start us, length us, event | category | flops | bytes accessed | tf_op | source)
XLA Modules:
  0.0 61.6 jit_solution(10585730264468660476)
XLA Ops:
  0.0 0.0 copy-start
  0.0 0.0 copy-start.2
  0.0 1.2 %x_faces.1 = (f32[3,6,2,256]{3,2,1,0:T(2,128)S(1)}, f32[3,6,2,256]{3,2,1,0:T(2,128)S(1)}) custom-call(f32[3,10,64,256]{3,2,1,0:T(8,128)} %flow.5), custom_call_target="tpu_custom_call" | custom-call | tf_op jit(solution)/shard_map/x_faces/pallas_call | solution.py:233
  1.2 0.1 collective-permute-start
  1.3 2.0 %collective-permute-start.3 = (f32[3,6,2,256]{3,2,1,0:T(2,128)S(1)}, f32[3,6,2,256]{3,2,1,0:T(2,128)S(1)}, u32[]{:S(2)}, u32[]{:S(2)}) collective-permute-start(f32[3,6,2,256]{3,2,1,0:T(2,128)S(1)} %get-tuple-element.28), channel_id=1, source_target_pairs={{0,8},{8,0},{16,24},{24,16},{32,40},{40,32},{48,56},{56,48},{64,72... | collective-permute-start | bytes 110600 | tf_op jit(solution)/shard_map/ppermute | solution.py:26
  3.3 0.0 copy-done
  3.3 0.4 y_faces.1
  3.7 3.9 %collective-permute-start.1 = (f32[80,128]{1,0:T(8,128)S(1)}, f32[80,128]{1,0:T(8,128)S(1)}, u32[]{:S(2)}, u32[]{:S(2)}) collective-permute-start(f32[80,128]{1,0:T(8,128)S(1)} %get-tuple-element.26), channel_id=1, source_target_pairs={{0,7},{1,2},{2,1},{3,4},{4,3},{5,6},{6,5},{7,0},{8,15},{9,10},{10,... | collective-permute-start | bytes 122888 | tf_op jit(solution)/shard_map/ppermute | solution.py:26
  7.6 0.0 copy-start.1
  7.6 0.0 collective-permute-start.2
  7.6 0.0 copy-done.2
  7.6 1.5 %inner.1 = (f32[6,64,256]{2,1,0:T(8,128)S(1)}, f32[6,64,256]{2,1,0:T(8,128)S(1)}, f32[6,64,256]{2,1,0:T(8,128)S(1)}, f32[6,64,256]{2,1,0:T(8,128)S(1)}, f32[6,64...) custom-call(f32[3,10,64,256]{3,2,1,0:T(8,128)S(1)} %copy-done, f32[10,64,256]{2,1,0:T(8,128)S(1)} %copy-done.2), custom_call_target="tpu_custom_call" | custom-call | flops 2500000000 | bytes 5000000 | tf_op jit(solution)/shard_map/inner/pallas_call | solution.py:259
  9.1 0.0 collective-permute-done.refs_8_
  9.1 0.0 collective-permute-done.3.refs_11_
  9.1 0.8 %collective-permute-done.1.refs_9_ = f32[80,128]{1,0:T(8,128)S(1)} collective-permute-done((f32[80,128]{1,0:T(8,128)S(1)}, f32[80,128]{1,0:T(8,128)S(1)}, u32[]{:S(2)}, u32[]{:S(2)}) %collective-permute-start.1) | collective-permute-done | bytes 40992 | tf_op jit(solution)/shard_map/ppermute | solution.py:26
  9.9 1.7 %collective-permute-done.2.refs_10_ = f32[80,128]{1,0:T(8,128)S(1)} collective-permute-done((f32[80,128]{1,0:T(8,128)S(1)}, f32[80,128]{1,0:T(8,128)S(1)}, u32[]{:S(2)}, u32[]{:S(2)}) %collective-permute-start.2) | collective-permute-done | bytes 40992 | tf_op jit(solution)/shard_map/ppermute | solution.py:26
  11.6 0.0 copy-done.1
  11.6 0.7 %field.1 = f32[64,1536]{1,0:T(8,128)S(1)} custom-call(f32[6,64,256]{2,1,0:T(8,128)S(1)} %get-tuple-element.18.refs_0_, f32[6,64,256]{2,1,0:T(8,128)S(1)} %get-tuple-element.19.refs_1_, f32[6,64,256]{2,1,0:T(8,128)S(1)} %get-tuple-element.20.refs_2_, f32[6,64,256]{2,1,0:T(8,128)S(1)} %get-tuple-element.21.refs_3_, ...), custom_call_target="tpu_custom_call" | custom-call | tf_op jit(solution)/shard_map/field/pallas_call | solution.py:269
  12.2 11.0 %all_to_all.15.parts = f32[8,8,1536]{2,1,0:T(8,128)S(1)} all-to-all(f32[8,8,1536]{2,1,0:T(8,128)S(1)} %bitcast.1), channel_id=1, replica_groups=mesh['y_hi'=2,'z'=8,'core'=2,'x'=4,'y_lo'=2] {'x','y_lo'}, dimensions={0} | all-to-all | bytes 786432 | tf_op jit(solution)/shard_map/all_to_all | solution.py:281
  23.2 0.8 %total.1 = (bf16[1,8,1536]{2,1,0:T(8,128)(2,1)S(1)}, bf16[16,8,1536]{2,1,0:T(8,128)(2,1)}) custom-call(f32[8,8,1536]{2,1,0:T(8,128)S(1)} %all_to_all.15.parts), custom_call_target="tpu_custom_call" | custom-call | tf_op jit(solution)/shard_map/total/pallas_call | solution.py:282
  24.0 10.0 %all-to-all-start.1 = ((bf16[16,8,1536]{2,1,0:T(8,128)(2,1)}), bf16[16,8,1536]{2,1,0:T(8,128)(2,1)S(1)}, u32[]{:S(2)}, u32[]{:S(2)}) async-start(bf16[16,8,1536]{2,1,0:T(8,128)(2,1)} %get-tuple-element.30), calls=%async_computation.1 | async-start | bytes 786432 | tf_op jit(solution)/shard_map/all_to_all | solution.py:293
  34.0 0.4 collective-permute-start.4
  34.4 3.4 %collective-permute-done.4 = bf16[1,8,1536]{2,1,0:T(8,128)(2,1)S(1)} collective-permute-done((bf16[1,8,1536]{2,1,0:T(8,128)(2,1)S(1)}, bf16[1,8,1536]{2,1,0:T(8,128)(2,1)S(1)}, u32[]{:S(2)}, u32[]{:S(2)}) %collective-permute-start.4) | collective-permute-done | bytes 24608 | tf_op jit(solution)/shard_map/ppermute | solution.py:31
  37.9 0.5 collective-permute-start.7
  38.4 2.1 %collective-permute-start.6 = (bf16[2,8,1536]{2,1,0:T(8,128)(2,1)S(1)}, bf16[2,8,1536]{2,1,0:T(8,128)(2,1)S(1)}, u32[]{:S(2)}, u32[]{:S(2)}) collective-permute-start(bf16[2,8,1536]{2,1,0:T(8,128)(2,1)S(1)} %pad_maximum_fusion.refs_0_), channel_id=1, source_target_pairs={{0,4},{2,6},{4,0},{6,2},{1,5},{3,7},{5,1},{7,3},{8,12},{10,14},{12... | collective-permute-start | bytes 147464 | tf_op jit(solution)/shard_map/ppermute | solution.py:31
  40.5 1.5 %collective-permute-start.5 = (bf16[2,8,1536]{2,1,0:T(8,128)(2,1)S(1)}, bf16[2,8,1536]{2,1,0:T(8,128)(2,1)S(1)}, u32[]{:S(2)}, u32[]{:S(2)}) collective-permute-start(bf16[2,8,1536]{2,1,0:T(8,128)(2,1)S(1)} %pad_maximum_fusion.refs_0_), channel_id=1, source_target_pairs={{0,6},{2,0},{4,2},{6,4},{1,7},{3,1},{5,3},{7,5},{8,14},{10,8},{12,... | collective-permute-start | bytes 147464 | tf_op jit(solution)/shard_map/ppermute | solution.py:31
  41.9 3.7 %all-to-all-done.1.refs_1_ = bf16[16,8,1536]{2,1,0:T(8,128)(2,1)S(1)} async-done(((bf16[16,8,1536]{2,1,0:T(8,128)(2,1)}), bf16[16,8,1536]{2,1,0:T(8,128)(2,1)S(1)}, u32[]{:S(2)}, u32[]{:S(2)}) %all-to-all-start.1) | async-done | bytes 393248 | tf_op jit(solution)/shard_map/all_to_all | solution.py:293
  45.7 0.0 collective-permute-start.8
  45.7 0.0 collective-permute-done.7.refs_3_
  45.7 0.0 collective-permute-done.6.refs_2_
  45.7 0.0 collective-permute-done.5.refs_1_
  45.7 1.7 %collective-permute-done.8.refs_2_ = bf16[16,8,1536]{2,1,0:T(8,128)(2,1)S(1)} collective-permute-done((bf16[16,8,1536]{2,1,0:T(8,128)(2,1)S(1)}, bf16[16,8,1536]{2,1,0:T(8,128)(2,1)S(1)}, u32[]{:S(2)}, u32[]{:S(2)}) %collective-permute-start.8) | collective-permute-done | bytes 393248 | tf_op jit(solution)/shard_map/ppermute | solution.py:31
  47.4 0.5 block.1
  47.9 12.7 %all_to_all.16.refs_0_ = f32[8,128,128]{2,1,0:T(8,128)S(1)} all-to-all(f32[8,128,128]{2,1,0:T(8,128)S(1)} %block.1), channel_id=1, replica_groups=mesh['y_hi'=2,'z'=8,'core'=2,'x'=4,'y_lo'=2] {'x','y_lo'}, dimensions={0} | all-to-all | bytes 1048576 | tf_op jit(solution)/shard_map/all_to_all | solution.py:326
  60.6 1.0 %place.1 = f32[64,2048]{1,0:T(8,128)} custom-call(f32[8,128,128]{2,1,0:T(8,128)S(1)} %all_to_all.16.refs_0_), custom_call_target="tpu_custom_call" | custom-call | tf_op jit(solution)/shard_map/place/pallas_call | solution.py:327
  (3 shorter events, 0.0 us)
Async XLA Ops:
  0.0 3.3 %copy-start = (f32[3,10,64,256]{3,2,1,0:T(8,128)S(1)}, f32[3,10,64,256]{3,2,1,0:T(8,128)}, u32[]{:S(2)}) copy-start(f32[3,10,64,256]{3,2,1,0:T(8,128)} %flow.5) | copy-start | bytes 5898244
  0.0 7.6 %copy-start.2 = (f32[10,64,256]{2,1,0:T(8,128)S(1)}, f32[10,64,256]{2,1,0:T(8,128)}, u32[]{:S(2)}) copy-start(f32[10,64,256]{2,1,0:T(8,128)} %thermal.1) | copy-start | bytes 1966084
  1.2 7.9 %collective-permute-start = (f32[3,6,2,256]{3,2,1,0:T(2,128)S(1)}, f32[3,6,2,256]{3,2,1,0:T(2,128)S(1)}, u32[]{:S(2)}, u32[]{:S(2)}) collective-permute-start(f32[3,6,2,256]{3,2,1,0:T(2,128)S(1)} %get-tuple-element.25), channel_id=1, source_target_pairs={{0,248},{8,16},{16,8},{24,32},{32,24},{40,48},{48,40},{56,64},{64,... | collective-permute-start | bytes 110600 | tf_op jit(solution)/shard_map/ppermute | solution.py:26
  1.3 7.8 %collective-permute-start.3 = (f32[3,6,2,256]{3,2,1,0:T(2,128)S(1)}, f32[3,6,2,256]{3,2,1,0:T(2,128)S(1)}, u32[]{:S(2)}, u32[]{:S(2)}) collective-permute-start(f32[3,6,2,256]{3,2,1,0:T(2,128)S(1)} %get-tuple-element.28), channel_id=1, source_target_pairs={{0,8},{8,0},{16,24},{24,16},{32,40},{40,32},{48,56},{56,48},{64,72... | collective-permute-start | bytes 110600 | tf_op jit(solution)/shard_map/ppermute | solution.py:26
  3.7 6.2 %collective-permute-start.1 = (f32[80,128]{1,0:T(8,128)S(1)}, f32[80,128]{1,0:T(8,128)S(1)}, u32[]{:S(2)}, u32[]{:S(2)}) collective-permute-start(f32[80,128]{1,0:T(8,128)S(1)} %get-tuple-element.26), channel_id=1, source_target_pairs={{0,7},{1,2},{2,1},{3,4},{4,3},{5,6},{6,5},{7,0},{8,15},{9,10},{10,... | collective-permute-start | bytes 122888 | tf_op jit(solution)/shard_map/ppermute | solution.py:26
  7.6 4.0 %copy-start.1 = (bf16[256,256]{1,0:T(8,128)(2,1)S(1)}, bf16[256,256]{1,0:T(8,128)(2,1)}, u32[]{:S(2)}) copy-start(bf16[256,256]{1,0:T(8,128)(2,1)} %refs_7_.1) | copy-start | bytes 393220
  7.6 4.0 %collective-permute-start.2 = (f32[80,128]{1,0:T(8,128)S(1)}, f32[80,128]{1,0:T(8,128)S(1)}, u32[]{:S(2)}, u32[]{:S(2)}) collective-permute-start(f32[80,128]{1,0:T(8,128)S(1)} %get-tuple-element.27), channel_id=1, source_target_pairs={{0,1},{1,0},{2,3},{3,2},{4,5},{5,4},{6,7},{7,6},{8,9},{9,8},{10,11... | collective-permute-start | bytes 122888 | tf_op jit(solution)/shard_map/ppermute | solution.py:26
  24.0 21.7 %all-to-all-start.1 = ((bf16[16,8,1536]{2,1,0:T(8,128)(2,1)}), bf16[16,8,1536]{2,1,0:T(8,128)(2,1)S(1)}, u32[]{:S(2)}, u32[]{:S(2)}) async-start(bf16[16,8,1536]{2,1,0:T(8,128)(2,1)} %get-tuple-element.30), calls=%async_computation.1 | async-start | bytes 786432 | tf_op jit(solution)/shard_map/all_to_all | solution.py:293
  34.0 3.9 %collective-permute-start.4 = (bf16[1,8,1536]{2,1,0:T(8,128)(2,1)S(1)}, bf16[1,8,1536]{2,1,0:T(8,128)(2,1)S(1)}, u32[]{:S(2)}, u32[]{:S(2)}) collective-permute-start(bf16[1,8,1536]{2,1,0:T(8,128)(2,1)S(1)} %get-tuple-element.29.source), channel_id=1, source_target_pairs={{0,1},{1,0},{2,3},{3,2},{4,5},{5,4},{6,7},{7,6},{8,9},{9,8},{10,11... | collective-permute-start | bytes 73736 | tf_op jit(solution)/shard_map/ppermute | solution.py:31
  37.9 7.8 %collective-permute-start.7 = (bf16[2,8,1536]{2,1,0:T(8,128)(2,1)S(1)}, bf16[2,8,1536]{2,1,0:T(8,128)(2,1)S(1)}, u32[]{:S(2)}, u32[]{:S(2)}) collective-permute-start(bf16[2,8,1536]{2,1,0:T(8,128)(2,1)S(1)} %pad_maximum_fusion.refs_0_), channel_id=1, source_target_pairs={{0,2},{2,4},{4,6},{6,0},{1,3},{3,5},{5,7},{7,1},{8,10},{10,12},{12... | collective-permute-start | bytes 147464 | tf_op jit(solution)/shard_map/ppermute | solution.py:31
  38.4 7.3 %collective-permute-start.6 = (bf16[2,8,1536]{2,1,0:T(8,128)(2,1)S(1)}, bf16[2,8,1536]{2,1,0:T(8,128)(2,1)S(1)}, u32[]{:S(2)}, u32[]{:S(2)}) collective-permute-start(bf16[2,8,1536]{2,1,0:T(8,128)(2,1)S(1)} %pad_maximum_fusion.refs_0_), channel_id=1, source_target_pairs={{0,4},{2,6},{4,0},{6,2},{1,5},{3,7},{5,1},{7,3},{8,12},{10,14},{12... | collective-permute-start | bytes 147464 | tf_op jit(solution)/shard_map/ppermute | solution.py:31
  40.5 5.2 %collective-permute-start.5 = (bf16[2,8,1536]{2,1,0:T(8,128)(2,1)S(1)}, bf16[2,8,1536]{2,1,0:T(8,128)(2,1)S(1)}, u32[]{:S(2)}, u32[]{:S(2)}) collective-permute-start(bf16[2,8,1536]{2,1,0:T(8,128)(2,1)S(1)} %pad_maximum_fusion.refs_0_), channel_id=1, source_target_pairs={{0,6},{2,0},{4,2},{6,4},{1,7},{3,1},{5,3},{7,5},{8,14},{10,8},{12,... | collective-permute-start | bytes 147464 | tf_op jit(solution)/shard_map/ppermute | solution.py:31
  45.7 1.7 %collective-permute-start.8 = (bf16[16,8,1536]{2,1,0:T(8,128)(2,1)S(1)}, bf16[16,8,1536]{2,1,0:T(8,128)(2,1)S(1)}, u32[]{:S(2)}, u32[]{:S(2)}) collective-permute-start(bf16[16,8,1536]{2,1,0:T(8,128)(2,1)S(1)} %all-to-all-done.1.refs_1_), channel_id=1, source_target_pairs={{0,8},{8,0},{1,9},{9,1},{2,10},{10,2},{3,11},{11,3},{4,12},{12,4},... | collective-permute-start | bytes 1179656 | tf_op jit(solution)/shard_map/ppermute | solution.py:31

commit v7 on v6

--- a/solution.py
+++ b/solution.py
@@ -10,7 +10,7 @@
 FAR = ("y_hi", "z")
 EAST = ("y_hi", "z", "core")
 NORTH = ("x", "y_lo")
-ORDER = (0, 3, 6, 1, 4, 7, 2, 5, 8, 11, 14, 9, 12, 15, 10, 13)
+ORDER = (8, 11, 14, 9, 12, 15, 10, 13, 0, 3, 6, 1, 4, 7, 2, 5)
 LIMIT = 48 * 1024 * 1024
 
 

time: 61.8 us -> 61.3 us (level)
  waiting for transfers between devices: 11.3 us -> 9.75 us
  starting transfers between devices: 20.5 us -> 21.4 us
    all_to_all x1, waiting for transfers between devices: 3.74 us -> 2.8 us  [body(): right = lax.all_to_all(to_far, FAR, 0, 0, axis_index_groups=[list(ORDER)])]
    ppermute x5, starting transfers between devices: 4.48 us -> 5.38 us  [shifted(): lax.ppermute(value, axes, [(k, (k + step) % count) for k in range(count)])]
    ppermute x5, waiting for transfers between devices: 5.1 us -> 4.48 us  [shifted(): lax.ppermute(value, axes, [(k, (k + step) % count) for k in range(count)])]
where the time goes in v7:
time: 61.3 us; the launch traced here: 61 us
  blocking collectives  23.8 us (39%)
  starting transfers between devices  21.4 us (35%)
  waiting for transfers between devices  9.75 us (16%)
  Pallas kernels  5.98 us (10%)
    all_to_all x1, blocking collectives, body(): blocks = lax.all_to_all(block, NORTH, 0, 0)  12.8 us
    all_to_all x1, blocking collectives, body(): gathered = lax.all_to_all(partial.reshape(north, piece, depth), NORTH, 0, 0)  11 us
    all_to_all x1, starting transfers between devices, body(): right = lax.all_to_all(to_far, FAR, 0, 0, axis_index_groups=[list(ORDER)])  10.1 us
    ppermute x4, starting transfers between devices, exchanged(): return lax.ppermute(value, axes, list(enumerate(flip)))  5.97 us
    ppermute x5, starting transfers between devices, shifted(): lax.ppermute(value, axes, [(k, (k + step) % count) for k in range(count)])  5.38 us
    ppermute x5, waiting for transfers between devices, shifted(): lax.ppermute(value, axes, [(k, (k + step) % count) for k in range(count)])  4.48 us
    all_to_all x1, waiting for transfers between devices, body(): right = lax.all_to_all(to_far, FAR, 0, 0, axis_index_groups=[list(ORDER)])  2.8 us
    ppermute x4, waiting for transfers between devices, exchanged(): return lax.ppermute(value, axes, list(enumerate(flip)))  2.47 us
  transfers between devices with their start and end apart: 10, of which 5 were waited for; matrix products, arithmetic and copies ran while one was open for 0% of the time, Pallas kernels for 3%

profile of v7, /device:TPU:32, one launch (start us, length us, event | category | flops | bytes accessed | tf_op | source)
XLA Modules:
  0.0 61.0 jit_solution(2185555811053339808)
XLA Ops:
  0.0 0.0 copy-start
  0.0 0.0 copy-start.2
  0.0 1.2 %x_faces.1 = (f32[3,6,2,256]{3,2,1,0:T(2,128)S(1)}, f32[3,6,2,256]{3,2,1,0:T(2,128)S(1)}) custom-call(f32[3,10,64,256]{3,2,1,0:T(8,128)} %flow.5), custom_call_target="tpu_custom_call" | custom-call | tf_op jit(solution)/shard_map/x_faces/pallas_call | solution.py:233
  1.2 0.1 collective-permute-start
  1.3 2.0 %collective-permute-start.3 = (f32[3,6,2,256]{3,2,1,0:T(2,128)S(1)}, f32[3,6,2,256]{3,2,1,0:T(2,128)S(1)}, u32[]{:S(2)}, u32[]{:S(2)}) collective-permute-start(f32[3,6,2,256]{3,2,1,0:T(2,128)S(1)} %get-tuple-element.28), channel_id=1, source_target_pairs={{0,8},{8,0},{16,24},{24,16},{32,40},{40,32},{48,56},{56,48},{64,72... | collective-permute-start | bytes 110600 | tf_op jit(solution)/shard_map/ppermute | solution.py:26
  3.3 0.0 copy-done
  3.3 0.4 y_faces.1
  3.7 3.9 %collective-permute-start.1 = (f32[80,128]{1,0:T(8,128)S(1)}, f32[80,128]{1,0:T(8,128)S(1)}, u32[]{:S(2)}, u32[]{:S(2)}) collective-permute-start(f32[80,128]{1,0:T(8,128)S(1)} %get-tuple-element.26), channel_id=1, source_target_pairs={{0,7},{1,2},{2,1},{3,4},{4,3},{5,6},{6,5},{7,0},{8,15},{9,10},{10,... | collective-permute-start | bytes 122888 | tf_op jit(solution)/shard_map/ppermute | solution.py:26
  7.6 0.0 copy-start.1
  7.6 0.0 collective-permute-start.2
  7.6 0.0 copy-done.2
  7.6 1.5 %inner.1 = (f32[6,64,256]{2,1,0:T(8,128)S(1)}, f32[6,64,256]{2,1,0:T(8,128)S(1)}, f32[6,64,256]{2,1,0:T(8,128)S(1)}, f32[6,64,256]{2,1,0:T(8,128)S(1)}, f32[6,64...) custom-call(f32[3,10,64,256]{3,2,1,0:T(8,128)S(1)} %copy-done, f32[10,64,256]{2,1,0:T(8,128)S(1)} %copy-done.2), custom_call_target="tpu_custom_call" | custom-call | flops 2500000000 | bytes 5000000 | tf_op jit(solution)/shard_map/inner/pallas_call | solution.py:259
  9.1 0.0 collective-permute-done.refs_8_
  9.1 0.0 collective-permute-done.3.refs_11_
  9.1 0.8 %collective-permute-done.1.refs_9_ = f32[80,128]{1,0:T(8,128)S(1)} collective-permute-done((f32[80,128]{1,0:T(8,128)S(1)}, f32[80,128]{1,0:T(8,128)S(1)}, u32[]{:S(2)}, u32[]{:S(2)}) %collective-permute-start.1) | collective-permute-done | bytes 40992 | tf_op jit(solution)/shard_map/ppermute | solution.py:26
  9.9 1.7 %collective-permute-done.2.refs_10_ = f32[80,128]{1,0:T(8,128)S(1)} collective-permute-done((f32[80,128]{1,0:T(8,128)S(1)}, f32[80,128]{1,0:T(8,128)S(1)}, u32[]{:S(2)}, u32[]{:S(2)}) %collective-permute-start.2) | collective-permute-done | bytes 40992 | tf_op jit(solution)/shard_map/ppermute | solution.py:26
  11.6 0.0 copy-done.1
  11.6 0.7 %field.1 = f32[64,1536]{1,0:T(8,128)S(1)} custom-call(f32[6,64,256]{2,1,0:T(8,128)S(1)} %get-tuple-element.18.refs_0_, f32[6,64,256]{2,1,0:T(8,128)S(1)} %get-tuple-element.19.refs_1_, f32[6,64,256]{2,1,0:T(8,128)S(1)} %get-tuple-element.20.refs_2_, f32[6,64,256]{2,1,0:T(8,128)S(1)} %get-tuple-element.21.refs_3_, ...), custom_call_target="tpu_custom_call" | custom-call | tf_op jit(solution)/shard_map/field/pallas_call | solution.py:269
  12.2 11.0 %all_to_all.15.parts = f32[8,8,1536]{2,1,0:T(8,128)S(1)} all-to-all(f32[8,8,1536]{2,1,0:T(8,128)S(1)} %bitcast.1), channel_id=1, replica_groups=mesh['y_hi'=2,'z'=8,'core'=2,'x'=4,'y_lo'=2] {'x','y_lo'}, dimensions={0} | all-to-all | bytes 786432 | tf_op jit(solution)/shard_map/all_to_all | solution.py:281
  23.2 0.8 %total.1 = (bf16[1,8,1536]{2,1,0:T(8,128)(2,1)S(1)}, bf16[16,8,1536]{2,1,0:T(8,128)(2,1)}) custom-call(f32[8,8,1536]{2,1,0:T(8,128)S(1)} %all_to_all.15.parts), custom_call_target="tpu_custom_call" | custom-call | tf_op jit(solution)/shard_map/total/pallas_call | solution.py:282
  24.0 10.1 %all-to-all-start.1 = ((bf16[16,8,1536]{2,1,0:T(8,128)(2,1)}), bf16[16,8,1536]{2,1,0:T(8,128)(2,1)S(1)}, u32[]{:S(2)}, u32[]{:S(2)}) async-start(bf16[16,8,1536]{2,1,0:T(8,128)(2,1)} %get-tuple-element.30), calls=%async_computation.1 | async-start | bytes 786432 | tf_op jit(solution)/shard_map/all_to_all | solution.py:293
  34.1 1.0 %collective-permute-start.4 = (bf16[1,8,1536]{2,1,0:T(8,128)(2,1)S(1)}, bf16[1,8,1536]{2,1,0:T(8,128)(2,1)S(1)}, u32[]{:S(2)}, u32[]{:S(2)}) collective-permute-start(bf16[1,8,1536]{2,1,0:T(8,128)(2,1)S(1)} %get-tuple-element.29.source), channel_id=1, source_target_pairs={{0,1},{1,0},{2,3},{3,2},{4,5},{5,4},{6,7},{7,6},{8,9},{9,8},{10,11... | collective-permute-start | bytes 73736 | tf_op jit(solution)/shard_map/ppermute | solution.py:31
  35.1 2.8 %collective-permute-done.4 = bf16[1,8,1536]{2,1,0:T(8,128)(2,1)S(1)} collective-permute-done((bf16[1,8,1536]{2,1,0:T(8,128)(2,1)S(1)}, bf16[1,8,1536]{2,1,0:T(8,128)(2,1)S(1)}, u32[]{:S(2)}, u32[]{:S(2)}) %collective-permute-start.4) | collective-permute-done | bytes 24608 | tf_op jit(solution)/shard_map/ppermute | solution.py:31
  37.9 0.5 collective-permute-start.7
  38.4 2.1 %collective-permute-start.6 = (bf16[2,8,1536]{2,1,0:T(8,128)(2,1)S(1)}, bf16[2,8,1536]{2,1,0:T(8,128)(2,1)S(1)}, u32[]{:S(2)}, u32[]{:S(2)}) collective-permute-start(bf16[2,8,1536]{2,1,0:T(8,128)(2,1)S(1)} %pad_maximum_fusion.refs_0_), channel_id=1, source_target_pairs={{0,4},{2,6},{4,0},{6,2},{1,5},{3,7},{5,1},{7,3},{8,12},{10,14},{12... | collective-permute-start | bytes 147464 | tf_op jit(solution)/shard_map/ppermute | solution.py:31
  40.5 1.8 %collective-permute-start.5 = (bf16[2,8,1536]{2,1,0:T(8,128)(2,1)S(1)}, bf16[2,8,1536]{2,1,0:T(8,128)(2,1)S(1)}, u32[]{:S(2)}, u32[]{:S(2)}) collective-permute-start(bf16[2,8,1536]{2,1,0:T(8,128)(2,1)S(1)} %pad_maximum_fusion.refs_0_), channel_id=1, source_target_pairs={{0,6},{2,0},{4,2},{6,4},{1,7},{3,1},{5,3},{7,5},{8,14},{10,8},{12,... | collective-permute-start | bytes 147464 | tf_op jit(solution)/shard_map/ppermute | solution.py:31
  42.3 2.8 %all-to-all-done.1.refs_1_ = bf16[16,8,1536]{2,1,0:T(8,128)(2,1)S(1)} async-done(((bf16[16,8,1536]{2,1,0:T(8,128)(2,1)}), bf16[16,8,1536]{2,1,0:T(8,128)(2,1)S(1)}, u32[]{:S(2)}, u32[]{:S(2)}) %all-to-all-start.1) | async-done | bytes 393248 | tf_op jit(solution)/shard_map/all_to_all | solution.py:293
  45.1 0.0 collective-permute-start.8
  45.1 0.0 collective-permute-done.7.refs_3_
  45.1 0.0 collective-permute-done.6.refs_2_
  45.1 0.0 collective-permute-done.5.refs_1_
  45.1 1.7 %collective-permute-done.8.refs_2_ = bf16[16,8,1536]{2,1,0:T(8,128)(2,1)S(1)} collective-permute-done((bf16[16,8,1536]{2,1,0:T(8,128)(2,1)S(1)}, bf16[16,8,1536]{2,1,0:T(8,128)(2,1)S(1)}, u32[]{:S(2)}, u32[]{:S(2)}) %collective-permute-start.8) | collective-permute-done | bytes 393248 | tf_op jit(solution)/shard_map/ppermute | solution.py:31
  46.8 0.5 block.1
  47.3 12.8 %all_to_all.16.refs_0_ = f32[8,128,128]{2,1,0:T(8,128)S(1)} all-to-all(f32[8,128,128]{2,1,0:T(8,128)S(1)} %block.1), channel_id=1, replica_groups=mesh['y_hi'=2,'z'=8,'core'=2,'x'=4,'y_lo'=2] {'x','y_lo'}, dimensions={0} | all-to-all | bytes 1048576 | tf_op jit(solution)/shard_map/all_to_all | solution.py:326
  60.0 1.0 %place.1 = f32[64,2048]{1,0:T(8,128)} custom-call(f32[8,128,128]{2,1,0:T(8,128)S(1)} %all_to_all.16.refs_0_), custom_call_target="tpu_custom_call" | custom-call | tf_op jit(solution)/shard_map/place/pallas_call | solution.py:327
  (3 shorter events, 0.0 us)
Async XLA Ops:
  0.0 3.3 %copy-start = (f32[3,10,64,256]{3,2,1,0:T(8,128)S(1)}, f32[3,10,64,256]{3,2,1,0:T(8,128)}, u32[]{:S(2)}) copy-start(f32[3,10,64,256]{3,2,1,0:T(8,128)} %flow.5) | copy-start | bytes 5898244
  0.0 7.6 %copy-start.2 = (f32[10,64,256]{2,1,0:T(8,128)S(1)}, f32[10,64,256]{2,1,0:T(8,128)}, u32[]{:S(2)}) copy-start(f32[10,64,256]{2,1,0:T(8,128)} %thermal.1) | copy-start | bytes 1966084
  1.2 7.9 %collective-permute-start = (f32[3,6,2,256]{3,2,1,0:T(2,128)S(1)}, f32[3,6,2,256]{3,2,1,0:T(2,128)S(1)}, u32[]{:S(2)}, u32[]{:S(2)}) collective-permute-start(f32[3,6,2,256]{3,2,1,0:T(2,128)S(1)} %get-tuple-element.25), channel_id=1, source_target_pairs={{0,248},{8,16},{16,8},{24,32},{32,24},{40,48},{48,40},{56,64},{64,... | collective-permute-start | bytes 110600 | tf_op jit(solution)/shard_map/ppermute | solution.py:26
  1.3 7.8 %collective-permute-start.3 = (f32[3,6,2,256]{3,2,1,0:T(2,128)S(1)}, f32[3,6,2,256]{3,2,1,0:T(2,128)S(1)}, u32[]{:S(2)}, u32[]{:S(2)}) collective-permute-start(f32[3,6,2,256]{3,2,1,0:T(2,128)S(1)} %get-tuple-element.28), channel_id=1, source_target_pairs={{0,8},{8,0},{16,24},{24,16},{32,40},{40,32},{48,56},{56,48},{64,72... | collective-permute-start | bytes 110600 | tf_op jit(solution)/shard_map/ppermute | solution.py:26
  3.7 6.2 %collective-permute-start.1 = (f32[80,128]{1,0:T(8,128)S(1)}, f32[80,128]{1,0:T(8,128)S(1)}, u32[]{:S(2)}, u32[]{:S(2)}) collective-permute-start(f32[80,128]{1,0:T(8,128)S(1)} %get-tuple-element.26), channel_id=1, source_target_pairs={{0,7},{1,2},{2,1},{3,4},{4,3},{5,6},{6,5},{7,0},{8,15},{9,10},{10,... | collective-permute-start | bytes 122888 | tf_op jit(solution)/shard_map/ppermute | solution.py:26
  7.6 4.0 %copy-start.1 = (bf16[256,256]{1,0:T(8,128)(2,1)S(1)}, bf16[256,256]{1,0:T(8,128)(2,1)}, u32[]{:S(2)}) copy-start(bf16[256,256]{1,0:T(8,128)(2,1)} %refs_7_.1) | copy-start | bytes 393220
  7.6 4.0 %collective-permute-start.2 = (f32[80,128]{1,0:T(8,128)S(1)}, f32[80,128]{1,0:T(8,128)S(1)}, u32[]{:S(2)}, u32[]{:S(2)}) collective-permute-start(f32[80,128]{1,0:T(8,128)S(1)} %get-tuple-element.27), channel_id=1, source_target_pairs={{0,1},{1,0},{2,3},{3,2},{4,5},{5,4},{6,7},{7,6},{8,9},{9,8},{10,11... | collective-permute-start | bytes 122888 | tf_op jit(solution)/shard_map/ppermute | solution.py:26
  24.0 21.1 %all-to-all-start.1 = ((bf16[16,8,1536]{2,1,0:T(8,128)(2,1)}), bf16[16,8,1536]{2,1,0:T(8,128)(2,1)S(1)}, u32[]{:S(2)}, u32[]{:S(2)}) async-start(bf16[16,8,1536]{2,1,0:T(8,128)(2,1)} %get-tuple-element.30), calls=%async_computation.1 | async-start | bytes 786432 | tf_op jit(solution)/shard_map/all_to_all | solution.py:293
  34.1 3.8 %collective-permute-start.4 = (bf16[1,8,1536]{2,1,0:T(8,128)(2,1)S(1)}, bf16[1,8,1536]{2,1,0:T(8,128)(2,1)S(1)}, u32[]{:S(2)}, u32[]{:S(2)}) collective-permute-start(bf16[1,8,1536]{2,1,0:T(8,128)(2,1)S(1)} %get-tuple-element.29.source), channel_id=1, source_target_pairs={{0,1},{1,0},{2,3},{3,2},{4,5},{5,4},{6,7},{7,6},{8,9},{9,8},{10,11... | collective-permute-start | bytes 73736 | tf_op jit(solution)/shard_map/ppermute | solution.py:31
  37.9 7.2 %collective-permute-start.7 = (bf16[2,8,1536]{2,1,0:T(8,128)(2,1)S(1)}, bf16[2,8,1536]{2,1,0:T(8,128)(2,1)S(1)}, u32[]{:S(2)}, u32[]{:S(2)}) collective-permute-start(bf16[2,8,1536]{2,1,0:T(8,128)(2,1)S(1)} %pad_maximum_fusion.refs_0_), channel_id=1, source_target_pairs={{0,2},{2,4},{4,6},{6,0},{1,3},{3,5},{5,7},{7,1},{8,10},{10,12},{12... | collective-permute-start | bytes 147464 | tf_op jit(solution)/shard_map/ppermute | solution.py:31
  38.4 6.7 %collective-permute-start.6 = (bf16[2,8,1536]{2,1,0:T(8,128)(2,1)S(1)}, bf16[2,8,1536]{2,1,0:T(8,128)(2,1)S(1)}, u32[]{:S(2)}, u32[]{:S(2)}) collective-permute-start(bf16[2,8,1536]{2,1,0:T(8,128)(2,1)S(1)} %pad_maximum_fusion.refs_0_), channel_id=1, source_target_pairs={{0,4},{2,6},{4,0},{6,2},{1,5},{3,7},{5,1},{7,3},{8,12},{10,14},{12... | collective-permute-start | bytes 147464 | tf_op jit(solution)/shard_map/ppermute | solution.py:31
  40.5 4.6 %collective-permute-start.5 = (bf16[2,8,1536]{2,1,0:T(8,128)(2,1)S(1)}, bf16[2,8,1536]{2,1,0:T(8,128)(2,1)S(1)}, u32[]{:S(2)}, u32[]{:S(2)}) collective-permute-start(bf16[2,8,1536]{2,1,0:T(8,128)(2,1)S(1)} %pad_maximum_fusion.refs_0_), channel_id=1, source_target_pairs={{0,6},{2,0},{4,2},{6,4},{1,7},{3,1},{5,3},{7,5},{8,14},{10,8},{12,... | collective-permute-start | bytes 147464 | tf_op jit(solution)/shard_map/ppermute | solution.py:31
  45.1 1.7 %collective-permute-start.8 = (bf16[16,8,1536]{2,1,0:T(8,128)(2,1)S(1)}, bf16[16,8,1536]{2,1,0:T(8,128)(2,1)S(1)}, u32[]{:S(2)}, u32[]{:S(2)}) collective-permute-start(bf16[16,8,1536]{2,1,0:T(8,128)(2,1)S(1)} %all-to-all-done.1.refs_1_), channel_id=1, source_target_pairs={{0,8},{8,0},{1,9},{9,1},{2,10},{10,2},{3,11},{11,3},{4,12},{12,4},... | collective-permute-start | bytes 1179656 | tf_op jit(solution)/shard_map/ppermute | solution.py:31

commit v8 on v7

--- a/solution.py
+++ b/solution.py
@@ -10,7 +10,8 @@
 FAR = ("y_hi", "z")
 EAST = ("y_hi", "z", "core")
 NORTH = ("x", "y_lo")
-ORDER = (8, 11, 14, 9, 12, 15, 10, 13, 0, 3, 6, 1, 4, 7, 2, 5)
+RING = (0, 3, 6, 1, 4, 7, 2, 5)
+ORDER = tuple(8 + at for at in RING) + RING
 LIMIT = 48 * 1024 * 1024
 
 
@@ -182,39 +183,44 @@
     target[...] = source[...]
 
 
-def arrange_kernel(*refs):
-    pairs, left = refs[:4], refs[4]
+def products(rows, left, scale):
+    count, piece, depth = rows.shape
+    a = left[...].reshape(left.shape[0] * piece, depth)
+    half = count // 2
+    sides = []
+    for slots in (slice(half, count), slice(0, half)):
+        w = rows[slots].reshape(half * piece, depth)
+        sides.append(lax.dot_general(w, a, (((1,), (1,)), ((), ())), preferred_element_type=jnp.float32))
+    return jnp.concatenate(sides, axis=1) * scale
+
+
+def arrange_kernel(scale, *refs):
+    pairs, own, left, share = refs[:4], refs[4], refs[5], refs[6]
     x, y_lo = lax.axis_index("x"), lax.axis_index("y_lo")
     for step, pair in enumerate(pairs):
         at = 2 * lax.rem(x + step, 4)
         left[at + y_lo] = pair[0]
         left[at + 1 - y_lo] = pair[1]
-
-
-def block_kernel(scale, left, own, other, out, right):
+    share[...] = products(own, left, scale)
+
+
+def block_kernel(scale, left, share, other, out):
     core = lax.axis_index("core")
-    count, piece, depth = own.shape
-    a = left[...].reshape(left.shape[0] * piece, depth)
-    half = count // 2
-    for slot, at in enumerate(ORDER):
-        right[core, at] = own[slot]
-        right[1 - core, at] = other[slot]
-    sides = []
-    for side in range(2):
-        w = right[:, side * half : (side + 1) * half].reshape(count * piece, depth)
-        sides.append(lax.dot_general(w, a, (((1,), (1,)), ((), ())), preferred_element_type=jnp.float32))
-    block = jnp.concatenate(sides, axis=1) * scale
+    mine, theirs = share[...], products(other, left, scale)
+    size = mine.shape[0]
+    near, away = pl.multiple_of(core * size, size), pl.multiple_of((1 - core) * size, size)
     for at in range(out.shape[0]):
-        out[at] = block
+        out[at, pl.ds(near, size)] = mine
+        out[at, pl.ds(away, size)] = theirs
 
 
 def place_kernel(piece, blocks, out):
     count, total, _ = blocks.shape
     tiles = total // (2 * piece)
     side = out.shape[0]
-    for tile in range(tiles):
+    for slot, tile in enumerate(RING):
         rows = [
-            blocks[at, (core * tiles + tile) * piece : (core * tiles + tile + 1) * piece, :]
+            blocks[at, (core * tiles + slot) * piece : (core * tiles + slot + 1) * piece, :]
             for core in range(2)
             for at in range(count)
         ]
@@ -303,26 +309,28 @@
     )(own)
     pair = jnp.concatenate([own, beside])
     pairs = [pair] + [shifted(pair, "x", -step) for step in range(1, 4)]
-    left = pl.pallas_call(
-        arrange_kernel,
-        out_shape=jax.ShapeDtypeStruct((north, piece, depth), jnp.bfloat16),
-        in_specs=[VMEM] * 4,
-        out_specs=VMEM,
+    scale = 1.0 / depth
+    left, share = pl.pallas_call(
+        lambda *refs: arrange_kernel(scale, *refs),
+        out_shape=(
+            jax.ShapeDtypeStruct((north, piece, depth), jnp.bfloat16),
+            jax.ShapeDtypeStruct((far * piece // 2, 128), f32),
+        ),
+        in_specs=[VMEM] * 5,
+        out_specs=(VMEM, VMEM),
         compiler_params=params(),
         cost_estimate=pl.CostEstimate(flops=5_000_000_000, bytes_accessed=4 * piece * depth * north, transcendentals=0),
         name="arrange",
-    )(*pairs)
+    )(*pairs, right)
     other = shifted(right, "core", 1)
-    scale = 1.0 / depth
     block = pl.pallas_call(
         lambda *refs: block_kernel(scale, *refs),
         out_shape=jax.ShapeDtypeStruct((north, far * piece, 128), f32),
         in_specs=[VMEM] * 3,
         out_specs=VMEM,
-        scratch_shapes=[pltpu.VMEM((2, far, piece, depth), jnp.bfloat16)],
         compiler_params=params(),
         name="block",
-    )(left, right, other)
+    )(left, share, other)
     blocks = lax.all_to_all(block, NORTH, 0, 0)
     return pl.pallas_call(
         lambda *refs: place_kernel(piece, *refs),

time: 61.3 us -> 61.2 us (level)
  transfers between devices with their start and end apart: 10 -> 10, of which waited for: 5 -> 5; matrix products, arithmetic and copies ran while one was open for 0% -> 0% of each run, Pallas kernels for 3% -> 4%
where the time goes in v8:
time: 61.2 us; the launch traced here: 60.9 us
  blocking collectives  23.8 us (39%)
  starting transfers between devices  21.4 us (35%)
  waiting for transfers between devices  9.43 us (15%)
  Pallas kernels  6.17 us (10%)
    all_to_all x1, blocking collectives, body(): blocks = lax.all_to_all(block, NORTH, 0, 0)  12.8 us
    all_to_all x1, blocking collectives, body(): gathered = lax.all_to_all(partial.reshape(north, piece, depth), NORTH, 0, 0)  11 us
    all_to_all x1, starting transfers between devices, body(): right = lax.all_to_all(to_far, FAR, 0, 0, axis_index_groups=[list(ORDER)])  10.1 us
    ppermute x4, starting transfers between devices, exchanged(): return lax.ppermute(value, axes, list(enumerate(flip)))  5.97 us
    ppermute x5, starting transfers between devices, shifted(): lax.ppermute(value, axes, [(k, (k + step) % count) for k in range(count)])  5.38 us
    ppermute x5, waiting for transfers between devices, shifted(): lax.ppermute(value, axes, [(k, (k + step) % count) for k in range(count)])  4.17 us
    all_to_all x1, waiting for transfers between devices, body(): right = lax.all_to_all(to_far, FAR, 0, 0, axis_index_groups=[list(ORDER)])  2.8 us
    ppermute x4, waiting for transfers between devices, exchanged(): return lax.ppermute(value, axes, list(enumerate(flip)))  2.47 us
  transfers between devices with their start and end apart: 10, of which 5 were waited for; matrix products, arithmetic and copies ran while one was open for 0% of the time, Pallas kernels for 4%

profile of v8, /device:TPU:32, one launch (start us, length us, event | category | flops | bytes accessed | tf_op | source)
XLA Modules:
  0.0 60.9 jit_solution(15828073250044178761)
XLA Ops:
  0.0 0.0 copy-start
  0.0 0.0 copy-start.2
  0.0 1.2 %x_faces.1 = (f32[3,6,2,256]{3,2,1,0:T(2,128)S(1)}, f32[3,6,2,256]{3,2,1,0:T(2,128)S(1)}) custom-call(f32[3,10,64,256]{3,2,1,0:T(8,128)} %flow.5), custom_call_target="tpu_custom_call" | custom-call | tf_op jit(solution)/shard_map/x_faces/pallas_call | solution.py:239
  1.2 0.1 collective-permute-start
  1.3 2.0 %collective-permute-start.3 = (f32[3,6,2,256]{3,2,1,0:T(2,128)S(1)}, f32[3,6,2,256]{3,2,1,0:T(2,128)S(1)}, u32[]{:S(2)}, u32[]{:S(2)}) collective-permute-start(f32[3,6,2,256]{3,2,1,0:T(2,128)S(1)} %get-tuple-element.30), channel_id=1, source_target_pairs={{0,8},{8,0},{16,24},{24,16},{32,40},{40,32},{48,56},{56,48},{64,72... | collective-permute-start | bytes 110600 | tf_op jit(solution)/shard_map/ppermute | solution.py:27
  3.3 0.0 copy-done
  3.3 0.4 y_faces.1
  3.7 3.9 %collective-permute-start.1 = (f32[80,128]{1,0:T(8,128)S(1)}, f32[80,128]{1,0:T(8,128)S(1)}, u32[]{:S(2)}, u32[]{:S(2)}) collective-permute-start(f32[80,128]{1,0:T(8,128)S(1)} %get-tuple-element.28), channel_id=1, source_target_pairs={{0,7},{1,2},{2,1},{3,4},{4,3},{5,6},{6,5},{7,0},{8,15},{9,10},{10,... | collective-permute-start | bytes 122888 | tf_op jit(solution)/shard_map/ppermute | solution.py:27
  7.6 0.0 copy-start.1
  7.6 0.0 collective-permute-start.2
  7.6 0.0 copy-done.2
  7.6 1.5 %inner.1 = (f32[6,64,256]{2,1,0:T(8,128)S(1)}, f32[6,64,256]{2,1,0:T(8,128)S(1)}, f32[6,64,256]{2,1,0:T(8,128)S(1)}, f32[6,64,256]{2,1,0:T(8,128)S(1)}, f32[6,64...) custom-call(f32[3,10,64,256]{3,2,1,0:T(8,128)S(1)} %copy-done, f32[10,64,256]{2,1,0:T(8,128)S(1)} %copy-done.2), custom_call_target="tpu_custom_call" | custom-call | flops 2500000000 | bytes 5000000 | tf_op jit(solution)/shard_map/inner/pallas_call | solution.py:265
  9.1 0.0 collective-permute-done.refs_8_
  9.1 0.0 collective-permute-done.3.refs_11_
  9.1 0.8 %collective-permute-done.1.refs_9_ = f32[80,128]{1,0:T(8,128)S(1)} collective-permute-done((f32[80,128]{1,0:T(8,128)S(1)}, f32[80,128]{1,0:T(8,128)S(1)}, u32[]{:S(2)}, u32[]{:S(2)}) %collective-permute-start.1) | collective-permute-done | bytes 40992 | tf_op jit(solution)/shard_map/ppermute | solution.py:27
  9.9 1.7 %collective-permute-done.2.refs_10_ = f32[80,128]{1,0:T(8,128)S(1)} collective-permute-done((f32[80,128]{1,0:T(8,128)S(1)}, f32[80,128]{1,0:T(8,128)S(1)}, u32[]{:S(2)}, u32[]{:S(2)}) %collective-permute-start.2) | collective-permute-done | bytes 40992 | tf_op jit(solution)/shard_map/ppermute | solution.py:27
  11.6 0.0 copy-done.1
  11.6 0.7 %field.1 = f32[64,1536]{1,0:T(8,128)S(1)} custom-call(f32[6,64,256]{2,1,0:T(8,128)S(1)} %get-tuple-element.20.refs_0_, f32[6,64,256]{2,1,0:T(8,128)S(1)} %get-tuple-element.21.refs_1_, f32[6,64,256]{2,1,0:T(8,128)S(1)} %get-tuple-element.22.refs_2_, f32[6,64,256]{2,1,0:T(8,128)S(1)} %get-tuple-element.23.refs_3_, ...), custom_call_target="tpu_custom_call" | custom-call | tf_op jit(solution)/shard_map/field/pallas_call | solution.py:275
  12.2 11.0 %all_to_all.15.parts = f32[8,8,1536]{2,1,0:T(8,128)S(1)} all-to-all(f32[8,8,1536]{2,1,0:T(8,128)S(1)} %bitcast.1), channel_id=1, replica_groups=mesh['y_hi'=2,'z'=8,'core'=2,'x'=4,'y_lo'=2] {'x','y_lo'}, dimensions={0} | all-to-all | bytes 786432 | tf_op jit(solution)/shard_map/all_to_all | solution.py:287
  23.2 0.8 %total.1 = (bf16[1,8,1536]{2,1,0:T(8,128)(2,1)S(1)}, bf16[16,8,1536]{2,1,0:T(8,128)(2,1)}) custom-call(f32[8,8,1536]{2,1,0:T(8,128)S(1)} %all_to_all.15.parts), custom_call_target="tpu_custom_call" | custom-call | tf_op jit(solution)/shard_map/total/pallas_call | solution.py:288
  24.0 10.1 %all-to-all-start.1 = ((bf16[16,8,1536]{2,1,0:T(8,128)(2,1)}), bf16[16,8,1536]{2,1,0:T(8,128)(2,1)S(1)}, u32[]{:S(2)}, u32[]{:S(2)}) async-start(bf16[16,8,1536]{2,1,0:T(8,128)(2,1)} %get-tuple-element.32), calls=%async_computation.1 | async-start | bytes 786432 | tf_op jit(solution)/shard_map/all_to_all | solution.py:299
  34.1 1.0 %collective-permute-start.4 = (bf16[1,8,1536]{2,1,0:T(8,128)(2,1)S(1)}, bf16[1,8,1536]{2,1,0:T(8,128)(2,1)S(1)}, u32[]{:S(2)}, u32[]{:S(2)}) collective-permute-start(bf16[1,8,1536]{2,1,0:T(8,128)(2,1)S(1)} %get-tuple-element.31.source), channel_id=1, source_target_pairs={{0,1},{1,0},{2,3},{3,2},{4,5},{5,4},{6,7},{7,6},{8,9},{9,8},{10,11... | collective-permute-start | bytes 73736 | tf_op jit(solution)/shard_map/ppermute | solution.py:32
  35.1 2.8 %collective-permute-done.4 = bf16[1,8,1536]{2,1,0:T(8,128)(2,1)S(1)} collective-permute-done((bf16[1,8,1536]{2,1,0:T(8,128)(2,1)S(1)}, bf16[1,8,1536]{2,1,0:T(8,128)(2,1)S(1)}, u32[]{:S(2)}, u32[]{:S(2)}) %collective-permute-start.4) | collective-permute-done | bytes 24608 | tf_op jit(solution)/shard_map/ppermute | solution.py:32
  37.9 0.5 collective-permute-start.7
  38.4 2.1 %collective-permute-start.6 = (bf16[2,8,1536]{2,1,0:T(8,128)(2,1)S(1)}, bf16[2,8,1536]{2,1,0:T(8,128)(2,1)S(1)}, u32[]{:S(2)}, u32[]{:S(2)}) collective-permute-start(bf16[2,8,1536]{2,1,0:T(8,128)(2,1)S(1)} %pad_maximum_fusion.refs_0_), channel_id=1, source_target_pairs={{0,4},{2,6},{4,0},{6,2},{1,5},{3,7},{5,1},{7,3},{8,12},{10,14},{12... | collective-permute-start | bytes 147464 | tf_op jit(solution)/shard_map/ppermute | solution.py:32
  40.5 1.8 %collective-permute-start.5 = (bf16[2,8,1536]{2,1,0:T(8,128)(2,1)S(1)}, bf16[2,8,1536]{2,1,0:T(8,128)(2,1)S(1)}, u32[]{:S(2)}, u32[]{:S(2)}) collective-permute-start(bf16[2,8,1536]{2,1,0:T(8,128)(2,1)S(1)} %pad_maximum_fusion.refs_0_), channel_id=1, source_target_pairs={{0,6},{2,0},{4,2},{6,4},{1,7},{3,1},{5,3},{7,5},{8,14},{10,8},{12,... | collective-permute-start | bytes 147464 | tf_op jit(solution)/shard_map/ppermute | solution.py:32
  42.3 2.8 %all-to-all-done.1.refs_4_ = bf16[16,8,1536]{2,1,0:T(8,128)(2,1)S(1)} async-done(((bf16[16,8,1536]{2,1,0:T(8,128)(2,1)}), bf16[16,8,1536]{2,1,0:T(8,128)(2,1)S(1)}, u32[]{:S(2)}, u32[]{:S(2)}) %all-to-all-start.1) | async-done | bytes 393248 | tf_op jit(solution)/shard_map/all_to_all | solution.py:299
  45.1 0.0 collective-permute-start.8
  45.1 0.0 collective-permute-done.7.refs_3_
  45.1 0.0 collective-permute-done.6.refs_2_
  45.1 0.0 collective-permute-done.5.refs_1_
  45.1 0.3 arrange.1
  45.5 1.3 %collective-permute-done.8.refs_2_ = bf16[16,8,1536]{2,1,0:T(8,128)(2,1)S(1)} collective-permute-done((bf16[16,8,1536]{2,1,0:T(8,128)(2,1)S(1)}, bf16[16,8,1536]{2,1,0:T(8,128)(2,1)S(1)}, u32[]{:S(2)}, u32[]{:S(2)}) %collective-permute-start.8) | collective-permute-done | bytes 393248 | tf_op jit(solution)/shard_map/ppermute | solution.py:32
  46.8 0.3 block.1
  47.1 12.8 %all_to_all.16.refs_0_ = f32[8,128,128]{2,1,0:T(8,128)S(1)} all-to-all(f32[8,128,128]{2,1,0:T(8,128)S(1)} %block.1), channel_id=1, replica_groups=mesh['y_hi'=2,'z'=8,'core'=2,'x'=4,'y_lo'=2] {'x','y_lo'}, dimensions={0} | all-to-all | bytes 1048576 | tf_op jit(solution)/shard_map/all_to_all | solution.py:334
  59.9 1.0 %place.1 = f32[64,2048]{1,0:T(8,128)} custom-call(f32[8,128,128]{2,1,0:T(8,128)S(1)} %all_to_all.16.refs_0_), custom_call_target="tpu_custom_call" | custom-call | tf_op jit(solution)/shard_map/place/pallas_call | solution.py:335
  (2 shorter events, 0.0 us)
Async XLA Ops:
  0.0 3.3 %copy-start = (f32[3,10,64,256]{3,2,1,0:T(8,128)S(1)}, f32[3,10,64,256]{3,2,1,0:T(8,128)}, u32[]{:S(2)}) copy-start(f32[3,10,64,256]{3,2,1,0:T(8,128)} %flow.5) | copy-start | bytes 5898244
  0.0 7.6 %copy-start.2 = (f32[10,64,256]{2,1,0:T(8,128)S(1)}, f32[10,64,256]{2,1,0:T(8,128)}, u32[]{:S(2)}) copy-start(f32[10,64,256]{2,1,0:T(8,128)} %thermal.1) | copy-start | bytes 1966084
  1.2 7.9 %collective-permute-start = (f32[3,6,2,256]{3,2,1,0:T(2,128)S(1)}, f32[3,6,2,256]{3,2,1,0:T(2,128)S(1)}, u32[]{:S(2)}, u32[]{:S(2)}) collective-permute-start(f32[3,6,2,256]{3,2,1,0:T(2,128)S(1)} %get-tuple-element.27), channel_id=1, source_target_pairs={{0,248},{8,16},{16,8},{24,32},{32,24},{40,48},{48,40},{56,64},{64,... | collective-permute-start | bytes 110600 | tf_op jit(solution)/shard_map/ppermute | solution.py:27
  1.3 7.8 %collective-permute-start.3 = (f32[3,6,2,256]{3,2,1,0:T(2,128)S(1)}, f32[3,6,2,256]{3,2,1,0:T(2,128)S(1)}, u32[]{:S(2)}, u32[]{:S(2)}) collective-permute-start(f32[3,6,2,256]{3,2,1,0:T(2,128)S(1)} %get-tuple-element.30), channel_id=1, source_target_pairs={{0,8},{8,0},{16,24},{24,16},{32,40},{40,32},{48,56},{56,48},{64,72... | collective-permute-start | bytes 110600 | tf_op jit(solution)/shard_map/ppermute | solution.py:27
  3.7 6.2 %collective-permute-start.1 = (f32[80,128]{1,0:T(8,128)S(1)}, f32[80,128]{1,0:T(8,128)S(1)}, u32[]{:S(2)}, u32[]{:S(2)}) collective-permute-start(f32[80,128]{1,0:T(8,128)S(1)} %get-tuple-element.28), channel_id=1, source_target_pairs={{0,7},{1,2},{2,1},{3,4},{4,3},{5,6},{6,5},{7,0},{8,15},{9,10},{10,... | collective-permute-start | bytes 122888 | tf_op jit(solution)/shard_map/ppermute | solution.py:27
  7.6 4.0 %copy-start.1 = (bf16[256,256]{1,0:T(8,128)(2,1)S(1)}, bf16[256,256]{1,0:T(8,128)(2,1)}, u32[]{:S(2)}) copy-start(bf16[256,256]{1,0:T(8,128)(2,1)} %refs_7_.1) | copy-start | bytes 393220
  7.6 4.0 %collective-permute-start.2 = (f32[80,128]{1,0:T(8,128)S(1)}, f32[80,128]{1,0:T(8,128)S(1)}, u32[]{:S(2)}, u32[]{:S(2)}) collective-permute-start(f32[80,128]{1,0:T(8,128)S(1)} %get-tuple-element.29), channel_id=1, source_target_pairs={{0,1},{1,0},{2,3},{3,2},{4,5},{5,4},{6,7},{7,6},{8,9},{9,8},{10,11... | collective-permute-start | bytes 122888 | tf_op jit(solution)/shard_map/ppermute | solution.py:27
  24.0 21.1 %all-to-all-start.1 = ((bf16[16,8,1536]{2,1,0:T(8,128)(2,1)}), bf16[16,8,1536]{2,1,0:T(8,128)(2,1)S(1)}, u32[]{:S(2)}, u32[]{:S(2)}) async-start(bf16[16,8,1536]{2,1,0:T(8,128)(2,1)} %get-tuple-element.32), calls=%async_computation.1 | async-start | bytes 786432 | tf_op jit(solution)/shard_map/all_to_all | solution.py:299
  34.1 3.8 %collective-permute-start.4 = (bf16[1,8,1536]{2,1,0:T(8,128)(2,1)S(1)}, bf16[1,8,1536]{2,1,0:T(8,128)(2,1)S(1)}, u32[]{:S(2)}, u32[]{:S(2)}) collective-permute-start(bf16[1,8,1536]{2,1,0:T(8,128)(2,1)S(1)} %get-tuple-element.31.source), channel_id=1, source_target_pairs={{0,1},{1,0},{2,3},{3,2},{4,5},{5,4},{6,7},{7,6},{8,9},{9,8},{10,11... | collective-permute-start | bytes 73736 | tf_op jit(solution)/shard_map/ppermute | solution.py:32
  37.9 7.2 %collective-permute-start.7 = (bf16[2,8,1536]{2,1,0:T(8,128)(2,1)S(1)}, bf16[2,8,1536]{2,1,0:T(8,128)(2,1)S(1)}, u32[]{:S(2)}, u32[]{:S(2)}) collective-permute-start(bf16[2,8,1536]{2,1,0:T(8,128)(2,1)S(1)} %pad_maximum_fusion.refs_0_), channel_id=1, source_target_pairs={{0,2},{2,4},{4,6},{6,0},{1,3},{3,5},{5,7},{7,1},{8,10},{10,12},{12... | collective-permute-start | bytes 147464 | tf_op jit(solution)/shard_map/ppermute | solution.py:32
  38.4 6.7 %collective-permute-start.6 = (bf16[2,8,1536]{2,1,0:T(8,128)(2,1)S(1)}, bf16[2,8,1536]{2,1,0:T(8,128)(2,1)S(1)}, u32[]{:S(2)}, u32[]{:S(2)}) collective-permute-start(bf16[2,8,1536]{2,1,0:T(8,128)(2,1)S(1)} %pad_maximum_fusion.refs_0_), channel_id=1, source_target_pairs={{0,4},{2,6},{4,0},{6,2},{1,5},{3,7},{5,1},{7,3},{8,12},{10,14},{12... | collective-permute-start | bytes 147464 | tf_op jit(solution)/shard_map/ppermute | solution.py:32
  40.5 4.6 %collective-permute-start.5 = (bf16[2,8,1536]{2,1,0:T(8,128)(2,1)S(1)}, bf16[2,8,1536]{2,1,0:T(8,128)(2,1)S(1)}, u32[]{:S(2)}, u32[]{:S(2)}) collective-permute-start(bf16[2,8,1536]{2,1,0:T(8,128)(2,1)S(1)} %pad_maximum_fusion.refs_0_), channel_id=1, source_target_pairs={{0,6},{2,0},{4,2},{6,4},{1,7},{3,1},{5,3},{7,5},{8,14},{10,8},{12,... | collective-permute-start | bytes 147464 | tf_op jit(solution)/shard_map/ppermute | solution.py:32
  45.1 1.7 %collective-permute-start.8 = (bf16[16,8,1536]{2,1,0:T(8,128)(2,1)S(1)}, bf16[16,8,1536]{2,1,0:T(8,128)(2,1)S(1)}, u32[]{:S(2)}, u32[]{:S(2)}) collective-permute-start(bf16[16,8,1536]{2,1,0:T(8,128)(2,1)S(1)} %all-to-all-done.1.refs_4_), channel_id=1, source_target_pairs={{0,8},{8,0},{1,9},{9,1},{2,10},{10,2},{3,11},{11,3},{4,12},{12,4},... | collective-permute-start | bytes 1179656 | tf_op jit(solution)/shard_map/ppermute | solution.py:32

commit v9 on v8

--- a/solution.py
+++ b/solution.py
@@ -7,6 +7,7 @@
 from jax.sharding import PartitionSpec as P
 
 VMEM = pl.BlockSpec(memory_space=pltpu.VMEM)
+ANY = pl.BlockSpec(memory_space=pl.ANY)
 FAR = ("y_hi", "z")
 EAST = ("y_hi", "z", "core")
 NORTH = ("x", "y_lo")
@@ -32,33 +33,32 @@
     return lax.ppermute(value, axes, [(k, (k + step) % count) for k in range(count)])
 
 
-def x_faces_kernel(flow, x_inner, x_outer, top, bottom, sems):
-    planes, rows = x_inner.shape[1], flow.shape[2]
-    middle = slice(2, planes + 2)
-    copies = [
-        pltpu.make_async_copy(flow.at[:, middle, 0:8], top, sems.at[0]),
-        pltpu.make_async_copy(flow.at[:, middle, rows - 8 : rows], bottom, sems.at[1]),
-    ]
-    for copy in copies:
-        copy.start()
-    for copy in copies:
-        copy.wait()
+def x_faces_kernel(flow, x_outer, rows_held, sem):
+    planes, rows = x_outer.shape[1], flow.shape[2]
     x_even = lax.axis_index("core") == 0
+    start = pl.multiple_of(jnp.where(x_even, 0, rows - 8), 8)
+    copy = pltpu.make_async_copy(
+        flow.at[:, pl.ds(2, planes), pl.ds(start, 8)], rows_held, sem
+    )
+    copy.start()
+    copy.wait()
     for comp in range(3):
         for plane in range(planes):
-            first, last = top[comp, plane, 0:2], bottom[comp, plane, 6:8]
-            x_inner[comp, plane] = jnp.where(x_even, last, first)
-            x_outer[comp, plane] = jnp.where(x_even, first, last)
-
-
-def y_faces_kernel(flow, y_inner, y_outer):
+            held = rows_held[comp, plane]
+            x_outer[comp, plane] = jnp.where(x_even, held[0:2], held[6:8])
+
+
+def other_faces_kernel(flow, x_inner, y_inner, y_outer):
     planes, rows, width = flow.shape[1] - 4, flow.shape[2], flow.shape[3]
-    y_even = lax.axis_index("y_lo") == 0
+    x_even, y_even = lax.axis_index("core") == 0, lax.axis_index("y_lo") == 0
     lane = lax.broadcasted_iota(jnp.int32, (rows, 128), 1)
     first = jnp.zeros((rows, 128), jnp.float32)
     last = jnp.zeros((rows, 128), jnp.float32)
     for comp in range(3):
         for plane in range(planes):
+            top = flow[comp, plane + 2, 0:2]
+            bottom = flow[comp, plane + 2, rows - 2 : rows]
+            x_inner[comp, plane, 0:2] = jnp.where(x_even, bottom, top)
             at = 2 * (comp * planes + plane)
             here = (lane == at) | (lane == at + 1)
             low = flow[comp, plane + 2, :, 0:128]
@@ -128,7 +128,7 @@
     blank = jnp.zeros((6, width), jnp.float32)
 
     def with_x(value, comp, plane):
-        inner, outer = x_inner[comp, plane], x_outer[comp, plane]
+        inner, outer = x_inner[comp, plane, 0:2], x_outer[comp, plane]
         low = jnp.where(x_even, outer, inner)
         high = jnp.where(x_even, inner, outer)
         head = jnp.concatenate([low[0:1] - 8.0 * low[1:2], low[1:2], blank], axis=0)
@@ -236,27 +236,24 @@
     f32 = jnp.float32
     x_face = jax.ShapeDtypeStruct((3, planes, 2, width), f32)
     y_face = jax.ShapeDtypeStruct((rows + 16, 128), f32)
-    x_inner, x_outer = pl.pallas_call(
+    x_long = jax.ShapeDtypeStruct((3, planes, 2, width), f32)
+    x_outer = pl.pallas_call(
         x_faces_kernel,
-        out_shape=(x_face, x_face),
-        in_specs=[pl.BlockSpec(memory_space=pltpu.HBM)],
-        out_specs=(VMEM, VMEM),
-        scratch_shapes=[
-            pltpu.VMEM((3, planes, 8, width), f32),
-            pltpu.VMEM((3, planes, 8, width), f32),
-            pltpu.SemaphoreType.DMA((2,)),
-        ],
+        out_shape=x_face,
+        in_specs=[ANY],
+        out_specs=VMEM,
+        scratch_shapes=[pltpu.VMEM((3, planes, 8, width), f32), pltpu.SemaphoreType.DMA],
         compiler_params=params(),
         name="x_faces",
     )(pltpu.with_memory_space_constraint(flow, pltpu.HBM))
-    y_inner, y_outer = pl.pallas_call(
-        y_faces_kernel,
-        out_shape=(y_face, y_face),
+    x_inner, y_inner, y_outer = pl.pallas_call(
+        other_faces_kernel,
+        out_shape=(x_long, y_face, y_face),
         in_specs=[VMEM],
-        out_specs=(VMEM, VMEM),
+        out_specs=(VMEM,) * 3,
         compiler_params=params(),
         cost_estimate=pl.CostEstimate(flops=500_000_000, bytes_accessed=1_000_000, transcendentals=0),
-        name="y_faces",
+        name="other_faces",
     )(flow)
     x_outer = exchanged(x_outer, EAST, True)
     y_outer = exchanged(y_outer, NORTH, True)

time: 61.2 us -> 61.1 us (level)
  no operation moved by 1% of the time
where the time goes in v9:
time: 61.1 us; the launch traced here: 60.8 us
  blocking collectives  23.8 us (39%)
  starting transfers between devices  20.8 us (34%)
  waiting for transfers between devices  9.62 us (16%)
  Pallas kernels  6.05 us (10%)
    all_to_all x1, blocking collectives, body(): blocks = lax.all_to_all(block, NORTH, 0, 0)  12.7 us
    all_to_all x1, blocking collectives, body(): gathered = lax.all_to_all(partial.reshape(north, piece, depth), NORTH, 0, 0)  11.1 us
    all_to_all x1, starting transfers between devices, body(): right = lax.all_to_all(to_far, FAR, 0, 0, axis_index_groups=[list(ORDER)])  10.1 us
    ppermute x4, starting transfers between devices, exchanged(): return lax.ppermute(value, axes, list(enumerate(flip)))  5.56 us
    ppermute x5, starting transfers between devices, shifted(): lax.ppermute(value, axes, [(k, (k + step) % count) for k in range(count)])  5.13 us
    ppermute x5, waiting for transfers between devices, shifted(): lax.ppermute(value, axes, [(k, (k + step) % count) for k in range(count)])  4.33 us
    all_to_all x1, waiting for transfers between devices, body(): right = lax.all_to_all(to_far, FAR, 0, 0, axis_index_groups=[list(ORDER)])  2.82 us
    ppermute x4, waiting for transfers between devices, exchanged(): return lax.ppermute(value, axes, list(enumerate(flip)))  2.47 us
  transfers between devices with their start and end apart: 10, of which 5 were waited for; matrix products, arithmetic and copies ran while one was open for 0% of the time, Pallas kernels for 4%

profile of v9, /device:TPU:32, one launch (start us, length us, event | category | flops | bytes accessed | tf_op | source)
XLA Modules:
  0.0 60.8 jit_solution(5450440247497679278)
XLA Ops:
  0.0 0.0 copy-start
  0.0 0.0 copy-start.2
  0.0 1.1 %x_faces.1 = f32[3,6,2,256]{3,2,1,0:T(2,128)S(1)} custom-call(f32[3,10,64,256]{3,2,1,0:T(8,128)} %flow.5), custom_call_target="tpu_custom_call" | custom-call | tf_op jit(solution)/shard_map/x_faces/pallas_call | solution.py:240
  1.1 0.1 collective-permute-start
  1.2 0.4 copy-done
  1.6 0.4 other_faces.1
  2.0 1.7 %collective-permute-start.3 = (f32[3,6,2,256]{3,2,1,0:T(2,128)S(1)}, f32[3,6,2,256]{3,2,1,0:T(2,128)S(1)}, u32[]{:S(2)}, u32[]{:S(2)}) collective-permute-start(f32[3,6,2,256]{3,2,1,0:T(2,128)S(1)} %get-tuple-element.28), channel_id=1, source_target_pairs={{0,8},{8,0},{16,24},{24,16},{32,40},{40,32},{48,56},{56,48},{64,72... | collective-permute-start | bytes 110600 | tf_op jit(solution)/shard_map/ppermute | solution.py:28
  3.7 3.8 %collective-permute-start.1 = (f32[80,128]{1,0:T(8,128)S(1)}, f32[80,128]{1,0:T(8,128)S(1)}, u32[]{:S(2)}, u32[]{:S(2)}) collective-permute-start(f32[80,128]{1,0:T(8,128)S(1)} %get-tuple-element.26), channel_id=1, source_target_pairs={{0,7},{1,2},{2,1},{3,4},{4,3},{5,6},{6,5},{7,0},{8,15},{9,10},{10,... | collective-permute-start | bytes 122888 | tf_op jit(solution)/shard_map/ppermute | solution.py:28
  7.4 0.0 copy-start.1
  7.4 0.0 collective-permute-start.2
  7.5 0.0 copy-done.2
  7.5 1.5 %inner.1 = (f32[6,64,256]{2,1,0:T(8,128)S(1)}, f32[6,64,256]{2,1,0:T(8,128)S(1)}, f32[6,64,256]{2,1,0:T(8,128)S(1)}, f32[6,64,256]{2,1,0:T(8,128)S(1)}, f32[6,64...) custom-call(f32[3,10,64,256]{3,2,1,0:T(8,128)S(1)} %copy-done, f32[10,64,256]{2,1,0:T(8,128)S(1)} %copy-done.2), custom_call_target="tpu_custom_call" | custom-call | flops 2500000000 | bytes 5000000 | tf_op jit(solution)/shard_map/inner/pallas_call | solution.py:262
  9.0 0.0 collective-permute-done.refs_8_
  9.0 0.0 collective-permute-done.3.refs_11_
  9.0 0.8 %collective-permute-done.1.refs_9_ = f32[80,128]{1,0:T(8,128)S(1)} collective-permute-done((f32[80,128]{1,0:T(8,128)S(1)}, f32[80,128]{1,0:T(8,128)S(1)}, u32[]{:S(2)}, u32[]{:S(2)}) %collective-permute-start.1) | collective-permute-done | bytes 40992 | tf_op jit(solution)/shard_map/ppermute | solution.py:28
  9.8 1.7 %collective-permute-done.2.refs_10_ = f32[80,128]{1,0:T(8,128)S(1)} collective-permute-done((f32[80,128]{1,0:T(8,128)S(1)}, f32[80,128]{1,0:T(8,128)S(1)}, u32[]{:S(2)}, u32[]{:S(2)}) %collective-permute-start.2) | collective-permute-done | bytes 40992 | tf_op jit(solution)/shard_map/ppermute | solution.py:28
  11.5 0.0 copy-done.1
  11.5 0.7 %field.1 = f32[64,1536]{1,0:T(8,128)S(1)} custom-call(f32[6,64,256]{2,1,0:T(8,128)S(1)} %get-tuple-element.19.refs_0_, f32[6,64,256]{2,1,0:T(8,128)S(1)} %get-tuple-element.20.refs_1_, f32[6,64,256]{2,1,0:T(8,128)S(1)} %get-tuple-element.21.refs_2_, f32[6,64,256]{2,1,0:T(8,128)S(1)} %get-tuple-element.22.refs_3_, ...), custom_call_target="tpu_custom_call" | custom-call | tf_op jit(solution)/shard_map/field/pallas_call | solution.py:272
  12.1 11.1 %all_to_all.15.parts = f32[8,8,1536]{2,1,0:T(8,128)S(1)} all-to-all(f32[8,8,1536]{2,1,0:T(8,128)S(1)} %bitcast.1), channel_id=1, replica_groups=mesh['y_hi'=2,'z'=8,'core'=2,'x'=4,'y_lo'=2] {'x','y_lo'}, dimensions={0} | all-to-all | bytes 786432 | tf_op jit(solution)/shard_map/all_to_all | solution.py:284
  23.2 0.8 %total.1 = (bf16[1,8,1536]{2,1,0:T(8,128)(2,1)S(1)}, bf16[16,8,1536]{2,1,0:T(8,128)(2,1)}) custom-call(f32[8,8,1536]{2,1,0:T(8,128)S(1)} %all_to_all.15.parts), custom_call_target="tpu_custom_call" | custom-call | tf_op jit(solution)/shard_map/total/pallas_call | solution.py:285
  24.0 10.1 %all-to-all-start.1 = ((bf16[16,8,1536]{2,1,0:T(8,128)(2,1)}), bf16[16,8,1536]{2,1,0:T(8,128)(2,1)S(1)}, u32[]{:S(2)}, u32[]{:S(2)}) async-start(bf16[16,8,1536]{2,1,0:T(8,128)(2,1)} %get-tuple-element.30), calls=%async_computation.1 | async-start | bytes 786432 | tf_op jit(solution)/shard_map/all_to_all | solution.py:296
  34.1 0.9 %collective-permute-start.4 = (bf16[1,8,1536]{2,1,0:T(8,128)(2,1)S(1)}, bf16[1,8,1536]{2,1,0:T(8,128)(2,1)S(1)}, u32[]{:S(2)}, u32[]{:S(2)}) collective-permute-start(bf16[1,8,1536]{2,1,0:T(8,128)(2,1)S(1)} %get-tuple-element.29.source), channel_id=1, source_target_pairs={{0,1},{1,0},{2,3},{3,2},{4,5},{5,4},{6,7},{7,6},{8,9},{9,8},{10,11... | collective-permute-start | bytes 73736 | tf_op jit(solution)/shard_map/ppermute | solution.py:33
  35.0 3.0 %collective-permute-done.4 = bf16[1,8,1536]{2,1,0:T(8,128)(2,1)S(1)} collective-permute-done((bf16[1,8,1536]{2,1,0:T(8,128)(2,1)S(1)}, bf16[1,8,1536]{2,1,0:T(8,128)(2,1)S(1)}, u32[]{:S(2)}, u32[]{:S(2)}) %collective-permute-start.4) | collective-permute-done | bytes 24608 | tf_op jit(solution)/shard_map/ppermute | solution.py:33
  38.0 0.4 collective-permute-start.7
  38.3 2.1 %collective-permute-start.6 = (bf16[2,8,1536]{2,1,0:T(8,128)(2,1)S(1)}, bf16[2,8,1536]{2,1,0:T(8,128)(2,1)S(1)}, u32[]{:S(2)}, u32[]{:S(2)}) collective-permute-start(bf16[2,8,1536]{2,1,0:T(8,128)(2,1)S(1)} %pad_maximum_fusion.refs_0_), channel_id=1, source_target_pairs={{0,4},{2,6},{4,0},{6,2},{1,5},{3,7},{5,1},{7,3},{8,12},{10,14},{12... | collective-permute-start | bytes 147464 | tf_op jit(solution)/shard_map/ppermute | solution.py:33
  40.4 1.8 %collective-permute-start.5 = (bf16[2,8,1536]{2,1,0:T(8,128)(2,1)S(1)}, bf16[2,8,1536]{2,1,0:T(8,128)(2,1)S(1)}, u32[]{:S(2)}, u32[]{:S(2)}) collective-permute-start(bf16[2,8,1536]{2,1,0:T(8,128)(2,1)S(1)} %pad_maximum_fusion.refs_0_), channel_id=1, source_target_pairs={{0,6},{2,0},{4,2},{6,4},{1,7},{3,1},{5,3},{7,5},{8,14},{10,8},{12,... | collective-permute-start | bytes 147464 | tf_op jit(solution)/shard_map/ppermute | solution.py:33
  42.2 2.8 %all-to-all-done.1.refs_4_ = bf16[16,8,1536]{2,1,0:T(8,128)(2,1)S(1)} async-done(((bf16[16,8,1536]{2,1,0:T(8,128)(2,1)}), bf16[16,8,1536]{2,1,0:T(8,128)(2,1)S(1)}, u32[]{:S(2)}, u32[]{:S(2)}) %all-to-all-start.1) | async-done | bytes 393248 | tf_op jit(solution)/shard_map/all_to_all | solution.py:296
  45.0 0.0 collective-permute-start.8
  45.0 0.0 collective-permute-done.7.refs_3_
  45.0 0.0 collective-permute-done.6.refs_2_
  45.0 0.0 collective-permute-done.5.refs_1_
  45.0 0.3 arrange.1
  45.4 1.4 %collective-permute-done.8.refs_2_ = bf16[16,8,1536]{2,1,0:T(8,128)(2,1)S(1)} collective-permute-done((bf16[16,8,1536]{2,1,0:T(8,128)(2,1)S(1)}, bf16[16,8,1536]{2,1,0:T(8,128)(2,1)S(1)}, u32[]{:S(2)}, u32[]{:S(2)}) %collective-permute-start.8) | collective-permute-done | bytes 393248 | tf_op jit(solution)/shard_map/ppermute | solution.py:33
  46.7 0.3 block.1
  47.1 12.7 %all_to_all.16.refs_0_ = f32[8,128,128]{2,1,0:T(8,128)S(1)} all-to-all(f32[8,128,128]{2,1,0:T(8,128)S(1)} %block.1), channel_id=1, replica_groups=mesh['y_hi'=2,'z'=8,'core'=2,'x'=4,'y_lo'=2] {'x','y_lo'}, dimensions={0} | all-to-all | bytes 1048576 | tf_op jit(solution)/shard_map/all_to_all | solution.py:331
  59.8 1.0 %place.1 = f32[64,2048]{1,0:T(8,128)} custom-call(f32[8,128,128]{2,1,0:T(8,128)S(1)} %all_to_all.16.refs_0_), custom_call_target="tpu_custom_call" | custom-call | tf_op jit(solution)/shard_map/place/pallas_call | solution.py:332
  (2 shorter events, 0.0 us)
Async XLA Ops:
  0.0 1.6 %copy-start = (f32[3,10,64,256]{3,2,1,0:T(8,128)S(1)}, f32[3,10,64,256]{3,2,1,0:T(8,128)}, u32[]{:S(2)}) copy-start(f32[3,10,64,256]{3,2,1,0:T(8,128)} %flow.5) | copy-start | bytes 5898244
  0.0 7.5 %copy-start.2 = (f32[10,64,256]{2,1,0:T(8,128)S(1)}, f32[10,64,256]{2,1,0:T(8,128)}, u32[]{:S(2)}) copy-start(f32[10,64,256]{2,1,0:T(8,128)} %thermal.1) | copy-start | bytes 1966084
  1.1 7.9 %collective-permute-start = (f32[3,6,2,256]{3,2,1,0:T(2,128)S(1)}, f32[3,6,2,256]{3,2,1,0:T(2,128)S(1)}, u32[]{:S(2)}, u32[]{:S(2)}) collective-permute-start(f32[3,6,2,256]{3,2,1,0:T(2,128)S(1)} %x_faces.1), channel_id=1, source_target_pairs={{0,248},{8,16},{16,8},{24,32},{32,24},{40,48},{48,40},{56,64},{64,... | collective-permute-start | bytes 110600 | tf_op jit(solution)/shard_map/ppermute | solution.py:28
  2.0 7.0 %collective-permute-start.3 = (f32[3,6,2,256]{3,2,1,0:T(2,128)S(1)}, f32[3,6,2,256]{3,2,1,0:T(2,128)S(1)}, u32[]{:S(2)}, u32[]{:S(2)}) collective-permute-start(f32[3,6,2,256]{3,2,1,0:T(2,128)S(1)} %get-tuple-element.28), channel_id=1, source_target_pairs={{0,8},{8,0},{16,24},{24,16},{32,40},{40,32},{48,56},{56,48},{64,72... | collective-permute-start | bytes 110600 | tf_op jit(solution)/shard_map/ppermute | solution.py:28
  3.7 6.1 %collective-permute-start.1 = (f32[80,128]{1,0:T(8,128)S(1)}, f32[80,128]{1,0:T(8,128)S(1)}, u32[]{:S(2)}, u32[]{:S(2)}) collective-permute-start(f32[80,128]{1,0:T(8,128)S(1)} %get-tuple-element.26), channel_id=1, source_target_pairs={{0,7},{1,2},{2,1},{3,4},{4,3},{5,6},{6,5},{7,0},{8,15},{9,10},{10,... | collective-permute-start | bytes 122888 | tf_op jit(solution)/shard_map/ppermute | solution.py:28
  7.4 4.0 %copy-start.1 = (bf16[256,256]{1,0:T(8,128)(2,1)S(1)}, bf16[256,256]{1,0:T(8,128)(2,1)}, u32[]{:S(2)}) copy-start(bf16[256,256]{1,0:T(8,128)(2,1)} %refs_7_.1) | copy-start | bytes 393220
  7.4 4.0 %collective-permute-start.2 = (f32[80,128]{1,0:T(8,128)S(1)}, f32[80,128]{1,0:T(8,128)S(1)}, u32[]{:S(2)}, u32[]{:S(2)}) collective-permute-start(f32[80,128]{1,0:T(8,128)S(1)} %get-tuple-element.27), channel_id=1, source_target_pairs={{0,1},{1,0},{2,3},{3,2},{4,5},{5,4},{6,7},{7,6},{8,9},{9,8},{10,11... | collective-permute-start | bytes 122888 | tf_op jit(solution)/shard_map/ppermute | solution.py:28
  24.0 21.0 %all-to-all-start.1 = ((bf16[16,8,1536]{2,1,0:T(8,128)(2,1)}), bf16[16,8,1536]{2,1,0:T(8,128)(2,1)S(1)}, u32[]{:S(2)}, u32[]{:S(2)}) async-start(bf16[16,8,1536]{2,1,0:T(8,128)(2,1)} %get-tuple-element.30), calls=%async_computation.1 | async-start | bytes 786432 | tf_op jit(solution)/shard_map/all_to_all | solution.py:296
  34.1 3.9 %collective-permute-start.4 = (bf16[1,8,1536]{2,1,0:T(8,128)(2,1)S(1)}, bf16[1,8,1536]{2,1,0:T(8,128)(2,1)S(1)}, u32[]{:S(2)}, u32[]{:S(2)}) collective-permute-start(bf16[1,8,1536]{2,1,0:T(8,128)(2,1)S(1)} %get-tuple-element.29.source), channel_id=1, source_target_pairs={{0,1},{1,0},{2,3},{3,2},{4,5},{5,4},{6,7},{7,6},{8,9},{9,8},{10,11... | collective-permute-start | bytes 73736 | tf_op jit(solution)/shard_map/ppermute | solution.py:33
  38.0 7.0 %collective-permute-start.7 = (bf16[2,8,1536]{2,1,0:T(8,128)(2,1)S(1)}, bf16[2,8,1536]{2,1,0:T(8,128)(2,1)S(1)}, u32[]{:S(2)}, u32[]{:S(2)}) collective-permute-start(bf16[2,8,1536]{2,1,0:T(8,128)(2,1)S(1)} %pad_maximum_fusion.refs_0_), channel_id=1, source_target_pairs={{0,2},{2,4},{4,6},{6,0},{1,3},{3,5},{5,7},{7,1},{8,10},{10,12},{12... | collective-permute-start | bytes 147464 | tf_op jit(solution)/shard_map/ppermute | solution.py:33
  38.3 6.7 %collective-permute-start.6 = (bf16[2,8,1536]{2,1,0:T(8,128)(2,1)S(1)}, bf16[2,8,1536]{2,1,0:T(8,128)(2,1)S(1)}, u32[]{:S(2)}, u32[]{:S(2)}) collective-permute-start(bf16[2,8,1536]{2,1,0:T(8,128)(2,1)S(1)} %pad_maximum_fusion.refs_0_), channel_id=1, source_target_pairs={{0,4},{2,6},{4,0},{6,2},{1,5},{3,7},{5,1},{7,3},{8,12},{10,14},{12... | collective-permute-start | bytes 147464 | tf_op jit(solution)/shard_map/ppermute | solution.py:33
  40.4 4.6 %collective-permute-start.5 = (bf16[2,8,1536]{2,1,0:T(8,128)(2,1)S(1)}, bf16[2,8,1536]{2,1,0:T(8,128)(2,1)S(1)}, u32[]{:S(2)}, u32[]{:S(2)}) collective-permute-start(bf16[2,8,1536]{2,1,0:T(8,128)(2,1)S(1)} %pad_maximum_fusion.refs_0_), channel_id=1, source_target_pairs={{0,6},{2,0},{4,2},{6,4},{1,7},{3,1},{5,3},{7,5},{8,14},{10,8},{12,... | collective-permute-start | bytes 147464 | tf_op jit(solution)/shard_map/ppermute | solution.py:33
  45.0 1.7 %collective-permute-start.8 = (bf16[16,8,1536]{2,1,0:T(8,128)(2,1)S(1)}, bf16[16,8,1536]{2,1,0:T(8,128)(2,1)S(1)}, u32[]{:S(2)}, u32[]{:S(2)}) collective-permute-start(bf16[16,8,1536]{2,1,0:T(8,128)(2,1)S(1)} %all-to-all-done.1.refs_4_), channel_id=1, source_target_pairs={{0,8},{8,0},{1,9},{9,1},{2,10},{10,2},{3,11},{11,3},{4,12},{12,4},... | collective-permute-start | bytes 1179656 | tf_op jit(solution)/shard_map/ppermute | solution.py:33

commit v10 on v9

--- a/solution.py
+++ b/solution.py
@@ -197,7 +197,7 @@
 def arrange_kernel(scale, *refs):
     pairs, own, left, share = refs[:4], refs[4], refs[5], refs[6]
     x, y_lo = lax.axis_index("x"), lax.axis_index("y_lo")
-    for step, pair in enumerate(pairs):
+    for step, pair in zip((0, 1, 3, 2), pairs):
         at = 2 * lax.rem(x + step, 4)
         left[at + y_lo] = pair[0]
         left[at + 1 - y_lo] = pair[1]
@@ -305,7 +305,7 @@
         name="own",
     )(own)
     pair = jnp.concatenate([own, beside])
-    pairs = [pair] + [shifted(pair, "x", -step) for step in range(1, 4)]
+    pairs = [pair] + [shifted(pair, "x", -step) for step in (1, 3, 2)]
     scale = 1.0 / depth
     left, share = pl.pallas_call(
         lambda *refs: arrange_kernel(scale, *refs),

time: 61.1 us -> 61.1 us (level)
  no operation moved by 1% of the time
where the time goes in v10:
time: 61.1 us; the launch traced here: 60.8 us
  blocking collectives  23.8 us (39%)
  starting transfers between devices  21.4 us (35%)
  waiting for transfers between devices  9.01 us (15%)
  Pallas kernels  6.05 us (10%)
    all_to_all x1, blocking collectives, body(): blocks = lax.all_to_all(block, NORTH, 0, 0)  12.7 us
    all_to_all x1, blocking collectives, body(): gathered = lax.all_to_all(partial.reshape(north, piece, depth), NORTH, 0, 0)  11.1 us
    all_to_all x1, starting transfers between devices, body(): right = lax.all_to_all(to_far, FAR, 0, 0, axis_index_groups=[list(ORDER)])  10.1 us
    ppermute x5, starting transfers between devices, shifted(): lax.ppermute(value, axes, [(k, (k + step) % count) for k in range(count)])  5.73 us
    ppermute x4, starting transfers between devices, exchanged(): return lax.ppermute(value, axes, list(enumerate(flip)))  5.56 us
    ppermute x5, waiting for transfers between devices, shifted(): lax.ppermute(value, axes, [(k, (k + step) % count) for k in range(count)])  4.33 us
    ppermute x4, waiting for transfers between devices, exchanged(): return lax.ppermute(value, axes, list(enumerate(flip)))  2.47 us
    all_to_all x1, waiting for transfers between devices, body(): right = lax.all_to_all(to_far, FAR, 0, 0, axis_index_groups=[list(ORDER)])  2.21 us
  transfers between devices with their start and end apart: 10, of which 5 were waited for; matrix products, arithmetic and copies ran while one was open for 0% of the time, Pallas kernels for 4%

profile of v10, /device:TPU:32, one launch (start us, length us, event | category | flops | bytes accessed | tf_op | source)
XLA Modules:
  0.0 60.8 jit_solution(7832163506063032007)
XLA Ops:
  0.0 0.0 copy-start
  0.0 0.0 copy-start.2
  0.0 1.1 %x_faces.1 = f32[3,6,2,256]{3,2,1,0:T(2,128)S(1)} custom-call(f32[3,10,64,256]{3,2,1,0:T(8,128)} %flow.5), custom_call_target="tpu_custom_call" | custom-call | tf_op jit(solution)/shard_map/x_faces/pallas_call | solution.py:240
  1.1 0.1 collective-permute-start
  1.2 0.4 copy-done
  1.6 0.4 other_faces.1
  2.0 1.7 %collective-permute-start.3 = (f32[3,6,2,256]{3,2,1,0:T(2,128)S(1)}, f32[3,6,2,256]{3,2,1,0:T(2,128)S(1)}, u32[]{:S(2)}, u32[]{:S(2)}) collective-permute-start(f32[3,6,2,256]{3,2,1,0:T(2,128)S(1)} %get-tuple-element.28), channel_id=1, source_target_pairs={{0,8},{8,0},{16,24},{24,16},{32,40},{40,32},{48,56},{56,48},{64,72... | collective-permute-start | bytes 110600 | tf_op jit(solution)/shard_map/ppermute | solution.py:28
  3.7 3.8 %collective-permute-start.1 = (f32[80,128]{1,0:T(8,128)S(1)}, f32[80,128]{1,0:T(8,128)S(1)}, u32[]{:S(2)}, u32[]{:S(2)}) collective-permute-start(f32[80,128]{1,0:T(8,128)S(1)} %get-tuple-element.26), channel_id=1, source_target_pairs={{0,7},{1,2},{2,1},{3,4},{4,3},{5,6},{6,5},{7,0},{8,15},{9,10},{10,... | collective-permute-start | bytes 122888 | tf_op jit(solution)/shard_map/ppermute | solution.py:28
  7.4 0.0 copy-start.1
  7.4 0.0 collective-permute-start.2
  7.5 0.0 copy-done.2
  7.5 1.5 %inner.1 = (f32[6,64,256]{2,1,0:T(8,128)S(1)}, f32[6,64,256]{2,1,0:T(8,128)S(1)}, f32[6,64,256]{2,1,0:T(8,128)S(1)}, f32[6,64,256]{2,1,0:T(8,128)S(1)}, f32[6,64...) custom-call(f32[3,10,64,256]{3,2,1,0:T(8,128)S(1)} %copy-done, f32[10,64,256]{2,1,0:T(8,128)S(1)} %copy-done.2), custom_call_target="tpu_custom_call" | custom-call | flops 2500000000 | bytes 5000000 | tf_op jit(solution)/shard_map/inner/pallas_call | solution.py:262
  9.0 0.0 collective-permute-done.refs_8_
  9.0 0.0 collective-permute-done.3.refs_11_
  9.0 0.8 %collective-permute-done.1.refs_9_ = f32[80,128]{1,0:T(8,128)S(1)} collective-permute-done((f32[80,128]{1,0:T(8,128)S(1)}, f32[80,128]{1,0:T(8,128)S(1)}, u32[]{:S(2)}, u32[]{:S(2)}) %collective-permute-start.1) | collective-permute-done | bytes 40992 | tf_op jit(solution)/shard_map/ppermute | solution.py:28
  9.8 1.7 %collective-permute-done.2.refs_10_ = f32[80,128]{1,0:T(8,128)S(1)} collective-permute-done((f32[80,128]{1,0:T(8,128)S(1)}, f32[80,128]{1,0:T(8,128)S(1)}, u32[]{:S(2)}, u32[]{:S(2)}) %collective-permute-start.2) | collective-permute-done | bytes 40992 | tf_op jit(solution)/shard_map/ppermute | solution.py:28
  11.5 0.0 copy-done.1
  11.5 0.7 %field.1 = f32[64,1536]{1,0:T(8,128)S(1)} custom-call(f32[6,64,256]{2,1,0:T(8,128)S(1)} %get-tuple-element.19.refs_0_, f32[6,64,256]{2,1,0:T(8,128)S(1)} %get-tuple-element.20.refs_1_, f32[6,64,256]{2,1,0:T(8,128)S(1)} %get-tuple-element.21.refs_2_, f32[6,64,256]{2,1,0:T(8,128)S(1)} %get-tuple-element.22.refs_3_, ...), custom_call_target="tpu_custom_call" | custom-call | tf_op jit(solution)/shard_map/field/pallas_call | solution.py:272
  12.1 11.1 %all_to_all.15.parts = f32[8,8,1536]{2,1,0:T(8,128)S(1)} all-to-all(f32[8,8,1536]{2,1,0:T(8,128)S(1)} %bitcast.1), channel_id=1, replica_groups=mesh['y_hi'=2,'z'=8,'core'=2,'x'=4,'y_lo'=2] {'x','y_lo'}, dimensions={0} | all-to-all | bytes 786432 | tf_op jit(solution)/shard_map/all_to_all | solution.py:284
  23.2 0.8 %total.1 = (bf16[1,8,1536]{2,1,0:T(8,128)(2,1)S(1)}, bf16[16,8,1536]{2,1,0:T(8,128)(2,1)}) custom-call(f32[8,8,1536]{2,1,0:T(8,128)S(1)} %all_to_all.15.parts), custom_call_target="tpu_custom_call" | custom-call | tf_op jit(solution)/shard_map/total/pallas_call | solution.py:285
  24.0 10.1 %all-to-all-start.1 = ((bf16[16,8,1536]{2,1,0:T(8,128)(2,1)}), bf16[16,8,1536]{2,1,0:T(8,128)(2,1)S(1)}, u32[]{:S(2)}, u32[]{:S(2)}) async-start(bf16[16,8,1536]{2,1,0:T(8,128)(2,1)} %get-tuple-element.30), calls=%async_computation.1 | async-start | bytes 786432 | tf_op jit(solution)/shard_map/all_to_all | solution.py:296
  34.1 0.9 %collective-permute-start.4 = (bf16[1,8,1536]{2,1,0:T(8,128)(2,1)S(1)}, bf16[1,8,1536]{2,1,0:T(8,128)(2,1)S(1)}, u32[]{:S(2)}, u32[]{:S(2)}) collective-permute-start(bf16[1,8,1536]{2,1,0:T(8,128)(2,1)S(1)} %get-tuple-element.29.source), channel_id=1, source_target_pairs={{0,1},{1,0},{2,3},{3,2},{4,5},{5,4},{6,7},{7,6},{8,9},{9,8},{10,11... | collective-permute-start | bytes 73736 | tf_op jit(solution)/shard_map/ppermute | solution.py:33
  35.0 3.0 %collective-permute-done.4 = bf16[1,8,1536]{2,1,0:T(8,128)(2,1)S(1)} collective-permute-done((bf16[1,8,1536]{2,1,0:T(8,128)(2,1)S(1)}, bf16[1,8,1536]{2,1,0:T(8,128)(2,1)S(1)}, u32[]{:S(2)}, u32[]{:S(2)}) %collective-permute-start.4) | collective-permute-done | bytes 24608 | tf_op jit(solution)/shard_map/ppermute | solution.py:33
  38.0 1.6 %collective-permute-start.7 = (bf16[2,8,1536]{2,1,0:T(8,128)(2,1)S(1)}, bf16[2,8,1536]{2,1,0:T(8,128)(2,1)S(1)}, u32[]{:S(2)}, u32[]{:S(2)}) collective-permute-start(bf16[2,8,1536]{2,1,0:T(8,128)(2,1)S(1)} %pad_maximum_fusion.refs_0_), channel_id=1, source_target_pairs={{0,4},{2,6},{4,0},{6,2},{1,5},{3,7},{5,1},{7,3},{8,12},{10,14},{12... | collective-permute-start | bytes 147464 | tf_op jit(solution)/shard_map/ppermute | solution.py:33
  39.5 0.3 collective-permute-start.6
  39.8 3.0 %collective-permute-start.5 = (bf16[2,8,1536]{2,1,0:T(8,128)(2,1)S(1)}, bf16[2,8,1536]{2,1,0:T(8,128)(2,1)S(1)}, u32[]{:S(2)}, u32[]{:S(2)}) collective-permute-start(bf16[2,8,1536]{2,1,0:T(8,128)(2,1)S(1)} %pad_maximum_fusion.refs_0_), channel_id=1, source_target_pairs={{0,6},{2,0},{4,2},{6,4},{1,7},{3,1},{5,3},{7,5},{8,14},{10,8},{12,... | collective-permute-start | bytes 147464 | tf_op jit(solution)/shard_map/ppermute | solution.py:33
  42.8 2.2 %all-to-all-done.1.refs_4_ = bf16[16,8,1536]{2,1,0:T(8,128)(2,1)S(1)} async-done(((bf16[16,8,1536]{2,1,0:T(8,128)(2,1)}), bf16[16,8,1536]{2,1,0:T(8,128)(2,1)S(1)}, u32[]{:S(2)}, u32[]{:S(2)}) %all-to-all-start.1) | async-done | bytes 393248 | tf_op jit(solution)/shard_map/all_to_all | solution.py:296
  45.0 0.0 collective-permute-start.8
  45.0 0.0 collective-permute-done.7.refs_3_
  45.0 0.0 collective-permute-done.6.refs_2_
  45.0 0.0 collective-permute-done.5.refs_1_
  45.0 0.3 arrange.1
  45.4 1.4 %collective-permute-done.8.refs_2_ = bf16[16,8,1536]{2,1,0:T(8,128)(2,1)S(1)} collective-permute-done((bf16[16,8,1536]{2,1,0:T(8,128)(2,1)S(1)}, bf16[16,8,1536]{2,1,0:T(8,128)(2,1)S(1)}, u32[]{:S(2)}, u32[]{:S(2)}) %collective-permute-start.8) | collective-permute-done | bytes 393248 | tf_op jit(solution)/shard_map/ppermute | solution.py:33
  46.7 0.3 block.1
  47.1 12.7 %all_to_all.16.refs_0_ = f32[8,128,128]{2,1,0:T(8,128)S(1)} all-to-all(f32[8,128,128]{2,1,0:T(8,128)S(1)} %block.1), channel_id=1, replica_groups=mesh['y_hi'=2,'z'=8,'core'=2,'x'=4,'y_lo'=2] {'x','y_lo'}, dimensions={0} | all-to-all | bytes 1048576 | tf_op jit(solution)/shard_map/all_to_all | solution.py:331
  59.8 1.0 %place.1 = f32[64,2048]{1,0:T(8,128)} custom-call(f32[8,128,128]{2,1,0:T(8,128)S(1)} %all_to_all.16.refs_0_), custom_call_target="tpu_custom_call" | custom-call | tf_op jit(solution)/shard_map/place/pallas_call | solution.py:332
  (2 shorter events, 0.0 us)
Async XLA Ops:
  0.0 1.6 %copy-start = (f32[3,10,64,256]{3,2,1,0:T(8,128)S(1)}, f32[3,10,64,256]{3,2,1,0:T(8,128)}, u32[]{:S(2)}) copy-start(f32[3,10,64,256]{3,2,1,0:T(8,128)} %flow.5) | copy-start | bytes 5898244
  0.0 7.5 %copy-start.2 = (f32[10,64,256]{2,1,0:T(8,128)S(1)}, f32[10,64,256]{2,1,0:T(8,128)}, u32[]{:S(2)}) copy-start(f32[10,64,256]{2,1,0:T(8,128)} %thermal.1) | copy-start | bytes 1966084
  1.1 7.9 %collective-permute-start = (f32[3,6,2,256]{3,2,1,0:T(2,128)S(1)}, f32[3,6,2,256]{3,2,1,0:T(2,128)S(1)}, u32[]{:S(2)}, u32[]{:S(2)}) collective-permute-start(f32[3,6,2,256]{3,2,1,0:T(2,128)S(1)} %x_faces.1), channel_id=1, source_target_pairs={{0,248},{8,16},{16,8},{24,32},{32,24},{40,48},{48,40},{56,64},{64,... | collective-permute-start | bytes 110600 | tf_op jit(solution)/shard_map/ppermute | solution.py:28
  2.0 7.0 %collective-permute-start.3 = (f32[3,6,2,256]{3,2,1,0:T(2,128)S(1)}, f32[3,6,2,256]{3,2,1,0:T(2,128)S(1)}, u32[]{:S(2)}, u32[]{:S(2)}) collective-permute-start(f32[3,6,2,256]{3,2,1,0:T(2,128)S(1)} %get-tuple-element.28), channel_id=1, source_target_pairs={{0,8},{8,0},{16,24},{24,16},{32,40},{40,32},{48,56},{56,48},{64,72... | collective-permute-start | bytes 110600 | tf_op jit(solution)/shard_map/ppermute | solution.py:28
  3.7 6.1 %collective-permute-start.1 = (f32[80,128]{1,0:T(8,128)S(1)}, f32[80,128]{1,0:T(8,128)S(1)}, u32[]{:S(2)}, u32[]{:S(2)}) collective-permute-start(f32[80,128]{1,0:T(8,128)S(1)} %get-tuple-element.26), channel_id=1, source_target_pairs={{0,7},{1,2},{2,1},{3,4},{4,3},{5,6},{6,5},{7,0},{8,15},{9,10},{10,... | collective-permute-start | bytes 122888 | tf_op jit(solution)/shard_map/ppermute | solution.py:28
  7.4 4.0 %copy-start.1 = (bf16[256,256]{1,0:T(8,128)(2,1)S(1)}, bf16[256,256]{1,0:T(8,128)(2,1)}, u32[]{:S(2)}) copy-start(bf16[256,256]{1,0:T(8,128)(2,1)} %refs_7_.1) | copy-start | bytes 393220
  7.4 4.0 %collective-permute-start.2 = (f32[80,128]{1,0:T(8,128)S(1)}, f32[80,128]{1,0:T(8,128)S(1)}, u32[]{:S(2)}, u32[]{:S(2)}) collective-permute-start(f32[80,128]{1,0:T(8,128)S(1)} %get-tuple-element.27), channel_id=1, source_target_pairs={{0,1},{1,0},{2,3},{3,2},{4,5},{5,4},{6,7},{7,6},{8,9},{9,8},{10,11... | collective-permute-start | bytes 122888 | tf_op jit(solution)/shard_map/ppermute | solution.py:28
  24.0 21.0 %all-to-all-start.1 = ((bf16[16,8,1536]{2,1,0:T(8,128)(2,1)}), bf16[16,8,1536]{2,1,0:T(8,128)(2,1)S(1)}, u32[]{:S(2)}, u32[]{:S(2)}) async-start(bf16[16,8,1536]{2,1,0:T(8,128)(2,1)} %get-tuple-element.30), calls=%async_computation.1 | async-start | bytes 786432 | tf_op jit(solution)/shard_map/all_to_all | solution.py:296
  34.1 3.9 %collective-permute-start.4 = (bf16[1,8,1536]{2,1,0:T(8,128)(2,1)S(1)}, bf16[1,8,1536]{2,1,0:T(8,128)(2,1)S(1)}, u32[]{:S(2)}, u32[]{:S(2)}) collective-permute-start(bf16[1,8,1536]{2,1,0:T(8,128)(2,1)S(1)} %get-tuple-element.29.source), channel_id=1, source_target_pairs={{0,1},{1,0},{2,3},{3,2},{4,5},{5,4},{6,7},{7,6},{8,9},{9,8},{10,11... | collective-permute-start | bytes 73736 | tf_op jit(solution)/shard_map/ppermute | solution.py:33
  38.0 7.0 %collective-permute-start.7 = (bf16[2,8,1536]{2,1,0:T(8,128)(2,1)S(1)}, bf16[2,8,1536]{2,1,0:T(8,128)(2,1)S(1)}, u32[]{:S(2)}, u32[]{:S(2)}) collective-permute-start(bf16[2,8,1536]{2,1,0:T(8,128)(2,1)S(1)} %pad_maximum_fusion.refs_0_), channel_id=1, source_target_pairs={{0,4},{2,6},{4,0},{6,2},{1,5},{3,7},{5,1},{7,3},{8,12},{10,14},{12... | collective-permute-start | bytes 147464 | tf_op jit(solution)/shard_map/ppermute | solution.py:33
  39.5 5.5 %collective-permute-start.6 = (bf16[2,8,1536]{2,1,0:T(8,128)(2,1)S(1)}, bf16[2,8,1536]{2,1,0:T(8,128)(2,1)S(1)}, u32[]{:S(2)}, u32[]{:S(2)}) collective-permute-start(bf16[2,8,1536]{2,1,0:T(8,128)(2,1)S(1)} %pad_maximum_fusion.refs_0_), channel_id=1, source_target_pairs={{0,2},{2,4},{4,6},{6,0},{1,3},{3,5},{5,7},{7,1},{8,10},{10,12},{12... | collective-permute-start | bytes 147464 | tf_op jit(solution)/shard_map/ppermute | solution.py:33
  39.8 5.2 %collective-permute-start.5 = (bf16[2,8,1536]{2,1,0:T(8,128)(2,1)S(1)}, bf16[2,8,1536]{2,1,0:T(8,128)(2,1)S(1)}, u32[]{:S(2)}, u32[]{:S(2)}) collective-permute-start(bf16[2,8,1536]{2,1,0:T(8,128)(2,1)S(1)} %pad_maximum_fusion.refs_0_), channel_id=1, source_target_pairs={{0,6},{2,0},{4,2},{6,4},{1,7},{3,1},{5,3},{7,5},{8,14},{10,8},{12,... | collective-permute-start | bytes 147464 | tf_op jit(solution)/shard_map/ppermute | solution.py:33
  45.0 1.7 %collective-permute-start.8 = (bf16[16,8,1536]{2,1,0:T(8,128)(2,1)S(1)}, bf16[16,8,1536]{2,1,0:T(8,128)(2,1)S(1)}, u32[]{:S(2)}, u32[]{:S(2)}) collective-permute-start(bf16[16,8,1536]{2,1,0:T(8,128)(2,1)S(1)} %all-to-all-done.1.refs_4_), channel_id=1, source_target_pairs={{0,8},{8,0},{1,9},{9,1},{2,10},{10,2},{3,11},{11,3},{4,12},{12,4},... | collective-permute-start | bytes 1179656 | tf_op jit(solution)/shard_map/ppermute | solution.py:33
